TPU v7x, 128 devices: a whole 4x4x4 slice. The times are simulated.
128 devices in a mesh: dp: 64 (over y, z, x), shard: 2 (over core).
Axes of the slice: x: 4, y: 4, z: 4, core: 2. Of those that a mesh axis runs over, the one named last changes fastest.
Arguments:
- tokens: bfloat16 [32768, 1024], P(('dp', 'shard')), may hold values from -24 to 24
- packed_proj: bfloat16 [1024, 3072], P(('dp', 'shard')), may hold values from -0.1875 to 0.1875
- mixer_proj: bfloat16 [1024, 1024], P(('dp', 'shard')), may hold values from -0.75 to 0.75
- expand_proj: bfloat16 [1024, 5248], P(('dp', 'shard')), may hold values from -0.1875 to 0.1875
- reduce_proj: bfloat16 [1024, 2624], P(('dp', 'shard')), may hold values from -0.125 to 0.125
- first_gain: bfloat16 [1024], P(('dp', 'shard')), may hold values from 0.25 to 1.75
- second_gain: bfloat16 [1024], P(('dp', 'shard')), may hold values from 0.25 to 1.75
- sequence_lengths: int32 [512], P(('dp', 'shard')), may hold values from 0 to 256, as said below
- cotangent: bfloat16 [32768, 1024], P(('dp', 'shard')), may hold values from -24 to 24
Outputs:
- block_output: bfloat16 [32768, 1024], P(('dp', 'shard'))
- input_grad: float32 [32768, 1024], P(('dp', 'shard'))
- packed_grad: float32 [1024, 3072], P(('dp', 'shard'))
- mixer_grad: float32 [1024, 1024], P(('dp', 'shard'))
- expand_grad: float32 [1024, 5248], P(('dp', 'shard'))
- reduce_grad: float32 [1024, 2624], P(('dp', 'shard'))
- first_gain_grad: float32 [1024], P(('dp', 'shard'))
- second_gain_grad: float32 [1024], P(('dp', 'shard'))
Inputs may be any that keep to these rules, and one draw needn't show every extreme that they name: `sequence_lengths`: each aligned group of 4 entries gives the sequences of one block of 256 slots in order; their sum is at most 256 and the block's remaining slots are padding. Lengths may be 0. In every draw one block holds a single sequence of 256 tokens.
All inputs are finite; a program needn't handle non-finite values.
Results may differ from a plain program's by a relative error of at most 0.019.
Values may be sent and summed in bfloat16 or wider, within the bound.
No kernel may reach another device: no remote copies, remote signals or barrier semaphores. Data moves between devices by JAX's collectives and lax.ppermute only.
A program may use at most 192 MiB of HBM per device.

v0:
```python
import jax
import jax.numpy as jnp
from jax import lax
from jax.sharding import PartitionSpec as P

H = 16
HD = 64


epsilon = 1e-05
rope_base = 160000.0
masked_score = -1e30


def sent_together(arrays, axis, split_dim, concat_dim, along):
    both = jnp.concatenate(arrays, axis=along)
    whole, at, gathered = (
        lax.all_to_all(both, axis, split_axis=split_dim, concat_axis=concat_dim, tiled=True),
        0,
        [],
    )
    for a in arrays:
        gathered.append(lax.slice_in_dim(whole, at, at + a.shape[along], axis=along))
        at += a.shape[along]
    return tuple(gathered)


def side_by_side(arrays, axis, dim, along):
    columns = [a.reshape(*a.shape[:along], -1) for a in arrays]
    both = jnp.concatenate(columns, axis=along)
    whole, at, gathered = (lax.all_gather(both, axis, axis=dim, tiled=True), 0, [])
    for a, column in zip(arrays, columns):
        section = whole[..., at : at + column.shape[along]]
        gathered.append(section.reshape(*section.shape[:along], *a.shape[along:]))
        at += column.shape[along]
    return tuple(gathered)


def sent_together_2(arrays, axis, dim, along):
    both = jnp.concatenate(arrays, axis=along)
    whole, at, gathered = (lax.all_gather(both, axis, axis=dim, tiled=True), 0, [])
    for a in arrays:
        gathered.append(lax.slice_in_dim(whole, at, at + a.shape[along], axis=along))
        at += a.shape[along]
    return tuple(gathered)


def joined_along(parts, dim):
    dims = list(parts.shape[1:])
    dims[dim] *= parts.shape[0]
    return jnp.moveaxis(parts, 0, dim).reshape(dims)


def from_everyone(shard, axis):
    copies = jnp.broadcast_to(shard, (lax.axis_size(axis), *shard.shape))
    return lax.all_to_all(copies, axis, split_axis=0, concat_axis=0, tiled=True)


def collect(shard, axis, dim):
    return joined_along(from_everyone(shard, axis), dim)


def of_everyone(shard, axis):
    everything = from_everyone(shard, axis)
    return jnp.sum(everything, axis=0)


def in_blocks(shard, dim, size):
    dims = shard.shape
    parts = shard.reshape(*dims[:dim], size, dims[dim] // size, *dims[dim + 1 :])
    return jnp.moveaxis(parts, dim, 0)


def sum_at_owner(shard, axis, dim):
    parts = in_blocks(shard, dim, lax.axis_size(axis))
    arrived = lax.all_to_all(parts, axis, split_axis=0, concat_axis=0, tiled=True)
    return arrived.astype(jnp.float32).sum(axis=0)


def taken_together(shard, axis):
    everything = from_everyone(shard, axis)
    return jnp.sum(everything.astype(jnp.float32), axis=0)


def side_by_side_2(arrays, axis, dim, along):
    columns = [a.reshape(*a.shape[:along], -1) for a in arrays]
    both = jnp.concatenate(columns, axis=along)
    whole, at, gathered = (lax.psum_scatter(both, axis, scatter_dimension=dim, tiled=True), 0, [])
    for a, column in zip(arrays, columns):
        section = whole[..., at : at + column.shape[along]]
        gathered.append(section.reshape(*section.shape[:along], *a.shape[along:]))
        at += column.shape[along]
    return tuple(gathered)


def token_layout(lengths, slot_count):
    places = jnp.arange(slot_count, dtype=jnp.int32)
    seq_ends = jnp.cumsum(lengths)
    seq_starts = seq_ends - lengths
    segment = jnp.sum((places[:, None] >= seq_ends[None, :]).astype(jnp.int32), axis=1)
    live_mask = places < seq_ends[-1]
    picked = (segment[:, None] == jnp.arange(lengths.shape[0], dtype=jnp.int32)[None, :]).astype(
        jnp.int32
    )
    offset = jnp.sum(picked * seq_starts[None, :], axis=1)
    position = jnp.where(live_mask, places - offset, 0)
    segment = jnp.where(live_mask, segment, lengths.shape[0] + places)
    return (live_mask, segment, position)


def rotary_tables(position, head_size):
    half_size = head_size // 2
    frequency = rope_base ** (-(jnp.arange(half_size, dtype=jnp.float32) * 2.0 / head_size))
    angles = position.astype(jnp.float32)[..., None] * frequency
    angles = jnp.concatenate([angles, angles], axis=-1)
    return (jnp.cos(angles), jnp.sin(angles))


def rotate(values, cosine_table, sine_table):
    half_size = values.shape[-1] // 2
    turned = jnp.concatenate([-values[..., half_size:], values[..., :half_size]], axis=-1)
    return values * cosine_table[..., None, :] + turned * sine_table[..., None, :]


def layer_norm(values, gain_vector):
    row_mean = jnp.mean(values, axis=-1, keepdims=True)
    centered = values - row_mean
    row_var = jnp.mean(centered * centered, axis=-1, keepdims=True)
    return centered * lax.rsqrt(row_var + epsilon) * gain_vector


def gelu_gate(gate_part, up_part):
    return jax.nn.gelu(gate_part, approximate=False) * up_part


def contract_last(left, right):
    return lax.dot_general(
        left, right, (((1,), (1,)), ((), ())), preferred_element_type=jnp.float32
    )


def contract_first(left, right):
    return lax.dot_general(
        left, right, (((0,), (0,)), ((), ())), preferred_element_type=jnp.float32
    )


def attention_forward(query_rows, key_rows, value_rows, allowed):
    score_scale = query_rows.shape[-1] ** (-0.5)
    scores = (
        jnp.einsum("qhd,khd->hqk", query_rows, key_rows, preferred_element_type=jnp.float32)
        * score_scale
    )
    scores = jnp.where(allowed, scores, masked_score)
    row_top = jnp.max(scores, axis=-1, keepdims=True)
    expd = jnp.exp(scores - row_top)
    row_total = jnp.sum(expd, axis=-1, keepdims=True)
    attention = expd / row_total
    log_total = row_top + jnp.log(row_total)
    mixed_heads = jnp.einsum(
        "hqk,khd->qhd",
        attention.astype(jnp.bfloat16),
        value_rows,
        preferred_element_type=jnp.float32,
    )
    return (mixed_heads, log_total)


def attention_backward(query_rows, key_rows, value_rows, allowed, log_total, grad_mixed):
    score_scale = query_rows.shape[-1] ** (-0.5)
    scores = (
        jnp.einsum("qhd,khd->hqk", query_rows, key_rows, preferred_element_type=jnp.float32)
        * score_scale
    )
    scores = jnp.where(allowed, scores, masked_score)
    attention = jnp.exp(scores - log_total)
    grad_attention = jnp.einsum(
        "qhd,khd->hqk", grad_mixed, value_rows, preferred_element_type=jnp.float32
    )
    row_delta = jnp.sum(attention * grad_attention, axis=-1, keepdims=True)
    grad_scores = (attention * (grad_attention - row_delta)).astype(jnp.bfloat16)
    grad_query = (
        jnp.einsum("hqk,khd->qhd", grad_scores, key_rows, preferred_element_type=jnp.float32)
        * score_scale
    )
    grad_key = (
        jnp.einsum("hqk,qhd->khd", grad_scores, query_rows, preferred_element_type=jnp.float32)
        * score_scale
    )
    grad_value = jnp.einsum(
        "hqk,qhd->khd",
        attention.astype(jnp.bfloat16),
        grad_mixed,
        preferred_element_type=jnp.float32,
    )
    return (grad_query, grad_key, grad_value)


def fetch_halves(packed_proj, mixer_proj, expand_proj, reduce_proj, first_gain, second_gain):
    parts = lax.axis_size("shard")
    rows = packed_proj.shape[0]
    model_width = packed_proj.shape[1] // 3
    hidden_width = reduce_proj.shape[1]
    packed_piece = packed_proj.reshape(1, rows, 3, parts, model_width // parts)
    expand_piece = expand_proj.reshape(1, rows, 2, parts, hidden_width // parts)
    reduce_piece = reduce_proj.reshape(1, rows, 1, parts, hidden_width // parts)
    mixer_piece = jnp.broadcast_to(
        mixer_proj.reshape(1, rows, 1, 1, model_width), (1, rows, 1, parts, model_width)
    )
    gains = jnp.stack([first_gain, second_gain], axis=1)
    gain_piece = jnp.broadcast_to(gains.reshape(1, rows, 1, 1, 2), (1, rows, 1, parts, 2))
    packed_s, expand_s, reduce_s, mixer_s, gain_s = (
        lax.all_to_all(packed_piece, "shard", split_axis=3, concat_axis=0, tiled=True),
        *sent_together((expand_piece, reduce_piece), "shard", 3, 0, 2),
        *sent_together((mixer_piece, gain_piece), "shard", 3, 0, 4),
    )
    packed_w, expand_w, reduce_w, mixer_w, gain_w = side_by_side(
        (packed_s, expand_s, reduce_s, mixer_s, gain_s), "dp", 0, 2
    )
    full_rows = packed_w.shape[0] * rows
    return (
        packed_w.reshape(full_rows, 3 * (model_width // parts)),
        mixer_w.reshape(full_rows, model_width),
        expand_w.reshape(full_rows, 2 * (hidden_width // parts)),
        reduce_w.reshape(full_rows, hidden_width // parts),
        gain_w.reshape(full_rows, 2),
    )


def chip_body(
    tokens,
    packed_proj,
    mixer_proj,
    expand_proj,
    reduce_proj,
    first_gain,
    second_gain,
    sequence_lengths,
    cotangent,
):
    parts = lax.axis_size("shard")
    own_index = lax.axis_index("shard")
    row_count = tokens.shape[0]
    model_width = tokens.shape[1]
    hidden_width = reduce_proj.shape[1]
    weight_rows = packed_proj.shape[0]
    part_width = model_width // parts
    part_hidden = hidden_width // parts
    part_heads = H // parts
    seq_slots = sequence_lengths.shape[0]
    both_rows, both_cotangent = sent_together_2((tokens, cotangent), "shard", 0, 1)
    both_lengths = collect(sequence_lengths, "shard", 0)
    live_list = []
    segment_list = []
    position_list = []
    for block in range(parts):
        live_block, segment_block, position_block = token_layout(
            both_lengths[block * seq_slots : (block + 1) * seq_slots], row_count
        )
        live_list.append(live_block)
        segment_list.append(segment_block + block * (seq_slots + row_count))
        position_list.append(position_block)
    live_mask = jnp.concatenate(live_list)
    segment = jnp.concatenate(segment_list)
    position = jnp.concatenate(position_list)
    chip_count = parts * row_count
    cosine_table, sine_table = rotary_tables(position, HD)
    live_float = live_mask.astype(jnp.float32)[:, None]
    live_own = lax.dynamic_slice_in_dim(live_float, own_index * row_count, row_count, 0)
    allowed = (segment[:, None] == segment[None, :])[None]
    packed_half, mixer_full, expand_half, reduce_half, gain_pair = fetch_halves(
        packed_proj, mixer_proj, expand_proj, reduce_proj, first_gain, second_gain
    )
    mixer_rows = lax.dynamic_slice_in_dim(mixer_full, own_index * part_width, part_width, 0)
    gain_one = gain_pair[:, 0].astype(jnp.float32)
    gain_two = gain_pair[:, 1].astype(jnp.float32)
    stream = both_rows.astype(jnp.float32)
    normed_one = layer_norm(stream, gain_one).astype(jnp.bfloat16)
    packed = jnp.dot(normed_one, packed_half, preferred_element_type=jnp.float32).reshape(
        chip_count, 3, part_heads, HD
    )
    query_rows = rotate(packed[:, 0], cosine_table, sine_table).astype(jnp.bfloat16)
    key_rows = rotate(packed[:, 1], cosine_table, sine_table).astype(jnp.bfloat16)
    value_rows = packed[:, 2].astype(jnp.bfloat16)
    mixed_heads, log_total = attention_forward(query_rows, key_rows, value_rows, allowed)
    mixed_heads = mixed_heads.reshape(chip_count, part_width).astype(jnp.bfloat16)
    attended = of_everyone(
        jnp.dot(mixed_heads, mixer_rows, preferred_element_type=jnp.float32), "shard"
    )
    residual = stream + attended
    normed_two = layer_norm(residual, gain_two).astype(jnp.bfloat16)
    gate_up = jnp.dot(normed_two, expand_half, preferred_element_type=jnp.float32)
    gate_part = gate_up[:, :part_hidden]
    up_part = gate_up[:, part_hidden:]
    hidden = gelu_gate(gate_part, up_part).astype(jnp.bfloat16)
    branch = sum_at_owner(contract_last(hidden, reduce_half).astype(jnp.bfloat16), "shard", 0)
    residual_own = lax.dynamic_slice_in_dim(residual, own_index * row_count, row_count, 0)
    block_output = (live_own * (residual_own + branch)).astype(jnp.bfloat16)
    packed_back, mixer_back_full, expand_back, reduce_back, gain_back = fetch_halves(
        packed_proj, mixer_proj, expand_proj, reduce_proj, first_gain, second_gain
    )
    mixer_back = lax.dynamic_slice_in_dim(mixer_back_full, own_index * part_width, part_width, 0)
    gain_one_back = gain_back[:, 0].astype(jnp.float32)
    gain_two_back = gain_back[:, 1].astype(jnp.float32)
    grad_top = live_float * both_cotangent.astype(jnp.float32)
    grad_branch = grad_top.astype(jnp.bfloat16)
    reduce_term = contract_first(grad_branch, hidden)
    grad_hidden = jnp.dot(grad_branch, reduce_back, preferred_element_type=jnp.float32)
    unused, pull_gate = jax.vjp(gelu_gate, gate_part, up_part)
    grad_gate, grad_up = pull_gate(grad_hidden)
    grad_gate_up = jnp.concatenate([grad_gate, grad_up], axis=1).astype(jnp.bfloat16)
    expand_term = contract_first(normed_two, grad_gate_up)
    grad_normed_two = taken_together(
        contract_last(grad_gate_up, expand_back).astype(jnp.bfloat16), "shard"
    ).astype(jnp.float32)
    unused, pull_second = jax.vjp(layer_norm, residual, gain_two_back)
    grad_residual_norm, unused_gain = pull_second(grad_normed_two)
    normal_own = layer_norm(residual_own, jnp.ones((model_width,), jnp.float32))
    grad_two_own = lax.dynamic_slice_in_dim(grad_normed_two, own_index * row_count, row_count, 0)
    second_gain_term = jnp.sum(grad_two_own * normal_own, axis=0)
    grad_residual = grad_top + grad_residual_norm
    grad_attended = grad_residual.astype(jnp.bfloat16)
    mixer_term = contract_first(mixed_heads, grad_attended)
    grad_mixed = (
        contract_last(grad_attended, mixer_back)
        .astype(jnp.bfloat16)
        .reshape(chip_count, part_heads, HD)
    )
    grad_query, grad_key, grad_value = attention_backward(
        query_rows, key_rows, value_rows, allowed, log_total, grad_mixed
    )
    grad_packed = jnp.stack(
        [
            rotate(grad_query, cosine_table, -sine_table),
            rotate(grad_key, cosine_table, -sine_table),
            grad_value,
        ],
        axis=1,
    )
    grad_packed = grad_packed.reshape(chip_count, 3 * part_width).astype(jnp.bfloat16)
    packed_term = contract_first(normed_one, grad_packed)
    grad_normed_one = sum_at_owner(
        contract_last(grad_packed, packed_back).astype(jnp.bfloat16), "shard", 0
    )
    stream_own = tokens.astype(jnp.float32)
    unused, pull_first = jax.vjp(layer_norm, stream_own, gain_one_back)
    grad_stream_norm, first_gain_term = pull_first(grad_normed_one)
    grad_residual_own = lax.dynamic_slice_in_dim(grad_residual, own_index * row_count, row_count, 0)
    input_grad = grad_residual_own + grad_stream_norm
    block_count = model_width // weight_rows
    mixer_whole = lax.dynamic_update_slice_in_dim(
        jnp.zeros((model_width, model_width), jnp.float32), mixer_term, own_index * part_width, 0
    )
    gain_whole = jnp.stack([first_gain_term, second_gain_term], axis=1)
    packed_share, expand_share, reduce_share, mixer_share, gain_share = side_by_side_2(
        (
            packed_term.reshape(block_count, weight_rows, 3, 1, part_width),
            expand_term.reshape(block_count, weight_rows, 2, 1, part_hidden),
            reduce_term.reshape(block_count, weight_rows, 1, 1, part_hidden),
            mixer_whole.reshape(block_count, weight_rows, 1, 1, model_width),
            gain_whole.reshape(block_count, weight_rows, 1, 1, 2),
        ),
        "dp",
        0,
        2,
    )
    packed_own, expand_own, reduce_own, mixer_own, gain_own = (
        lax.all_to_all(
            packed_share.astype(jnp.bfloat16), "shard", split_axis=0, concat_axis=3, tiled=True
        ).astype(packed_share.dtype),
        *tuple(
            (
                part.astype(jnp.float32)
                for part in sent_together(
                    (expand_share.astype(jnp.bfloat16), reduce_share.astype(jnp.bfloat16)),
                    "shard",
                    0,
                    3,
                    2,
                )
            )
        ),
        *tuple(
            (
                part.astype(jnp.float32)
                for part in sent_together(
                    (mixer_share.astype(jnp.bfloat16), gain_share.astype(jnp.bfloat16)),
                    "shard",
                    0,
                    3,
                    4,
                )
            )
        ),
    )
    packed_grad = packed_own.reshape(weight_rows, 3 * model_width)
    expand_grad = expand_own.reshape(weight_rows, 2 * hidden_width)
    reduce_grad = reduce_own.reshape(weight_rows, hidden_width)
    mixer_grad = jnp.sum(mixer_own, axis=3).reshape(weight_rows, model_width)
    gain_grads = jnp.sum(gain_own, axis=3).reshape(weight_rows, 2)
    return (
        block_output,
        input_grad,
        packed_grad,
        mixer_grad,
        expand_grad,
        reduce_grad,
        gain_grads[:, 0],
        gain_grads[:, 1],
    )


def body(
    tokens,
    packed_proj,
    mixer_proj,
    expand_proj,
    reduce_proj,
    first_gain,
    second_gain,
    sequence_lengths,
    cotangent,
):
    return chip_body(
        tokens,
        packed_proj,
        mixer_proj,
        expand_proj,
        reduce_proj,
        first_gain,
        second_gain,
        sequence_lengths,
        cotangent,
    )


def solution(mesh):
    in_specs = (
        P(("dp", "shard"), None),
        P(("dp", "shard"), None),
        P(("dp", "shard"), None),
        P(("dp", "shard"), None),
        P(("dp", "shard"), None),
        P(("dp", "shard")),
        P(("dp", "shard")),
        P(("dp", "shard")),
        P(("dp", "shard"), None),
    )
    out_specs = (
        P(("dp", "shard"), None),
        P(("dp", "shard"), None),
        P(("dp", "shard"), None),
        P(("dp", "shard"), None),
        P(("dp", "shard"), None),
        P(("dp", "shard"), None),
        P(("dp", "shard")),
        P(("dp", "shard")),
    )
    return jax.shard_map(body, mesh=mesh, in_specs=in_specs, out_specs=out_specs, check_vma=False)
```

profile of v0, /device:TPU:1, one launch (start us, length us, event | category | flops | bytes accessed | tf_op | source)
XLA Modules:
  0.0 592.1 jit_solution(6066610880922585639)
XLA Ops:
  7.3 2.3 pad_maximum_fusion.6
  10.8 4.8 all-to-all-start.2
  17.0 3.3 all-to-all-start.3
  20.6 0.8 all-to-all-done.3
  21.4 3.6 all-to-all-start.1
  25.0 1.0 all-to-all-done.1
  26.1 0.8 concatenate.77
  27.5 3.6 all-to-all-start
  31.0 1.0 all-to-all-done
  33.5 1.3 iota_compare_fusion.4
  35.6 1.3 select_add_fusion
  37.1 1.3 subtract_select_fusion.1
  38.5 1.0 broadcast_multiply_fusion.2
  39.9 1.4 convert_reduce_fusion.1
  41.4 1.7 fusion.22
  43.1 82.2 %all-gather.5.cloned.1.call-done = bf16[128,8,6498]{2,1,0:T(8,128)(2,1)} async-done(((bf16[2,8,6498]{2,1,0:T(8,128)(2,1)}), bf16[128,8,6498]{2,1,0:T(8,128)(2,1)}) %all-gather.5.cloned.1.call-update) | async-done | bytes 13307920 | tf_op jit(solution)/shard_map/all_gather | solution.py:31
  125.3 1.1 slice_bitcast_fusion.14
  126.3 0.9 slice_convert_fusion.1
  127.5 3.7 slice_bitcast_fusion.4
  131.2 4.8 copy.195
  136.0 3.9 fusion.54
  142.1 1.5 fusion.87
  143.7 1.2 fusion
  144.9 2.0 copy-done
  146.9 1.5 fusion.35
  148.6 2.7 slice_bitcast_fusion.7
  151.3 1.3 copy-done.8
  153.9 8.5 %all_to_all.137 = f32[2,512,1024]{2,1,0:T(8,128)} all-to-all(f32[2,512,1024]{2,1,0:T(8,128)S(1)} %broadcast_in_dim.47), channel_id=1, replica_groups=mesh['dp'=64,'shard'=2] {'shard'}, dimensions={0} | all-to-all | bytes 8388608 | tf_op jit(solution)/shard_map/all_to_all | solution.py:56
  162.4 4.1 reduce_sum.269
  166.6 3.4 fusion.86
  170.5 6.0 %fusion.3 = f32[512,2624]{0,1:T(8,128)S(1)} fusion(bf16[128,8,6498]{2,1,0:T(8,128)(2,1)} %all-gather.5.cloned.1.call-done, f32[512,1024]{1,0:T(8,128)S(1)} %get-tuple-element.35, f32[1024]{0:T(1024)S(1)} %bitcast.195, f32[512]{0:T(512)S(1)} %fusion.74, f32[512]{0:T(512)S(1)} %broadcast_multiply_fusion.4), kind=kOutput, calls=%fused_computation.11 | convolution fusion | flops 2753560576 | bytes 12984320 | tf_op jit(solution)/shard_map/dot_general | solution.py:292
  176.5 23.7 %add_convert_fusion = (bf16[512,1312]{0,1:T(8,128)(2,1)S(1)}, f32[512,1312]{0,1:T(8,128)S(1)}, f32[512,1312]{0,1:T(8,128)S(1)}) fusion(f32[512,2624]{0,1:T(8,128)S(1)} %fusion.3, bf16[128,8,6498]{2,1,0:T(8,128)(2,1)} %all-gather.5.cloned.1.call-done, f32[512]{0:T(512)S(1)} %add_convert_fusion.2, bf16[512,2048]{1,0:T(8,128)(2,1)S(1)} %copy-done.11), kind=kOutput, calls=%fused_computation.30 | convolution fusion | flops 1426341888 | bytes 16025600 | tf_op jit(solution)/shard_map/dot_general | solution.py:308
  200.1 2.6 multiply_convert_fusion.1
  202.7 5.8 fusion.30
  208.8 5.4 all_to_all.138
  216.4 1.3 copy-done.3
  217.7 1.3 copy-done.9
  220.2 2.2 fusion.39
  222.5 2.9 multiply_reduce_fusion
  225.4 2.6 multiply_convert_fusion
  228.0 2.8 broadcast_multiply_fusion
  230.8 2.1 broadcast_multiply_fusion.1
  232.9 6.3 %convolution_bitcast_fusion = f32[128,8,2624]{2,1,0:T(8,128)} fusion(bf16[512,1312]{0,1:T(8,128)(2,1)S(1)} %get-tuple-element.36, bf16[512,1312]{0,1:T(8,128)(2,1)S(1)} %get-tuple-element.32, f32[512,1024]{1,0:T(8,128)S(1)} %get-tuple-element.35, f32[1024]{0:T(1024)S(1)} %bitcast.198, f32[512]{0:T(512)S(1)} %fusion.74, f32[512]{0:T(512)S(1)} %broadcast_multiply_fusion.4), kind=kOutput, calls=%fused_computation.7 | convolution fusion | flops 2758934528 | bytes 15540224 | tf_op jit(solution)/shard_map/dot_general | solution.py:143
  239.5 2.3 copy.200
  241.8 5.9 %fusion.26 = bf16[512,1024]{1,0:T(8,128)(2,1)} fusion(bf16[512,1312]{0,1:T(8,128)(2,1)} %get-tuple-element.37, bf16[128,8,6498]{2,1,0:T(8,128)(2,1)} %all-gather.5.cloned.1.call-done), kind=kOutput, calls=%fused_computation.66 | convolution fusion | flops 1376256000 | bytes 5275648 | tf_op jit(solution)/shard_map/dot_general | solution.py:137
  247.7 5.1 all-to-all-start.5
  252.9 2.5 broadcast_in_dim.53
  255.4 2.0 convolution_dynamic-update-slice_fusion
  257.4 1.7 convert_reduce_fusion.3
  259.3 1.1 multiply_reduce_fusion.3
  260.8 1.5 slice_negate_fusion
  264.0 4.3 fusion.27
  268.3 4.2 all_to_all.139
  274.1 6.3 %fusion.56 = f32[128,8,1536]{2,1,0:T(8,128)} fusion(bf16[512,1536,1]{0,1,2:T(8,128)(2,1)} %bitcast.176, bf16[1024,512]{1,0:T(8,128)(2,1)} %copy.200), kind=kOutput, calls=%fused_computation.103 | convolution fusion | flops 1610612736 | bytes 8912896 | tf_op jit(solution)/shard_map/dot_general | solution.py:143
  280.4 4.5 convolution_bitcast_fusion.1
  284.9 31.6 %concatenate.86 = f32[128,8,6498]{2,1,0:T(8,128)} concatenate(f32[128,8,1536]{2,1,0:T(8,128)} %fusion.56, f32[128,8,2624]{2,1,0:T(8,128)} %convolution_bitcast_fusion, f32[128,8,1312]{2,1,0:T(8,128)} %convolution_bitcast_fusion.1, f32[128,8,1024]{2,1,0:T(8,128)} %bitcast.59, f32[128,8,1]{2,1,0:T(8,128)S(1)} %stack.44, f32[128,8,1]{2,1,0:T(8,128)S(1)} %stack.45), dimensions={2} | concatenate | bytes 53231616 | tf_op jit(solution)/shard_map/concatenate | solution.py:87
  316.5 1.6 copy-done.5
  318.1 2.4 add_add_fusion.3
  320.5 245.8 %reduce-scatter.2.cloned.1.call-done = f32[2,8,6498]{2,1,0:T(8,128)} async-done(((f32[128,8,6498]{2,1,0:T(8,128)}), f32[2,8,6498]{2,1,0:T(8,128)}) %reduce-scatter.2.cloned.1.call-update) | async-done | bytes 415888 | tf_op jit(solution)/shard_map/reduce_scatter | solution.py:88
  566.3 1.0 convert.42
  567.5 5.9 all_to_all.140
  574.3 3.8 all_to_all.141
  578.9 3.8 all_to_all.142
  584.4 0.8 reshape.442
  (176 shorter events, 21.8 us)
Async XLA Ops:
  7.2 2.4 copy-start.29
  7.2 2.6 copy-start.27
  7.2 8.4 %copy-start.34 = (bf16[8]{0:T(256)(128)(2,1)S(1)}, bf16[8]{0:T(256)(128)(2,1)}, u32[]{:S(2)}) copy-start(bf16[8]{0:T(256)(128)(2,1)} %param.15) | copy-start | bytes 52
  7.2 8.4 %copy-start.35 = (bf16[8]{0:T(256)(128)(2,1)S(1)}, bf16[8]{0:T(256)(128)(2,1)}, u32[]{:S(2)}) copy-start(bf16[8]{0:T(256)(128)(2,1)} %param.14) | copy-start | bytes 52
  7.2 8.5 %copy-start.28 = (bf16[8,3072]{1,0:T(8,128)(2,1)S(1)}, bf16[8,3072]{1,0:T(8,128)(2,1)}, u32[]{:S(2)}) copy-start(bf16[8,3072]{1,0:T(8,128)(2,1)} %param.10) | copy-start | bytes 147460
  7.2 9.2 %copy-start.30 = (bf16[8,1024]{1,0:T(8,128)(2,1)S(1)}, bf16[8,1024]{1,0:T(8,128)(2,1)}, u32[]{:S(2)}) copy-start(bf16[8,1024]{1,0:T(8,128)(2,1)} %param.11) | copy-start | bytes 49156
  7.2 19.7 %copy-start.36 = (s32[4]{0:T(128)S(1)}, s32[4]{0:T(128)}, u32[]{:S(2)}) copy-start(s32[4]{0:T(128)} %param.16) | copy-start | bytes 52
  7.2 32.7 %all-gather.3.cloned.1.call-start = ((), (), s32[]{:S(2)}) async-start(), calls=%async_computation.12 | async-start | bytes 3145728 | tf_op jit(solution)/shard_map/all_gather | solution.py:41
  9.6 30.0 %copy-start.6 = (bf16[256,1024]{1,0:T(8,128)(2,1)S(1)}, bf16[256,1024]{1,0:T(8,128)(2,1)}, u32[]{:S(2)}) copy-start(bf16[256,1024]{1,0:T(8,128)(2,1)} %param.9) | copy-start | bytes 1572868
  10.8 6.2 %all-to-all-start.2 = ((bf16[1,8,3,2,1312]{4,1,2,0,3:T(8,128)(2,1)}), bf16[1,8,3,2,1312]{4,1,2,0,3:T(8,128)(2,1)S(1)}, u32[]{:S(2)}, u32[]{:S(2)}) async-start(bf16[1,8,3,2,1312]{4,1,2,0,3:T(8,128)(2,1)} %copy.188), calls=%async_computation.2 | async-start | bytes 270336 | tf_op jit(solution)/shard_map/all_to_all | solution.py:18
  17.0 4.4 all-to-all-start.3
  21.4 4.7 all-to-all-start.1
  25.0 100.3 %all-gather.5.cloned.1.call-start = ((), (), s32[]{:S(2)}) async-start(), calls=%async_computation.13 | async-start | bytes 13578240 | tf_op jit(solution)/shard_map/all_gather | solution.py:31
  27.5 4.5 all-to-all-start
  43.1 93.0 %copy-start.31 = (f32[512]{0:T(512)}, f32[512]{0:T(512)S(1)}, u32[]{:S(2)}) copy-start(f32[512]{0:T(512)S(1)} %add_rsqrt_fusion) | copy-start | bytes 6148
  131.2 4.8 copy-start.10
  140.0 4.9 copy-start.7
  140.2 1.1 copy-start.25
  140.2 1.3 copy-start.26
  142.1 1.6 copy-start.13
  143.7 3.2 copy-start
  146.9 1.5 copy-start.20
  148.4 5.0 copy-start.18
  151.3 1.3 copy-start.8
  162.4 4.1 copy-start.32
  170.5 6.0 %copy-start.11 = (bf16[512,2048]{1,0:T(8,128)(2,1)S(1)}, bf16[512,2048]{1,0:T(8,128)(2,1)}, u32[]{:S(2)}) copy-start(bf16[512,2048]{1,0:T(8,128)(2,1)} %all-gather.3.cloned.1.call-done) | copy-start | bytes 6291460
  214.7 1.4 copy-start.1
  215.2 4.6 slice-start
  216.0 3.0 copy-start.9
  216.0 4.2 slice-start.1
  216.4 1.3 copy-start.3
  225.4 2.6 copy-start.14
  247.7 7.7 %copy-start.19 = (bf16[8,64,512]{2,1,0:T(8,128)(2,1)S(1)}, bf16[8,64,512]{2,1,0:T(8,128)(2,1)}, u32[]{:S(2)}) copy-start(bf16[8,64,512]{2,1,0:T(8,128)(2,1)} %copy-done.18) | copy-start | bytes 1572868
  247.7 9.7 %all-to-all-start.5 = ((bf16[2,256,1024]{2,1,0:T(8,128)(2,1)}), bf16[2,256,1024]{2,1,0:T(8,128)(2,1)}, u32[]{:S(2)}, u32[]{:S(2)}) async-start(bf16[2,256,1024]{2,1,0:T(8,128)(2,1)} %bitcast.177), calls=%async_computation.5 | async-start | bytes 2097152 | tf_op jit(solution)/shard_map/all_to_all | solution.py:76
  252.8 313.5 %reduce-scatter.2.cloned.1.call-start = ((), (), s32[]{:S(2)}) async-start(), calls=%async_computation.14 | async-start | bytes 27156480 | tf_op jit(solution)/shard_map/reduce_scatter | solution.py:88
  252.9 2.5 copy-start.4
  255.4 3.8 copy-start.33
  257.4 1.9 copy-start.2
  260.4 1.9 copy-start.15
  260.4 2.0 copy-start.16
  260.4 2.0 copy-start.24
  260.8 1.9 copy-start.17
  262.7 1.0 copy-start.21
  264.0 4.3 copy-start.22
  274.0 6.4 %copy-start.12 = (bf16[512,2048]{1,0:T(8,128)(2,1)S(1)}, bf16[512,2048]{1,0:T(8,128)(2,1)}, u32[]{:S(2)}) copy-start(bf16[512,2048]{1,0:T(8,128)(2,1)} %all-gather.3.cloned.1.call-done) | copy-start | bytes 6291460
  274.1 6.4 %copy-start.23 = (bf16[512,1312]{0,1:T(8,128)(2,1)S(1)}, bf16[512,1312]{0,1:T(8,128)(2,1)}, u32[]{:S(2)}) copy-start(bf16[512,1312]{0,1:T(8,128)(2,1)} %get-tuple-element.37) | copy-start | bytes 4030468
  316.5 1.6 copy-start.5
Sparse Core Ops, SparseCore 0:
  10.3 16.9 all-gather.2
  30.6 94.6 all-gather.4
  316.6 249.6 reduce-scatter.1
where the time goes:
time: 603 us; the launch traced here: 592 us
  waiting for transfers between devices  331 us (55%)
  matrix products  83.4 us (14%)
  local copies, waits for them, and re-layouts  69.5 us (12%)
  other arithmetic  41.3 us (7%)
  blocking collectives  31.6 us (5%)
  starting transfers between devices  20.5 us (3%)
  between operations  14.9 us (2%)
    reduce_scatter x1, waiting for transfers between devices, side_by_side_2(): lax.psum_scatter(both, axis, scatter_dimension=dim, tiled=True)  246 us
    all_gather x1, waiting for transfers between devices, side_by_side(): lax.all_gather(both, axis, axis=dim, tiled=True)  82.2 us
    concatenate x1, local copies, waits for them, and re-layouts, side_by_side_2(): both = jnp.concatenate(columns, axis=along)  31.6 us
    dot_general x1, matrix products, chip_body(): jnp.dot(grad_branch, reduce_back, preferred_element_type=jnp.float32)  23.7 us
    dot_general x4, matrix products, contract_first(): lax.dot_general(left, right, (((0,), (0,)), ((), ())), preferred_element_...  19.2 us
    dot_general x4, matrix products, contract_last(): lax.dot_general(left, right, (((1,), (1,)), ((), ())), preferred_element_...  16.8 us
    all_to_all x2, blocking collectives, from_everyone(): return lax.all_to_all(copies, axis, split_axis=0, concat_axis=0, tiled=True)  13.9 us
  transfers between devices with their start and end apart: 8, of which 5 were waited for; matrix products, arithmetic and copies ran while one was open for 4% of the time, Pallas kernels for 0%

commit v1 on v0

v1 whole, which is shorter than its diff:
```python
import functools

import jax
import jax.numpy as jnp
from jax import lax
from jax.experimental import pallas as pl
from jax.experimental.pallas import tpu as pltpu
from jax.sharding import Mesh
from jax.sharding import PartitionSpec as P

H = 16
HD = 64
PAIR = 2 * HD
PAIRS = H // 2
epsilon = 1e-05
rope_base = 160000.0
masked_score = -1e30
AXES = ("y", "z", "x")
ALL = ("y", "z", "x", "c")
VMEM = 60 * 1024 * 1024
bf16 = jnp.bfloat16
f32 = jnp.float32

D = 1024
FF = 2624
CHUNKS = 3
CW = 896
MIX_AT = 3 * D
GAIN_AT = 4 * D
FF_AT = 4 * D + 128
W_COLS = FF_AT + CHUNKS * 3 * CW
ROWS = 512
MIX_CUTS = ((0, 384), (384, 768), (768, 1024))
A_COLS = D + 384


def dot(a, b):
    return lax.dot_general(a, b, (((1,), (0,)), ((), ())), preferred_element_type=f32)


def dot_t(a, b):
    return lax.dot_general(a, b, (((1,), (1,)), ((), ())), preferred_element_type=f32)


def dot_first(a, b):
    return lax.dot_general(a, b, (((0,), (0,)), ((), ())), preferred_element_type=f32)


def norm_parts(values):
    centered = values - jnp.mean(values, axis=-1, keepdims=True)
    scale = lax.rsqrt(jnp.mean(centered * centered, axis=-1, keepdims=True) + epsilon)
    return centered * scale, scale


def half_swapped(v, low_half):
    return jnp.where(low_half, pltpu.roll(v, PAIR - HD // 2, 1), pltpu.roll(v, HD // 2, 1))


def pair_slice(p, at=0):
    return pl.ds(pl.multiple_of(p * PAIR + at, PAIR), PAIR)


def attend_kernel(
    tok_ref, cot_ref, seg_ref, segt_ref, cos_ref, sin_ref, perm_ref, w_ref,
    qkv_ref, prob_ref, res_ref, h2_ref, gt_ref, h1t_ref, h2t_ref, mt_ref, gtt_ref, gain_ref,
    wp, wm, wg, packed, bias, mixed, sems,
):
    copies = [
        pltpu.make_async_copy(w_ref.at[:, pl.ds(GAIN_AT, 128)], wg, sems.at[0]),
        pltpu.make_async_copy(w_ref.at[:, pl.ds(0, 3 * D)], wp, sems.at[1]),
        pltpu.make_async_copy(w_ref.at[:, pl.ds(MIX_AT, D)], wm, sems.at[2]),
    ]
    for c in copies:
        c.start()
    tokens = tok_ref[...].astype(f32)
    xhat, _ = norm_parts(tokens)
    bias[...] = jnp.where(seg_ref[...] == segt_ref[...], 0.0, masked_score)
    live = seg_ref[...] < 4
    gt = jnp.where(live, cot_ref[...].astype(f32), 0.0).astype(bf16)
    gt_ref[...] = gt
    gtt_ref[...] = dot_t(perm_ref[...], gt).astype(bf16)
    copies[0].wait()
    gains = jnp.transpose(wg[...].astype(f32))[:8]
    gain_ref[...] = gains
    h1 = (xhat * gains[0:1]).astype(bf16)
    copies[1].wait()
    packed[...] = dot(h1, wp[...])
    h1t_ref[...] = dot_t(perm_ref[...], h1).astype(bf16)
    low_half = lax.broadcasted_iota(jnp.int32, (1, PAIR), 1) % HD < HD // 2
    first = lax.broadcasted_iota(jnp.int32, (1, PAIR), 1) < HD
    zero = jnp.zeros((), bf16)

    def pair(p, carry):
        cos, sin = cos_ref[...], sin_ref[...]
        q = packed[:, pair_slice(p)]
        k = packed[:, pair_slice(p, D)]
        q = (q * cos + half_swapped(q, low_half) * sin).astype(bf16)
        k = (k * cos + half_swapped(k, low_half) * sin).astype(bf16)
        v = packed[:, pair_slice(p, 2 * D)].astype(bf16)
        qkv_ref[:, pair_slice(p)] = q
        qkv_ref[:, pair_slice(p, D)] = k
        qkv_ref[:, pair_slice(p, 2 * D)] = v
        outs = []
        for side in range(2):
            mine = first if side == 0 else jnp.logical_not(first)
            scores = dot_t(jnp.where(mine, q, zero), k) * (HD**-0.5) + bias[...]
            top = jnp.max(scores, axis=-1, keepdims=True)
            e = jnp.exp(scores - top)
            probs = e * (1.0 / jnp.sum(e, axis=-1, keepdims=True))
            prob_ref[2 * p + side] = probs
            outs.append(dot(probs.astype(bf16), v))
        mixed[:, pair_slice(p)] = jnp.where(first, outs[0], outs[1]).astype(bf16)
        return carry

    lax.fori_loop(0, PAIRS, pair, 0)
    mt_ref[...] = dot_t(perm_ref[...], mixed[...]).astype(bf16)
    copies[2].wait()
    residual = tokens + dot(mixed[...], wm[...])
    res_ref[...] = residual
    xhat2, _ = norm_parts(residual)
    h2 = (xhat2 * gains[1:2]).astype(bf16)
    h2_ref[...] = h2
    h2t_ref[...] = dot_t(perm_ref[...], h2).astype(bf16)


def gated_kernel(chunk, has_sum, *refs):
    h2_ref, gt_ref, h2t_ref, gtt_ref, w_ref = refs[:5]
    refs = refs[5:]
    if has_sum:
        branch_in, gh2_in = refs[:2]
        refs = refs[2:]
    branch_ref, gh2_ref, sib_ref, own_ref, w, gate, up, gh, hid, gg, gu, sems = refs
    base = FF_AT + chunk * 3 * CW
    copies = [
        pltpu.make_async_copy(
            w_ref.at[:, pl.ds(base + i * CW, CW)], w.at[:, pl.ds(i * CW, CW)], sems.at[i]
        )
        for i in range(3)
    ]
    for c in copies:
        c.start()
    copies[0].wait()
    gate[...] = dot(h2_ref[...], w[:, :CW])
    copies[1].wait()
    up[...] = dot(h2_ref[...], w[:, CW : 2 * CW])
    copies[2].wait()
    gh[...] = dot(gt_ref[...], w[:, 2 * CW :])
    block = 16

    def rows(i, carry):
        r = pl.ds(pl.multiple_of(i * block, block), block)
        g, u, d = gate[r, :], up[r, :], gh[r, :]
        cdf = 0.5 * (1.0 + lax.erf(g * (0.5**0.5)))
        act = g * cdf
        slope = cdf + g * (jnp.exp(-0.5 * g * g) * 0.3989422804014327)
        hid[r, :] = (act * u).astype(bf16)
        gg[r, :] = (d * u * slope).astype(bf16)
        gu[r, :] = (d * act).astype(bf16)
        return carry

    lax.fori_loop(0, gate.shape[0] // block, rows, 0)
    for to, rows_at in ((sib_ref, 0), (own_ref, ROWS)):
        h2t = h2t_ref[pl.ds(rows_at, ROWS), :]
        gtt = gtt_ref[pl.ds(rows_at, ROWS), :]
        to[:, pl.ds(0, CW)] = dot(h2t, gg[...]).astype(bf16)
        to[:, pl.ds(CW, CW)] = dot(h2t, gu[...]).astype(bf16)
        to[:, pl.ds(2 * CW, CW)] = dot(gtt, hid[...]).astype(bf16)
    branch = dot_t(hid[...], w[:, 2 * CW :])
    gh2 = dot_t(gg[...], w[:, :CW]) + dot_t(gu[...], w[:, CW : 2 * CW])
    if has_sum:
        branch = branch + branch_in[...]
        gh2 = gh2 + gh2_in[...]
    branch_ref[...] = branch
    gh2_ref[...] = gh2


def back_kernel(
    tok_ref, gt_ref, seg_ref, cos_ref, sin_ref, perm_ref, gain_ref, res_ref, branch_ref, gh2_ref,
    qkv_ref, prob_ref, h1t_ref, mt_ref, w_ref,
    out_ref, gin_ref, *rest,
):
    sibs, owns = rest[:3], rest[3:6]
    wp, wm, gr, gm, gp, sems = rest[6:]
    copies = [
        pltpu.make_async_copy(w_ref.at[:, pl.ds(MIX_AT, D)], wm, sems.at[0]),
        pltpu.make_async_copy(w_ref.at[:, pl.ds(0, 3 * D)], wp, sems.at[1]),
    ]
    for c in copies:
        c.start()
    residual = res_ref[...]
    live = seg_ref[...] < 4
    out_ref[...] = jnp.where(live, residual + branch_ref[...], 0.0).astype(bf16)
    xhat2, r2 = norm_parts(residual)
    gh2 = gh2_ref[...]
    second = jnp.sum(gh2 * xhat2, axis=0, keepdims=True)
    n = gh2 * gain_ref[1:2]
    spread = jnp.mean(n * xhat2, axis=-1, keepdims=True)
    grad_res = gt_ref[...].astype(f32) + r2 * (
        n - jnp.mean(n, axis=-1, keepdims=True) - xhat2 * spread
    )
    gr[...] = grad_res
    ga = grad_res.astype(bf16)
    copies[0].wait()
    gm[...] = dot_t(ga, wm[...]).astype(bf16)
    for half, group in ((0, sibs), (ROWS, owns)):
        mt = mt_ref[pl.ds(half, ROWS), :]
        for (lo, hi), to in zip(MIX_CUTS, group):
            to[:, pl.ds(D, hi - lo)] = dot(mt, ga[:, lo:hi]).astype(bf16)
    low_half = lax.broadcasted_iota(jnp.int32, (1, PAIR), 1) % HD < HD // 2
    first = lax.broadcasted_iota(jnp.int32, (1, PAIR), 1) < HD
    zero = jnp.zeros((), bf16)

    def pair(p, carry):
        cos, sin = cos_ref[...], sin_ref[...]
        q = qkv_ref[:, pair_slice(p)]
        k = qkv_ref[:, pair_slice(p, D)]
        v = qkv_ref[:, pair_slice(p, 2 * D)]
        g = gm[:, pair_slice(p)]
        dq, dk, dv = [], [], []
        for side in range(2):
            mine = first if side == 0 else jnp.logical_not(first)
            probs = prob_ref[2 * p + side]
            grad_probs = dot_t(jnp.where(mine, g, zero), v)
            weighted = probs * grad_probs
            delta = jnp.sum(weighted, axis=-1, keepdims=True)
            gs = (weighted - probs * delta).astype(bf16)
            dq.append(dot(gs, k))
            dk.append(dot_first(gs, q))
            dv.append(dot_first(probs.astype(bf16), g))
        dq = jnp.where(first, dq[0], dq[1]) * (HD**-0.5)
        dk = jnp.where(first, dk[0], dk[1]) * (HD**-0.5)
        dv = jnp.where(first, dv[0], dv[1])
        gp[:, pair_slice(p)] = (dq * cos - half_swapped(dq, low_half) * sin).astype(bf16)
        gp[:, pair_slice(p, D)] = (dk * cos - half_swapped(dk, low_half) * sin).astype(bf16)
        gp[:, pair_slice(p, 2 * D)] = dv.astype(bf16)
        return carry

    lax.fori_loop(0, PAIRS, pair, 0)
    for half, group in ((0, sibs), (ROWS, owns)):
        h1t = h1t_ref[pl.ds(half, ROWS), :]
        for i, to in enumerate(group):
            to[:, pl.ds(0, D)] = dot(h1t, gp[:, i * D : (i + 1) * D]).astype(bf16)
    copies[1].wait()
    gh1 = dot_t(gp[...], wp[...])
    xhat1, r1 = norm_parts(tok_ref[...].astype(f32))
    one = jnp.sum(gh1 * xhat1, axis=0, keepdims=True)
    m = gh1 * gain_ref[0:1]
    spread = jnp.mean(m * xhat1, axis=-1, keepdims=True)
    gin_ref[...] = gr[...] + r1 * (m - jnp.mean(m, axis=-1, keepdims=True) - xhat1 * spread)
    at = lax.broadcasted_iota(jnp.int32, (128, D), 0)
    both = jnp.where(at == 0, one, jnp.where(at == 1, second, 0.0)).astype(bf16)
    for half, group in ((0, sibs), (ROWS, owns)):
        group[2][:, pl.ds(D + 256, 128)] = dot_t(perm_ref[pl.ds(half, ROWS), :], both).astype(bf16)


def arr(shape, dtype):
    return jax.ShapeDtypeStruct(shape, dtype)


VSPEC = pl.BlockSpec(memory_space=pltpu.VMEM)
HSPEC = pl.BlockSpec(memory_space=pl.ANY)
PARAMS = pltpu.CompilerParams(vmem_limit_bytes=VMEM)


def token_layout(lengths, slot_count):
    places = jnp.arange(slot_count, dtype=jnp.int32)
    ends = jnp.cumsum(lengths)
    starts = ends - lengths
    segment = jnp.sum((places[:, None] >= ends[None, :]).astype(jnp.int32), axis=1)
    live = places < ends[-1]
    picked = (segment[:, None] == jnp.arange(lengths.shape[0], dtype=jnp.int32)[None, :]).astype(
        jnp.int32
    )
    position = jnp.where(live, places - jnp.sum(picked * starts[None, :], axis=1), 0)
    segment = jnp.where(live, segment, lengths.shape[0] + places)
    return segment, position


def rotary_tables(position):
    frequency = rope_base ** (-(jnp.arange(HD // 2, dtype=f32) * 2.0 / HD))
    angles = position.astype(f32)[:, None] * frequency
    cos, sin = jnp.cos(angles), jnp.sin(angles)
    return (
        jnp.concatenate([cos, cos, cos, cos], axis=-1),
        jnp.concatenate([-sin, sin, -sin, sin], axis=-1),
    )


def row_order(core):
    row = jnp.arange(D, dtype=jnp.int32)
    inner = row % ROWS
    side = jnp.where(row < ROWS, 1 - core, core)
    feature = inner // 8 * 16 + side * 8 + inner % 8
    return (feature[:, None] == jnp.arange(D, dtype=jnp.int32)[None, :]).astype(bf16)


def local_step(tokens, cotangent, lengths, core, weights):
    n = tokens.shape[0]
    segment, position = token_layout(lengths, n)
    cos, sin = rotary_tables(position)
    seg_col, seg_row = segment[:, None], segment[None, :]
    perm = row_order(core)
    qkv, probs, residual, h2, gt, h1t, h2t, mt, gtt, gains = pl.pallas_call(
        attend_kernel,
        out_shape=(
            arr((n, 3 * D), bf16), arr((H, n, n), f32), arr((n, D), f32), arr((n, D), bf16),
            arr((n, D), bf16), arr((D, n), bf16), arr((D, n), bf16), arr((D, n), bf16),
            arr((D, n), bf16), arr((8, D), f32),
        ),
        in_specs=[VSPEC] * 7 + [HSPEC],
        out_specs=(VSPEC,) * 10,
        scratch_shapes=[
            pltpu.VMEM((D, 3 * D), bf16), pltpu.VMEM((D, D), bf16), pltpu.VMEM((D, 128), bf16),
            pltpu.VMEM((n, 3 * D), f32), pltpu.VMEM((n, n), f32), pltpu.VMEM((n, D), bf16),
            pltpu.SemaphoreType.DMA((3,)),
        ],
        compiler_params=PARAMS,
        name="attend",
    )(tokens, cotangent, seg_col, seg_row, cos, sin, perm, weights)
    sums = ()
    ff_sib, ff_own = [], []
    for chunk in range(CHUNKS):
        *sums, sib, own = pl.pallas_call(
            functools.partial(gated_kernel, chunk, chunk > 0),
            out_shape=(
                arr((n, D), f32), arr((n, D), f32),
                arr((ROWS, 3 * CW), bf16), arr((ROWS, 3 * CW), bf16),
            ),
            in_specs=[VSPEC] * 4 + [HSPEC] + [VSPEC] * len(sums),
            out_specs=(VSPEC,) * 4,
            scratch_shapes=[pltpu.VMEM((D, 3 * CW), bf16)]
            + [pltpu.VMEM((n, CW), f32)] * 3
            + [pltpu.VMEM((n, CW), bf16)] * 3
            + [pltpu.SemaphoreType.DMA((3,))],
            compiler_params=PARAMS,
            name="gated",
        )(h2, gt, h2t, gtt, weights, *sums)
        ff_sib.append(sib)
        ff_own.append(own)
    branch, gh2 = sums
    block_output, input_grad, *att = pl.pallas_call(
        back_kernel,
        out_shape=(arr((n, D), bf16), arr((n, D), f32)) + (arr((ROWS, A_COLS), bf16),) * 6,
        in_specs=[VSPEC] * 14 + [HSPEC],
        out_specs=(VSPEC,) * 8,
        scratch_shapes=[
            pltpu.VMEM((D, 3 * D), bf16), pltpu.VMEM((D, D), bf16), pltpu.VMEM((n, D), f32),
            pltpu.VMEM((n, D), bf16), pltpu.VMEM((n, 3 * D), bf16), pltpu.SemaphoreType.DMA((2,)),
        ],
        compiler_params=PARAMS,
        name="back",
    )(
        tokens, gt, seg_col, cos, sin, perm, gains, residual, branch, gh2,
        qkv, probs, h1t, mt, weights,
    )
    return block_output, input_grad, ff_sib, ff_own, att[:3], att[3:]


def ring_pairs(n):
    return [(i * 2 + c, (i + 1 - 2 * c) % n * 2 + c) for i in range(n) for c in range(2)]


def onward(a, axis):
    return lax.ppermute(a, (axis, "c"), ring_pairs(lax.axis_size(axis)))


def picked(a, dim, j):
    return lax.dynamic_index_in_dim(a, jnp.mod(j, a.shape[dim]), dim, keepdims=False)


def ring_sum(a, dim, axis, last):
    step = 1 - 2 * lax.axis_index("c")
    me = lax.axis_index(axis)
    n = lax.axis_size(axis)
    current = picked(a, dim, me - step)
    for s in range(n - 1):
        current = onward(current, axis).astype(f32) + picked(a, dim, me - (s + 2) * step).astype(
            f32
        )
        if s < n - 2 or not last:
            current = current.astype(bf16)
    return current


def summed_part(sib, own, order):
    arrived = lax.ppermute(sib, "c", [(0, 1), (1, 0)])
    sizes = tuple(lax.axis_size(a) for a in AXES)
    whole = (own.astype(f32) + arrived.astype(f32)).astype(bf16).reshape(*sizes, 8, -1)
    left = list(AXES)
    for i, axis in enumerate(order):
        whole = ring_sum(whole, left.index(axis), axis, i == len(order) - 1)
        left.remove(axis)
    return whole


ORDERS = (("x", "y", "z"), ("y", "z", "x"), ("z", "x", "y"))


def body(
    tokens, packed_proj, mixer_proj, expand_proj, reduce_proj, first_gain, second_gain,
    sequence_lengths, cotangent,
):
    rows = packed_proj.shape[0]
    core = lax.axis_index("c")
    pad = CHUNKS * CW - FF
    gate, up, red = (
        jnp.pad(w, ((0, 0), (0, pad)))
        for w in (expand_proj[:, :FF], expand_proj[:, FF:], reduce_proj)
    )
    gains = jnp.pad(jnp.stack([first_gain, second_gain], axis=1), ((0, 0), (0, 126)))
    pieces = [packed_proj, mixer_proj, gains]
    for j in range(CHUNKS):
        pieces += [w[:, j * CW : (j + 1) * CW] for w in (gate, up, red)]
    shard = jnp.concatenate(pieces, axis=1)
    weights = lax.all_gather(shard, ALL, axis=0, tiled=True)
    block_output, input_grad, ff_sib, ff_own, att_sib, att_own = local_step(
        tokens, cotangent, sequence_lengths, core, weights
    )
    ff = [summed_part(s, o, order) for s, o, order in zip(ff_sib, ff_own, ORDERS)]
    att = [summed_part(s, o, order) for s, o, order in zip(att_sib, att_own, ORDERS)]
    ff = [f.reshape(rows, 3 * CW) for f in ff]
    att = [a.reshape(rows, A_COLS) for a in att]
    gate_g, up_g, red_g = (
        jnp.concatenate([f[:, i * CW : (i + 1) * CW] for f in ff], axis=1)[:, :FF]
        for i in range(3)
    )
    return (
        block_output,
        input_grad,
        jnp.concatenate([a[:, :D] for a in att], axis=1),
        jnp.concatenate([a[:, D : D + hi - lo] for a, (lo, hi) in zip(att, MIX_CUTS)], axis=1),
        jnp.concatenate([gate_g, up_g], axis=1),
        red_g,
        att[2][:, D + 256],
        att[2][:, D + 257],
    )


def solution(mesh):
    torus = Mesh(mesh.devices.reshape(4, 4, 4, 2), ALL)
    row, flat = P(ALL, None), P(ALL)
    return jax.shard_map(
        body,
        mesh=torus,
        in_specs=(row,) * 5 + (flat, flat, flat, row),
        out_specs=(row,) * 6 + (flat, flat),
        check_vma=False,
    )
```

time: 603 us -> 383 us (0.64)
  the two profiles are of different devices: /device:TPU:1 before, /device:TPU:0 now
where the time goes in v1:
time: 383 us; the launch traced here: 378 us
  waiting for transfers between devices  219 us (57%)
  Pallas kernels  80.5 us (21%)
  starting transfers between devices  32.3 us (8%)
  other arithmetic  20 us (5%)
  between operations  15.3 us (4%)
  local copies, waits for them, and re-layouts  10.9 us (3%)
    ppermute x54, waiting for transfers between devices, onward(): return lax.ppermute(a, (axis, 'c'), ring_pairs(lax.axis_size(axis)))  118 us
    all_gather x1, waiting for transfers between devices, body(): weights = lax.all_gather(shard, ALL, axis=0, tiled=True)  86.8 us
    pallas_call x3, Pallas kernels, local_step(): pl.pallas_call(functools.partial(gated_kernel, chunk, chunk > 0), out_sha...  36.5 us
    ppermute x54, starting transfers between devices, onward(): return lax.ppermute(a, (axis, 'c'), ring_pairs(lax.axis_size(axis)))  30.7 us
    pallas_call x1, Pallas kernels, local_step(): pl.pallas_call(back_kernel, out_shape=(arr((n, D), bf16), arr((n, D), f32...  22.5 us
    pallas_call x1, Pallas kernels, local_step(): pl.pallas_call(attend_kernel, out_shape=(arr((n, 3 * D), bf16), arr((H, n...  21.5 us
    ppermute x6, waiting for transfers between devices, summed_part(): arrived = lax.ppermute(sib, 'c', [(0, 1), (1, 0)])  14 us
  transfers between devices with their start and end apart: 61, of which 48 were waited for; matrix products, arithmetic and copies ran while one was open for 5% of the time, Pallas kernels for 0%

profile of v1, /device:TPU:0, one launch (start us, length us, event | category | flops | bytes accessed | tf_op | source)
XLA Modules:
  0.0 377.6 jit_solution(1483063921006824399)
XLA Ops:
  7.2 0.9 slice.113
  8.1 0.8 slice_select_fusion
  8.9 0.8 constant_dynamic-update-slice_fusion.11
  11.2 0.8 constant_dynamic-update-slice_fusion.7
  12.7 0.8 constant_dynamic-update-slice_fusion.4
  15.7 0.8 reduce-window.4
  19.3 1.0 pad_maximum_fusion.3
  20.3 1.2 compare_select_fusion.segt_ref
  21.5 1.3 add_select_fusion.seg_ref
  22.8 1.8 fusion.perm_ref
  24.6 86.8 %all-gather.2.cloned.1.call-done.w_ref.refs_4_ = bf16[1024,12288]{1,0:T(8,128)(2,1)} async-done(((bf16[8,12288]{1,0:T(8,128)(2,1)}), bf16[1024,12288]{1,0:T(8,128)(2,1)}) %all-gather.2.cloned.1.call-update) | async-done | bytes 25165840 | tf_op jit(solution)/shard_map/all_gather | solution.py:415
  111.4 21.5 %attend.1 = (bf16[256,3072]{1,0:T(8,128)(2,1)}, f32[16,256,256]{2,1,0:T(8,128)}, f32[256,1024]{1,0:T(8,128)}, bf16[256,1024]{1,0:T(8,128)(2,1)}, bf16[256,1024]{...) custom-call(bf16[256,1024]{1,0:T(8,128)(2,1)} %tok_ref.3, ...), custom_call_target="tpu_custom_call" | custom-call | tf_op jit(solution)/shard_map/attend/pallas_call | solution.py:303
  132.9 11.3 %gated.3 = (f32[256,1024]{1,0:T(8,128)}, f32[256,1024]{1,0:T(8,128)}, bf16[512,2688]{1,0:T(8,128)(2,1)}, bf16[512,2688]{1,0:T(8,128)(2,1)}) custom-call(bf16[256,1024]{1,0:T(8,128)(2,1)} %get-tuple-element.41.refs_0_, bf16[256,1024]{1,0:T(8,128)(2,1)} %get-tuple-element.38.refs_1_.gt_ref, bf16[1024,256]{1,0:T(8,128)(2,1)} %get-tuple-element.42.refs_2_, ...), custom_call_target="tpu_custom_call" | custom-call | tf_op jit(solution)/shard_map/gated/pallas_call | solution.py:323
  144.2 12.8 %gated.4 = (f32[256,1024]{1,0:T(8,128)}, f32[256,1024]{1,0:T(8,128)}, bf16[512,2688]{1,0:T(8,128)(2,1)}, bf16[512,2688]{1,0:T(8,128)(2,1)}) custom-call(bf16[256,1024]{1,0:T(8,128)(2,1)} %get-tuple-element.41.refs_0_, bf16[256,1024]{1,0:T(8,128)(2,1)} %get-tuple-element.38.refs_1_.gt_ref, bf16[1024,256]{1,0:T(8,128)(2,1)} %get-tuple-element.42.refs_2_, ...), custom_call_target="tpu_custom_call" | custom-call | tf_op jit(solution)/shard_map/gated/pallas_call | solution.py:323
  157.0 12.4 %gated.5 = (f32[256,1024]{1,0:T(8,128)}, f32[256,1024]{1,0:T(8,128)}, bf16[512,2688]{1,0:T(8,128)(2,1)}, bf16[512,2688]{1,0:T(8,128)(2,1)}) custom-call(bf16[256,1024]{1,0:T(8,128)(2,1)} %get-tuple-element.41.refs_0_, bf16[256,1024]{1,0:T(8,128)(2,1)} %get-tuple-element.38.refs_1_.gt_ref, bf16[1024,256]{1,0:T(8,128)(2,1)} %get-tuple-element.42.refs_2_, ...), custom_call_target="tpu_custom_call" | custom-call | tf_op jit(solution)/shard_map/gated/pallas_call | solution.py:323
  169.4 22.5 %back.1 = (bf16[256,1024]{1,0:T(8,128)(2,1)}, f32[256,1024]{1,0:T(8,128)}, bf16[512,1408]{1,0:T(8,128)(2,1)}, bf16[512,1408]{1,0:T(8,128)(2,1)}, bf16[512,1408]{...) custom-call(bf16[256,1024]{1,0:T(8,128)(2,1)} %tok_ref.3, ...), custom_call_target="tpu_custom_call" | custom-call | tf_op jit(solution)/shard_map/back/pallas_call | solution.py:341
  193.3 2.2 collective-permute-done
  195.7 1.8 add_convert_fusion.5
  197.6 1.5 collective-permute-start.1
  199.5 11.9 %collective-permute-done.20 = bf16[512,1408]{1,0:T(8,128)(2,1)S(1)} collective-permute-done((bf16[512,1408]{1,0:T(8,128)(2,1)}, bf16[512,1408]{1,0:T(8,128)(2,1)S(1)}, u32[]{:S(2)}, u32[]{:S(2)}) %collective-permute-start.20) | collective-permute-done | bytes 1441824 | tf_op jit(solution)/shard_map/ppermute | solution.py:386
  211.4 1.5 collective-permute-start.11
  213.5 1.0 collective-permute-start.21
  214.6 5.4 %collective-permute-done.11 = bf16[4,4,8,1408]{3,2,1,0:T(8,128)(2,1)S(1)} collective-permute-done((bf16[4,4,8,1408]{3,2,1,0:T(8,128)(2,1)S(1)}, bf16[4,4,8,1408]{3,2,1,0:T(8,128)(2,1)S(1)}, u32[]{:S(2)}, u32[]{:S(2)}) %collective-permute-start.11) | collective-permute-done | bytes 360480 | tf_op jit(solution)/shard_map/ppermute | solution.py:364
  220.1 1.5 collective-permute-start.2
  222.2 1.5 collective-permute-start.12
  223.8 4.9 %collective-permute-done.2 = bf16[4,4,8,1408]{3,2,1,0:T(8,128)(2,1)S(1)} collective-permute-done((bf16[4,4,8,1408]{3,2,1,0:T(8,128)(2,1)S(1)}, bf16[4,4,8,1408]{3,2,1,0:T(8,128)(2,1)S(1)}, u32[]{:S(2)}, u32[]{:S(2)}) %collective-permute-start.2) | collective-permute-done | bytes 360480 | tf_op jit(solution)/shard_map/ppermute | solution.py:364
  228.7 0.9 collective-permute-start.22
  229.7 1.1 collective-permute-done.12
  230.8 1.5 collective-permute-start.3
  232.4 4.9 %collective-permute-done.22 = bf16[4,4,8,1408]{3,2,0,1:T(8,128)(2,1)S(1)} collective-permute-done((bf16[4,4,8,1408]{3,2,0,1:T(8,128)(2,1)S(1)}, bf16[4,4,8,1408]{3,2,0,1:T(8,128)(2,1)S(1)}, u32[]{:S(2)}, u32[]{:S(2)}) %collective-permute-start.22) | collective-permute-done | bytes 360480 | tf_op jit(solution)/shard_map/ppermute | solution.py:364
  237.7 1.8 collective-permute-done.3
  240.1 5.8 %collective-permute-done.13 = bf16[4,4,8,1408]{3,2,1,0:T(8,128)(2,1)S(1)} collective-permute-done((bf16[4,4,8,1408]{3,2,1,0:T(8,128)(2,1)S(1)}, bf16[4,4,8,1408]{3,2,1,0:T(8,128)(2,1)S(1)}, u32[]{:S(2)}, u32[]{:S(2)}) %collective-permute-start.13) | collective-permute-done | bytes 360480 | tf_op jit(solution)/shard_map/ppermute | solution.py:364
  246.1 2.0 collective-permute-done.23
  248.4 3.3 collective-permute-done.4
  252.0 2.0 collective-permute-done.14
  254.3 3.1 collective-permute-done.24
  257.5 2.3 collective-permute-done.5
  260.1 3.1 collective-permute-done.15
  263.2 2.3 collective-permute-done.25
  268.3 1.0 copy-done
  271.3 1.7 collective-permute-start.7
  273.5 9.3 %collective-permute-done.7 = bf16[8,1408]{1,0:T(8,128)(2,1)S(1)} collective-permute-done((bf16[8,1408]{1,0:T(8,128)(2,1)S(1)}, bf16[8,1408]{1,0:T(8,128)(2,1)S(1)}, u32[]{:S(2)}, u32[]{:S(2)}) %collective-permute-start.7) | collective-permute-done | bytes 22560 | tf_op jit(solution)/shard_map/ppermute | solution.py:364
  282.9 4.9 %collective-permute-done.27 = bf16[8,1408]{1,0:T(8,128)(2,1)S(1)} collective-permute-done((bf16[8,1408]{1,0:T(8,128)(2,1)S(1)}, bf16[8,1408]{1,0:T(8,128)(2,1)S(1)}, u32[]{:S(2)}, u32[]{:S(2)}) %collective-permute-start.27) | collective-permute-done | bytes 22560 | tf_op jit(solution)/shard_map/ppermute | solution.py:364
  288.5 0.8 collective-permute-start.28
  289.4 3.4 collective-permute-done.18
  293.6 3.0 collective-permute-start.19
  296.6 1.2 collective-permute-done.9
  298.6 4.2 %collective-permute-done.29 = bf16[8,1408]{1,0:T(8,128)(2,1)S(1)} collective-permute-done((bf16[8,1408]{1,0:T(8,128)(2,1)S(1)}, bf16[8,1408]{1,0:T(8,128)(2,1)S(1)}, u32[]{:S(2)}, u32[]{:S(2)}) %collective-permute-start.29) | collective-permute-done | bytes 22560 | tf_op jit(solution)/shard_map/ppermute | solution.py:364
  306.1 11.2 %collective-permute-done.32 = bf16[4,4,8,2688]{3,2,1,0:T(8,128)(2,1)S(1)} collective-permute-done((bf16[4,4,8,2688]{3,2,1,0:T(8,128)(2,1)S(1)}, bf16[4,4,8,2688]{3,2,1,0:T(8,128)(2,1)S(1)}, u32[]{:S(2)}, u32[]{:S(2)}) %collective-permute-start.32) | collective-permute-done | bytes 688160 | tf_op jit(solution)/shard_map/ppermute | solution.py:364
  318.5 11.2 %collective-permute-done.33 = bf16[4,4,8,2688]{3,2,1,0:T(8,128)(2,1)S(1)} collective-permute-done((bf16[4,4,8,2688]{3,2,1,0:T(8,128)(2,1)S(1)}, bf16[4,4,8,2688]{3,2,1,0:T(8,128)(2,1)S(1)}, u32[]{:S(2)}, u32[]{:S(2)}) %collective-permute-start.33) | collective-permute-done | bytes 688160 | tf_op jit(solution)/shard_map/ppermute | solution.py:364
  330.8 2.4 collective-permute-start.54
  333.1 3.4 collective-permute-done.34
  337.5 2.0 collective-permute-start.55
  339.5 3.8 %collective-permute-done.35 = bf16[4,8,2688]{2,1,0:T(8,128)(2,1)S(1)} collective-permute-done((bf16[4,8,2688]{2,1,0:T(8,128)(2,1)S(1)}, bf16[4,8,2688]{2,1,0:T(8,128)(2,1)S(1)}, u32[]{:S(2)}, u32[]{:S(2)}) %collective-permute-start.35) | collective-permute-done | bytes 172064 | tf_op jit(solution)/shard_map/ppermute | solution.py:364
  344.2 2.0 collective-permute-start.56
  346.2 3.8 %collective-permute-done.36 = bf16[4,8,2688]{2,1,0:T(8,128)(2,1)S(1)} collective-permute-done((bf16[4,8,2688]{2,1,0:T(8,128)(2,1)S(1)}, bf16[4,8,2688]{2,1,0:T(8,128)(2,1)S(1)}, u32[]{:S(2)}, u32[]{:S(2)}) %collective-permute-start.36) | collective-permute-done | bytes 172064 | tf_op jit(solution)/shard_map/ppermute | solution.py:364
  350.5 2.4 collective-permute-start.47
  353.0 2.4 collective-permute-done.37
  355.8 1.2 collective-permute-start.48
  357.0 1.3 collective-permute-done.57
  358.3 2.4 collective-permute-done.38
  361.2 2.3 collective-permute-done.58
  363.6 2.4 collective-permute-done.39
  366.5 2.4 collective-permute-done.59
  (200 shorter events, 31.2 us)
Async XLA Ops:
  7.2 104.2 %all-gather.2.cloned.1.call-start = ((), (), s32[]{:S(2)}) async-start(), calls=%async_computation | async-start | bytes 25362432 | tf_op jit(solution)/shard_map/all_gather | solution.py:415
  192.0 3.5 collective-permute-start
  192.3 5.3 %collective-permute-start.10 = (bf16[512,1408]{1,0:T(8,128)(2,1)}, bf16[512,1408]{1,0:T(8,128)(2,1)S(1)}, u32[]{:S(2)}, u32[]{:S(2)}) collective-permute-start(bf16[512,1408]{1,0:T(8,128)(2,1)} %get-tuple-element.59), channel_id=1, source_target_pairs={{0,1},{1,0},{2,3},{3,2},{4,5},{5,4},{6,7},{7,6},{8,9},{9,8},{10,11... | collective-permute-start | bytes 4325384 | tf_op jit(solution)/shard_map/ppermute | solution.py:386
  192.6 73.0 %collective-permute-start.30 = (bf16[512,2688]{1,0:T(8,128)(2,1)}, bf16[512,2688]{1,0:T(8,128)(2,1)S(1)}, u32[]{:S(2)}, u32[]{:S(2)}) collective-permute-start(bf16[512,2688]{1,0:T(8,128)(2,1)} %get-tuple-element.63), channel_id=1, source_target_pairs={{0,1},{1,0},{2,3},{3,2},{4,5},{5,4},{6,7},{7,6},{8,9},{9,8},{10,11... | collective-permute-start | bytes 8257544 | tf_op jit(solution)/shard_map/ppermute | solution.py:386
  192.8 73.6 %collective-permute-start.40 = (bf16[512,2688]{1,0:T(8,128)(2,1)}, bf16[512,2688]{1,0:T(8,128)(2,1)S(1)}, u32[]{:S(2)}, u32[]{:S(2)}) collective-permute-start(bf16[512,2688]{1,0:T(8,128)(2,1)} %get-tuple-element.65), channel_id=1, source_target_pairs={{0,1},{1,0},{2,3},{3,2},{4,5},{5,4},{6,7},{7,6},{8,9},{9,8},{10,11... | collective-permute-start | bytes 8257544 | tf_op jit(solution)/shard_map/ppermute | solution.py:386
  193.1 75.1 %collective-permute-start.50 = (bf16[512,2688]{1,0:T(8,128)(2,1)}, bf16[512,2688]{1,0:T(8,128)(2,1)S(1)}, u32[]{:S(2)}, u32[]{:S(2)}) collective-permute-start(bf16[512,2688]{1,0:T(8,128)(2,1)} %get-tuple-element.67), channel_id=1, source_target_pairs={{0,1},{1,0},{2,3},{3,2},{4,5},{5,4},{6,7},{7,6},{8,9},{9,8},{10,11... | collective-permute-start | bytes 8257544 | tf_op jit(solution)/shard_map/ppermute | solution.py:386
  195.5 15.9 %collective-permute-start.20 = (bf16[512,1408]{1,0:T(8,128)(2,1)}, bf16[512,1408]{1,0:T(8,128)(2,1)S(1)}, u32[]{:S(2)}, u32[]{:S(2)}) collective-permute-start(bf16[512,1408]{1,0:T(8,128)(2,1)} %get-tuple-element.61), channel_id=1, source_target_pairs={{0,1},{1,0},{2,3},{3,2},{4,5},{5,4},{6,7},{7,6},{8,9},{9,8},{10,11... | collective-permute-start | bytes 4325384 | tf_op jit(solution)/shard_map/ppermute | solution.py:386
  195.7 3.4 copy-start.4
  197.6 15.9 %collective-permute-start.1 = (bf16[4,4,8,1408]{3,2,1,0:T(8,128)(2,1)S(1)}, bf16[4,4,8,1408]{3,2,1,0:T(8,128)(2,1)S(1)}, u32[]{:S(2)}, u32[]{:S(2)}) collective-permute-start(bf16[4,4,8,1408]{3,2,1,0:T(8,128)(2,1)S(1)} %dynamic-slice_bitcast_fusion.3), channel_id=1, source_target_pairs={{0,2},{1,7},{2,4},{3,1},{4,6},{5,3},{6,0},{7,5},{8,10},{9,15},{10,... | collective-permute-start | bytes 1081352 | tf_op jit(solution)/shard_map/ppermute | solution.py:364
  199.2 13.8 %copy-start.3 = (bf16[512,1408]{1,0:T(8,128)(2,1)S(1)}, bf16[512,1408]{1,0:T(8,128)(2,1)}, u32[]{:S(2)}) copy-start(bf16[512,1408]{1,0:T(8,128)(2,1)} %get-tuple-element.60) | copy-start | bytes 4325380
  211.4 8.6 %collective-permute-start.11 = (bf16[4,4,8,1408]{3,2,1,0:T(8,128)(2,1)S(1)}, bf16[4,4,8,1408]{3,2,1,0:T(8,128)(2,1)S(1)}, u32[]{:S(2)}, u32[]{:S(2)}) collective-permute-start(bf16[4,4,8,1408]{3,2,1,0:T(8,128)(2,1)S(1)} %dynamic-slice_bitcast_fusion.2), channel_id=1, source_target_pairs={{0,32},{1,97},{32,64},{33,1},{64,96},{65,33},{96,0},{97,65},{2,34}... | collective-permute-start | bytes 1081352 | tf_op jit(solution)/shard_map/ppermute | solution.py:364
  213.5 8.7 %collective-permute-start.21 = (bf16[4,4,8,1408]{3,2,0,1:T(8,128)(2,1)S(1)}, bf16[4,4,8,1408]{3,2,0,1:T(8,128)(2,1)S(1)}, u32[]{:S(2)}, u32[]{:S(2)}) collective-permute-start(bf16[4,4,8,1408]{3,2,0,1:T(8,128)(2,1)S(1)} %bitcast.257), channel_id=1, source_target_pairs={{0,8},{1,25},{8,16},{9,1},{16,24},{17,9},{24,0},{25,17},{2,10},{3,... | collective-permute-start | bytes 1081352 | tf_op jit(solution)/shard_map/ppermute | solution.py:364
  220.1 8.6 %collective-permute-start.2 = (bf16[4,4,8,1408]{3,2,1,0:T(8,128)(2,1)S(1)}, bf16[4,4,8,1408]{3,2,1,0:T(8,128)(2,1)S(1)}, u32[]{:S(2)}, u32[]{:S(2)}) collective-permute-start(bf16[4,4,8,1408]{3,2,1,0:T(8,128)(2,1)S(1)} %fusion.18), channel_id=1, source_target_pairs={{0,2},{1,7},{2,4},{3,1},{4,6},{5,3},{6,0},{7,5},{8,10},{9,15},{10,... | collective-permute-start | bytes 1081352 | tf_op jit(solution)/shard_map/ppermute | solution.py:364
  222.2 8.6 %collective-permute-start.12 = (bf16[4,4,8,1408]{3,2,1,0:T(8,128)(2,1)S(1)}, bf16[4,4,8,1408]{3,2,1,0:T(8,128)(2,1)S(1)}, u32[]{:S(2)}, u32[]{:S(2)}) collective-permute-start(bf16[4,4,8,1408]{3,2,1,0:T(8,128)(2,1)S(1)} %fusion.15), channel_id=1, source_target_pairs={{0,32},{1,97},{32,64},{33,1},{64,96},{65,33},{96,0},{97,65},{2,34}... | collective-permute-start | bytes 1081352 | tf_op jit(solution)/shard_map/ppermute | solution.py:364
  228.7 8.6 %collective-permute-start.22 = (bf16[4,4,8,1408]{3,2,0,1:T(8,128)(2,1)S(1)}, bf16[4,4,8,1408]{3,2,0,1:T(8,128)(2,1)S(1)}, u32[]{:S(2)}, u32[]{:S(2)}) collective-permute-start(bf16[4,4,8,1408]{3,2,0,1:T(8,128)(2,1)S(1)} %fusion.12), channel_id=1, source_target_pairs={{0,8},{1,25},{8,16},{9,1},{16,24},{17,9},{24,0},{25,17},{2,10},{3,... | collective-permute-start | bytes 1081352 | tf_op jit(solution)/shard_map/ppermute | solution.py:364
  230.8 8.6 %collective-permute-start.3 = (bf16[4,4,8,1408]{3,2,1,0:T(8,128)(2,1)S(1)}, bf16[4,4,8,1408]{3,2,1,0:T(8,128)(2,1)S(1)}, u32[]{:S(2)}, u32[]{:S(2)}) collective-permute-start(bf16[4,4,8,1408]{3,2,1,0:T(8,128)(2,1)S(1)} %fusion.17), channel_id=1, source_target_pairs={{0,2},{1,7},{2,4},{3,1},{4,6},{5,3},{6,0},{7,5},{8,10},{9,15},{10,... | collective-permute-start | bytes 1081352 | tf_op jit(solution)/shard_map/ppermute | solution.py:364
  237.3 8.6 %collective-permute-start.13 = (bf16[4,4,8,1408]{3,2,1,0:T(8,128)(2,1)S(1)}, bf16[4,4,8,1408]{3,2,1,0:T(8,128)(2,1)S(1)}, u32[]{:S(2)}, u32[]{:S(2)}) collective-permute-start(bf16[4,4,8,1408]{3,2,1,0:T(8,128)(2,1)S(1)} %fusion.14), channel_id=1, source_target_pairs={{0,32},{1,97},{32,64},{33,1},{64,96},{65,33},{96,0},{97,65},{2,34}... | collective-permute-start | bytes 1081352 | tf_op jit(solution)/shard_map/ppermute | solution.py:364
  239.5 8.6 %collective-permute-start.23 = (bf16[4,4,8,1408]{3,2,0,1:T(8,128)(2,1)S(1)}, bf16[4,4,8,1408]{3,2,0,1:T(8,128)(2,1)S(1)}, u32[]{:S(2)}, u32[]{:S(2)}) collective-permute-start(bf16[4,4,8,1408]{3,2,0,1:T(8,128)(2,1)S(1)} %fusion.11), channel_id=1, source_target_pairs={{0,8},{1,25},{8,16},{9,1},{16,24},{17,9},{24,0},{25,17},{2,10},{3,... | collective-permute-start | bytes 1081352 | tf_op jit(solution)/shard_map/ppermute | solution.py:364
  246.0 5.7 %collective-permute-start.4 = (bf16[4,8,1408]{2,1,0:T(8,128)(2,1)S(1)}, bf16[4,8,1408]{2,1,0:T(8,128)(2,1)S(1)}, u32[]{:S(2)}, u32[]{:S(2)}) collective-permute-start(bf16[4,8,1408]{2,1,0:T(8,128)(2,1)S(1)} %dynamic-slice_bitcast_fusion.9), channel_id=1, source_target_pairs={{0,32},{1,97},{32,64},{33,1},{64,96},{65,33},{96,0},{97,65},{2,34}... | collective-permute-start | bytes 270344 | tf_op jit(solution)/shard_map/ppermute | solution.py:364
  248.1 5.9 %collective-permute-start.14 = (bf16[4,8,1408]{2,1,0:T(8,128)(2,1)S(1)}, bf16[4,8,1408]{2,1,0:T(8,128)(2,1)S(1)}, u32[]{:S(2)}, u32[]{:S(2)}) collective-permute-start(bf16[4,8,1408]{2,1,0:T(8,128)(2,1)S(1)} %dynamic-slice_bitcast_fusion.8), channel_id=1, source_target_pairs={{0,8},{1,25},{8,16},{9,1},{16,24},{17,9},{24,0},{25,17},{2,10},{3,... | collective-permute-start | bytes 270344 | tf_op jit(solution)/shard_map/ppermute | solution.py:364
  248.3 17.3 %copy-start.2 = (bf16[512,2688]{1,0:T(8,128)(2,1)S(1)}, bf16[512,2688]{1,0:T(8,128)(2,1)}, u32[]{:S(2)}) copy-start(bf16[512,2688]{1,0:T(8,128)(2,1)} %get-tuple-element.62) | copy-start | bytes 8257540
  251.7 5.7 %collective-permute-start.24 = (bf16[4,8,1408]{2,1,0:T(8,128)(2,1)S(1)}, bf16[4,8,1408]{2,1,0:T(8,128)(2,1)S(1)}, u32[]{:S(2)}, u32[]{:S(2)}) collective-permute-start(bf16[4,8,1408]{2,1,0:T(8,128)(2,1)S(1)} %dynamic-slice_bitcast_fusion.7), channel_id=1, source_target_pairs={{0,2},{1,7},{2,4},{3,1},{4,6},{5,3},{6,0},{7,5},{8,10},{9,15},{10,... | collective-permute-start | bytes 270344 | tf_op jit(solution)/shard_map/ppermute | solution.py:364
  254.0 5.7 %collective-permute-start.5 = (bf16[4,8,1408]{2,1,0:T(8,128)(2,1)S(1)}, bf16[4,8,1408]{2,1,0:T(8,128)(2,1)S(1)}, u32[]{:S(2)}, u32[]{:S(2)}) collective-permute-start(bf16[4,8,1408]{2,1,0:T(8,128)(2,1)S(1)} %fusion.36), channel_id=1, source_target_pairs={{0,32},{1,97},{32,64},{33,1},{64,96},{65,33},{96,0},{97,65},{2,34}... | collective-permute-start | bytes 270344 | tf_op jit(solution)/shard_map/ppermute | solution.py:364
  257.4 5.7 %collective-permute-start.15 = (bf16[4,8,1408]{2,1,0:T(8,128)(2,1)S(1)}, bf16[4,8,1408]{2,1,0:T(8,128)(2,1)S(1)}, u32[]{:S(2)}, u32[]{:S(2)}) collective-permute-start(bf16[4,8,1408]{2,1,0:T(8,128)(2,1)S(1)} %fusion.33), channel_id=1, source_target_pairs={{0,8},{1,25},{8,16},{9,1},{16,24},{17,9},{24,0},{25,17},{2,10},{3,... | collective-permute-start | bytes 270344 | tf_op jit(solution)/shard_map/ppermute | solution.py:364
  259.8 5.7 %collective-permute-start.25 = (bf16[4,8,1408]{2,1,0:T(8,128)(2,1)S(1)}, bf16[4,8,1408]{2,1,0:T(8,128)(2,1)S(1)}, u32[]{:S(2)}, u32[]{:S(2)}) collective-permute-start(bf16[4,8,1408]{2,1,0:T(8,128)(2,1)S(1)} %fusion.30), channel_id=1, source_target_pairs={{0,2},{1,7},{2,4},{3,1},{4,6},{5,3},{6,0},{7,5},{8,10},{9,15},{10,... | collective-permute-start | bytes 270344 | tf_op jit(solution)/shard_map/ppermute | solution.py:364
  263.2 7.1 %collective-permute-start.6 = (bf16[4,8,1408]{2,1,0:T(8,128)(2,1)S(1)}, bf16[4,8,1408]{2,1,0:T(8,128)(2,1)S(1)}, u32[]{:S(2)}, u32[]{:S(2)}) collective-permute-start(bf16[4,8,1408]{2,1,0:T(8,128)(2,1)S(1)} %fusion.35), channel_id=1, source_target_pairs={{0,32},{1,97},{32,64},{33,1},{64,96},{65,33},{96,0},{97,65},{2,34}... | collective-permute-start | bytes 270344 | tf_op jit(solution)/shard_map/ppermute | solution.py:364
  265.5 5.7 %collective-permute-start.16 = (bf16[4,8,1408]{2,1,0:T(8,128)(2,1)S(1)}, bf16[4,8,1408]{2,1,0:T(8,128)(2,1)S(1)}, u32[]{:S(2)}, u32[]{:S(2)}) collective-permute-start(bf16[4,8,1408]{2,1,0:T(8,128)(2,1)S(1)} %fusion.32), channel_id=1, source_target_pairs={{0,8},{1,25},{8,16},{9,1},{16,24},{17,9},{24,0},{25,17},{2,10},{3,... | collective-permute-start | bytes 270344 | tf_op jit(solution)/shard_map/ppermute | solution.py:364
  265.6 7.4 %collective-permute-start.26 = (bf16[4,8,1408]{2,1,0:T(8,128)(2,1)S(1)}, bf16[4,8,1408]{2,1,0:T(8,128)(2,1)S(1)}, u32[]{:S(2)}, u32[]{:S(2)}) collective-permute-start(bf16[4,8,1408]{2,1,0:T(8,128)(2,1)S(1)} %fusion.29), channel_id=1, source_target_pairs={{0,2},{1,7},{2,4},{3,1},{4,6},{5,3},{6,0},{7,5},{8,10},{9,15},{10,... | collective-permute-start | bytes 270344 | tf_op jit(solution)/shard_map/ppermute | solution.py:364
  266.4 38.5 %collective-permute-start.31 = (bf16[4,4,8,2688]{3,2,1,0:T(8,128)(2,1)S(1)}, bf16[4,4,8,2688]{3,2,1,0:T(8,128)(2,1)S(1)}, u32[]{:S(2)}, u32[]{:S(2)}) collective-permute-start(bf16[4,4,8,2688]{3,2,1,0:T(8,128)(2,1)S(1)} %dynamic-slice_bitcast_fusion.1), channel_id=1, source_target_pairs={{0,2},{1,7},{2,4},{3,1},{4,6},{5,3},{6,0},{7,5},{8,10},{9,15},{10,... | collective-permute-start | bytes 2064392 | tf_op jit(solution)/shard_map/ppermute | solution.py:364
  268.2 37.1 %collective-permute-start.41 = (bf16[4,4,8,2688]{3,2,1,0:T(8,128)(2,1)S(1)}, bf16[4,4,8,2688]{3,2,1,0:T(8,128)(2,1)S(1)}, u32[]{:S(2)}, u32[]{:S(2)}) collective-permute-start(bf16[4,4,8,2688]{3,2,1,0:T(8,128)(2,1)S(1)} %dynamic-slice_bitcast_fusion), channel_id=1, source_target_pairs={{0,32},{1,97},{32,64},{33,1},{64,96},{65,33},{96,0},{97,65},{2,34}... | collective-permute-start | bytes 2064392 | tf_op jit(solution)/shard_map/ppermute | solution.py:364
  270.3 35.2 %collective-permute-start.51 = (bf16[4,4,8,2688]{3,2,0,1:T(8,128)(2,1)S(1)}, bf16[4,4,8,2688]{3,2,0,1:T(8,128)(2,1)S(1)}, u32[]{:S(2)}, u32[]{:S(2)}) collective-permute-start(bf16[4,4,8,2688]{3,2,0,1:T(8,128)(2,1)S(1)} %bitcast.256), channel_id=1, source_target_pairs={{0,8},{1,25},{8,16},{9,1},{16,24},{17,9},{24,0},{25,17},{2,10},{3,... | collective-permute-start | bytes 2064392 | tf_op jit(solution)/shard_map/ppermute | solution.py:364
  271.3 11.5 %collective-permute-start.7 = (bf16[8,1408]{1,0:T(8,128)(2,1)S(1)}, bf16[8,1408]{1,0:T(8,128)(2,1)S(1)}, u32[]{:S(2)}, u32[]{:S(2)}) collective-permute-start(bf16[8,1408]{1,0:T(8,128)(2,1)S(1)} %dynamic-slice_bitcast_fusion.15), channel_id=1, source_target_pairs={{0,8},{1,25},{8,16},{9,1},{16,24},{17,9},{24,0},{25,17},{2,10},{3,... | collective-permute-start | bytes 67592 | tf_op jit(solution)/shard_map/ppermute | solution.py:364
  273.0 9.8 %collective-permute-start.17 = (bf16[8,1408]{1,0:T(8,128)(2,1)S(1)}, bf16[8,1408]{1,0:T(8,128)(2,1)S(1)}, u32[]{:S(2)}, u32[]{:S(2)}) collective-permute-start(bf16[8,1408]{1,0:T(8,128)(2,1)S(1)} %dynamic-slice_bitcast_fusion.14), channel_id=1, source_target_pairs={{0,2},{1,7},{2,4},{3,1},{4,6},{5,3},{6,0},{7,5},{8,10},{9,15},{10,... | collective-permute-start | bytes 67592 | tf_op jit(solution)/shard_map/ppermute | solution.py:364
  282.8 5.0 %collective-permute-start.27 = (bf16[8,1408]{1,0:T(8,128)(2,1)S(1)}, bf16[8,1408]{1,0:T(8,128)(2,1)S(1)}, u32[]{:S(2)}, u32[]{:S(2)}) collective-permute-start(bf16[8,1408]{1,0:T(8,128)(2,1)S(1)} %dynamic-slice_bitcast_fusion.13), channel_id=1, source_target_pairs={{0,32},{1,97},{32,64},{33,1},{64,96},{65,33},{96,0},{97,65},{2,34}... | collective-permute-start | bytes 67592 | tf_op jit(solution)/shard_map/ppermute | solution.py:364
  282.8 5.7 %collective-permute-start.8 = (bf16[8,1408]{1,0:T(8,128)(2,1)S(1)}, bf16[8,1408]{1,0:T(8,128)(2,1)S(1)}, u32[]{:S(2)}, u32[]{:S(2)}) collective-permute-start(bf16[8,1408]{1,0:T(8,128)(2,1)S(1)} %fusion.49), channel_id=1, source_target_pairs={{0,8},{1,25},{8,16},{9,1},{16,24},{17,9},{24,0},{25,17},{2,10},{3,... | collective-permute-start | bytes 67592 | tf_op jit(solution)/shard_map/ppermute | solution.py:364
  287.8 5.0 %collective-permute-start.18 = (bf16[8,1408]{1,0:T(8,128)(2,1)S(1)}, bf16[8,1408]{1,0:T(8,128)(2,1)S(1)}, u32[]{:S(2)}, u32[]{:S(2)}) collective-permute-start(bf16[8,1408]{1,0:T(8,128)(2,1)S(1)} %fusion.47), channel_id=1, source_target_pairs={{0,2},{1,7},{2,4},{3,1},{4,6},{5,3},{6,0},{7,5},{8,10},{9,15},{10,... | collective-permute-start | bytes 67592 | tf_op jit(solution)/shard_map/ppermute | solution.py:364
  288.5 5.1 %collective-permute-start.28 = (bf16[8,1408]{1,0:T(8,128)(2,1)S(1)}, bf16[8,1408]{1,0:T(8,128)(2,1)S(1)}, u32[]{:S(2)}, u32[]{:S(2)}) collective-permute-start(bf16[8,1408]{1,0:T(8,128)(2,1)S(1)} %fusion.45), channel_id=1, source_target_pairs={{0,32},{1,97},{32,64},{33,1},{64,96},{65,33},{96,0},{97,65},{2,34}... | collective-permute-start | bytes 67592 | tf_op jit(solution)/shard_map/ppermute | solution.py:364
  292.8 5.0 %collective-permute-start.9 = (bf16[8,1408]{1,0:T(8,128)(2,1)S(1)}, bf16[8,1408]{1,0:T(8,128)(2,1)S(1)}, u32[]{:S(2)}, u32[]{:S(2)}) collective-permute-start(bf16[8,1408]{1,0:T(8,128)(2,1)S(1)} %fusion.48), channel_id=1, source_target_pairs={{0,8},{1,25},{8,16},{9,1},{16,24},{17,9},{24,0},{25,17},{2,10},{3,... | collective-permute-start | bytes 67592 | tf_op jit(solution)/shard_map/ppermute | solution.py:364
  293.6 5.0 %collective-permute-start.19 = (bf16[8,1408]{1,0:T(8,128)(2,1)S(1)}, bf16[8,1408]{1,0:T(8,128)(2,1)S(1)}, u32[]{:S(2)}, u32[]{:S(2)}) collective-permute-start(bf16[8,1408]{1,0:T(8,128)(2,1)S(1)} %fusion.46), channel_id=1, source_target_pairs={{0,2},{1,7},{2,4},{3,1},{4,6},{5,3},{6,0},{7,5},{8,10},{9,15},{10,... | collective-permute-start | bytes 67592 | tf_op jit(solution)/shard_map/ppermute | solution.py:364
  297.8 5.0 %collective-permute-start.29 = (bf16[8,1408]{1,0:T(8,128)(2,1)S(1)}, bf16[8,1408]{1,0:T(8,128)(2,1)S(1)}, u32[]{:S(2)}, u32[]{:S(2)}) collective-permute-start(bf16[8,1408]{1,0:T(8,128)(2,1)S(1)} %fusion.44), channel_id=1, source_target_pairs={{0,32},{1,97},{32,64},{33,1},{64,96},{65,33},{96,0},{97,65},{2,34}... | collective-permute-start | bytes 67592 | tf_op jit(solution)/shard_map/ppermute | solution.py:364
  305.1 12.2 %collective-permute-start.32 = (bf16[4,4,8,2688]{3,2,1,0:T(8,128)(2,1)S(1)}, bf16[4,4,8,2688]{3,2,1,0:T(8,128)(2,1)S(1)}, u32[]{:S(2)}, u32[]{:S(2)}) collective-permute-start(bf16[4,4,8,2688]{3,2,1,0:T(8,128)(2,1)S(1)} %fusion.9), channel_id=1, source_target_pairs={{0,2},{1,7},{2,4},{3,1},{4,6},{5,3},{6,0},{7,5},{8,10},{9,15},{10,... | collective-permute-start | bytes 2064392 | tf_op jit(solution)/shard_map/ppermute | solution.py:364
  305.5 12.2 %collective-permute-start.42 = (bf16[4,4,8,2688]{3,2,1,0:T(8,128)(2,1)S(1)}, bf16[4,4,8,2688]{3,2,1,0:T(8,128)(2,1)S(1)}, u32[]{:S(2)}, u32[]{:S(2)}) collective-permute-start(bf16[4,4,8,2688]{3,2,1,0:T(8,128)(2,1)S(1)} %fusion.6), channel_id=1, source_target_pairs={{0,32},{1,97},{32,64},{33,1},{64,96},{65,33},{96,0},{97,65},{2,34}... | collective-permute-start | bytes 2064392 | tf_op jit(solution)/shard_map/ppermute | solution.py:364
  305.7 12.5 %collective-permute-start.52 = (bf16[4,4,8,2688]{3,2,0,1:T(8,128)(2,1)S(1)}, bf16[4,4,8,2688]{3,2,0,1:T(8,128)(2,1)S(1)}, u32[]{:S(2)}, u32[]{:S(2)}) collective-permute-start(bf16[4,4,8,2688]{3,2,0,1:T(8,128)(2,1)S(1)} %fusion.3), channel_id=1, source_target_pairs={{0,8},{1,25},{8,16},{9,1},{16,24},{17,9},{24,0},{25,17},{2,10},{3,... | collective-permute-start | bytes 2064392 | tf_op jit(solution)/shard_map/ppermute | solution.py:364
  317.5 12.2 %collective-permute-start.33 = (bf16[4,4,8,2688]{3,2,1,0:T(8,128)(2,1)S(1)}, bf16[4,4,8,2688]{3,2,1,0:T(8,128)(2,1)S(1)}, u32[]{:S(2)}, u32[]{:S(2)}) collective-permute-start(bf16[4,4,8,2688]{3,2,1,0:T(8,128)(2,1)S(1)} %fusion.8), channel_id=1, source_target_pairs={{0,2},{1,7},{2,4},{3,1},{4,6},{5,3},{6,0},{7,5},{8,10},{9,15},{10,... | collective-permute-start | bytes 2064392 | tf_op jit(solution)/shard_map/ppermute | solution.py:364
  317.8 12.2 %collective-permute-start.43 = (bf16[4,4,8,2688]{3,2,1,0:T(8,128)(2,1)S(1)}, bf16[4,4,8,2688]{3,2,1,0:T(8,128)(2,1)S(1)}, u32[]{:S(2)}, u32[]{:S(2)}) collective-permute-start(bf16[4,4,8,2688]{3,2,1,0:T(8,128)(2,1)S(1)} %fusion.5), channel_id=1, source_target_pairs={{0,32},{1,97},{32,64},{33,1},{64,96},{65,33},{96,0},{97,65},{2,34}... | collective-permute-start | bytes 2064392 | tf_op jit(solution)/shard_map/ppermute | solution.py:364
  318.4 12.2 %collective-permute-start.53 = (bf16[4,4,8,2688]{3,2,0,1:T(8,128)(2,1)S(1)}, bf16[4,4,8,2688]{3,2,0,1:T(8,128)(2,1)S(1)}, u32[]{:S(2)}, u32[]{:S(2)}) collective-permute-start(bf16[4,4,8,2688]{3,2,0,1:T(8,128)(2,1)S(1)} %fusion.2), channel_id=1, source_target_pairs={{0,8},{1,25},{8,16},{9,1},{16,24},{17,9},{24,0},{25,17},{2,10},{3,... | collective-permute-start | bytes 2064392 | tf_op jit(solution)/shard_map/ppermute | solution.py:364
  329.9 6.7 %collective-permute-start.34 = (bf16[4,8,2688]{2,1,0:T(8,128)(2,1)S(1)}, bf16[4,8,2688]{2,1,0:T(8,128)(2,1)S(1)}, u32[]{:S(2)}, u32[]{:S(2)}) collective-permute-start(bf16[4,8,2688]{2,1,0:T(8,128)(2,1)S(1)} %dynamic-slice_bitcast_fusion.6), channel_id=1, source_target_pairs={{0,32},{1,97},{32,64},{33,1},{64,96},{65,33},{96,0},{97,65},{2,34}... | collective-permute-start | bytes 516104 | tf_op jit(solution)/shard_map/ppermute | solution.py:364
  330.2 6.7 %collective-permute-start.44 = (bf16[4,8,2688]{2,1,0:T(8,128)(2,1)S(1)}, bf16[4,8,2688]{2,1,0:T(8,128)(2,1)S(1)}, u32[]{:S(2)}, u32[]{:S(2)}) collective-permute-start(bf16[4,8,2688]{2,1,0:T(8,128)(2,1)S(1)} %dynamic-slice_bitcast_fusion.5), channel_id=1, source_target_pairs={{0,8},{1,25},{8,16},{9,1},{16,24},{17,9},{24,0},{25,17},{2,10},{3,... | collective-permute-start | bytes 516104 | tf_op jit(solution)/shard_map/ppermute | solution.py:364
  330.8 6.7 %collective-permute-start.54 = (bf16[4,8,2688]{2,1,0:T(8,128)(2,1)S(1)}, bf16[4,8,2688]{2,1,0:T(8,128)(2,1)S(1)}, u32[]{:S(2)}, u32[]{:S(2)}) collective-permute-start(bf16[4,8,2688]{2,1,0:T(8,128)(2,1)S(1)} %dynamic-slice_bitcast_fusion.4), channel_id=1, source_target_pairs={{0,2},{1,7},{2,4},{3,1},{4,6},{5,3},{6,0},{7,5},{8,10},{9,15},{10,... | collective-permute-start | bytes 516104 | tf_op jit(solution)/shard_map/ppermute | solution.py:364
  336.6 6.7 %collective-permute-start.35 = (bf16[4,8,2688]{2,1,0:T(8,128)(2,1)S(1)}, bf16[4,8,2688]{2,1,0:T(8,128)(2,1)S(1)}, u32[]{:S(2)}, u32[]{:S(2)}) collective-permute-start(bf16[4,8,2688]{2,1,0:T(8,128)(2,1)S(1)} %fusion.27), channel_id=1, source_target_pairs={{0,32},{1,97},{32,64},{33,1},{64,96},{65,33},{96,0},{97,65},{2,34}... | collective-permute-start | bytes 516104 | tf_op jit(solution)/shard_map/ppermute | solution.py:364
  337.0 6.7 %collective-permute-start.45 = (bf16[4,8,2688]{2,1,0:T(8,128)(2,1)S(1)}, bf16[4,8,2688]{2,1,0:T(8,128)(2,1)S(1)}, u32[]{:S(2)}, u32[]{:S(2)}) collective-permute-start(bf16[4,8,2688]{2,1,0:T(8,128)(2,1)S(1)} %fusion.24), channel_id=1, source_target_pairs={{0,8},{1,25},{8,16},{9,1},{16,24},{17,9},{24,0},{25,17},{2,10},{3,... | collective-permute-start | bytes 516104 | tf_op jit(solution)/shard_map/ppermute | solution.py:364
  337.5 6.7 %collective-permute-start.55 = (bf16[4,8,2688]{2,1,0:T(8,128)(2,1)S(1)}, bf16[4,8,2688]{2,1,0:T(8,128)(2,1)S(1)}, u32[]{:S(2)}, u32[]{:S(2)}) collective-permute-start(bf16[4,8,2688]{2,1,0:T(8,128)(2,1)S(1)} %fusion.21), channel_id=1, source_target_pairs={{0,2},{1,7},{2,4},{3,1},{4,6},{5,3},{6,0},{7,5},{8,10},{9,15},{10,... | collective-permute-start | bytes 516104 | tf_op jit(solution)/shard_map/ppermute | solution.py:364
  343.4 6.7 %collective-permute-start.36 = (bf16[4,8,2688]{2,1,0:T(8,128)(2,1)S(1)}, bf16[4,8,2688]{2,1,0:T(8,128)(2,1)S(1)}, u32[]{:S(2)}, u32[]{:S(2)}) collective-permute-start(bf16[4,8,2688]{2,1,0:T(8,128)(2,1)S(1)} %fusion.26), channel_id=1, source_target_pairs={{0,32},{1,97},{32,64},{33,1},{64,96},{65,33},{96,0},{97,65},{2,34}... | collective-permute-start | bytes 516104 | tf_op jit(solution)/shard_map/ppermute | solution.py:364
  343.7 6.7 %collective-permute-start.46 = (bf16[4,8,2688]{2,1,0:T(8,128)(2,1)S(1)}, bf16[4,8,2688]{2,1,0:T(8,128)(2,1)S(1)}, u32[]{:S(2)}, u32[]{:S(2)}) collective-permute-start(bf16[4,8,2688]{2,1,0:T(8,128)(2,1)S(1)} %fusion.23), channel_id=1, source_target_pairs={{0,8},{1,25},{8,16},{9,1},{16,24},{17,9},{24,0},{25,17},{2,10},{3,... | collective-permute-start | bytes 516104 | tf_op jit(solution)/shard_map/ppermute | solution.py:364
  344.2 8.6 %collective-permute-start.56 = (bf16[4,8,2688]{2,1,0:T(8,128)(2,1)S(1)}, bf16[4,8,2688]{2,1,0:T(8,128)(2,1)S(1)}, u32[]{:S(2)}, u32[]{:S(2)}) collective-permute-start(bf16[4,8,2688]{2,1,0:T(8,128)(2,1)S(1)} %fusion.20), channel_id=1, source_target_pairs={{0,2},{1,7},{2,4},{3,1},{4,6},{5,3},{6,0},{7,5},{8,10},{9,15},{10,... | collective-permute-start | bytes 516104 | tf_op jit(solution)/shard_map/ppermute | solution.py:364
  350.1 5.3 %collective-permute-start.37 = (bf16[8,2688]{1,0:T(8,128)(2,1)S(1)}, bf16[8,2688]{1,0:T(8,128)(2,1)S(1)}, u32[]{:S(2)}, u32[]{:S(2)}) collective-permute-start(bf16[8,2688]{1,0:T(8,128)(2,1)S(1)} %dynamic-slice_bitcast_fusion.12), channel_id=1, source_target_pairs={{0,8},{1,25},{8,16},{9,1},{16,24},{17,9},{24,0},{25,17},{2,10},{3,... | collective-permute-start | bytes 129032 | tf_op jit(solution)/shard_map/ppermute | solution.py:364
  350.5 5.3 %collective-permute-start.47 = (bf16[8,2688]{1,0:T(8,128)(2,1)S(1)}, bf16[8,2688]{1,0:T(8,128)(2,1)S(1)}, u32[]{:S(2)}, u32[]{:S(2)}) collective-permute-start(bf16[8,2688]{1,0:T(8,128)(2,1)S(1)} %dynamic-slice_bitcast_fusion.11), channel_id=1, source_target_pairs={{0,2},{1,7},{2,4},{3,1},{4,6},{5,3},{6,0},{7,5},{8,10},{9,15},{10,... | collective-permute-start | bytes 129032 | tf_op jit(solution)/shard_map/ppermute | solution.py:364
  352.9 5.3 %collective-permute-start.57 = (bf16[8,2688]{1,0:T(8,128)(2,1)S(1)}, bf16[8,2688]{1,0:T(8,128)(2,1)S(1)}, u32[]{:S(2)}, u32[]{:S(2)}) collective-permute-start(bf16[8,2688]{1,0:T(8,128)(2,1)S(1)} %dynamic-slice_bitcast_fusion.10), channel_id=1, source_target_pairs={{0,32},{1,97},{32,64},{33,1},{64,96},{65,33},{96,0},{97,65},{2,34}... | collective-permute-start | bytes 129032 | tf_op jit(solution)/shard_map/ppermute | solution.py:364
  355.4 5.3 %collective-permute-start.38 = (bf16[8,2688]{1,0:T(8,128)(2,1)S(1)}, bf16[8,2688]{1,0:T(8,128)(2,1)S(1)}, u32[]{:S(2)}, u32[]{:S(2)}) collective-permute-start(bf16[8,2688]{1,0:T(8,128)(2,1)S(1)} %fusion.43), channel_id=1, source_target_pairs={{0,8},{1,25},{8,16},{9,1},{16,24},{17,9},{24,0},{25,17},{2,10},{3,... | collective-permute-start | bytes 129032 | tf_op jit(solution)/shard_map/ppermute | solution.py:364
  355.8 5.3 %collective-permute-start.48 = (bf16[8,2688]{1,0:T(8,128)(2,1)S(1)}, bf16[8,2688]{1,0:T(8,128)(2,1)S(1)}, u32[]{:S(2)}, u32[]{:S(2)}) collective-permute-start(bf16[8,2688]{1,0:T(8,128)(2,1)S(1)} %fusion.41), channel_id=1, source_target_pairs={{0,2},{1,7},{2,4},{3,1},{4,6},{5,3},{6,0},{7,5},{8,10},{9,15},{10,... | collective-permute-start | bytes 129032 | tf_op jit(solution)/shard_map/ppermute | solution.py:364
  358.2 5.3 %collective-permute-start.58 = (bf16[8,2688]{1,0:T(8,128)(2,1)S(1)}, bf16[8,2688]{1,0:T(8,128)(2,1)S(1)}, u32[]{:S(2)}, u32[]{:S(2)}) collective-permute-start(bf16[8,2688]{1,0:T(8,128)(2,1)S(1)} %fusion.39), channel_id=1, source_target_pairs={{0,32},{1,97},{32,64},{33,1},{64,96},{65,33},{96,0},{97,65},{2,34}... | collective-permute-start | bytes 129032 | tf_op jit(solution)/shard_map/ppermute | solution.py:364
  360.8 5.3 %collective-permute-start.39 = (bf16[8,2688]{1,0:T(8,128)(2,1)S(1)}, bf16[8,2688]{1,0:T(8,128)(2,1)S(1)}, u32[]{:S(2)}, u32[]{:S(2)}) collective-permute-start(bf16[8,2688]{1,0:T(8,128)(2,1)S(1)} %fusion.42), channel_id=1, source_target_pairs={{0,8},{1,25},{8,16},{9,1},{16,24},{17,9},{24,0},{25,17},{2,10},{3,... | collective-permute-start | bytes 129032 | tf_op jit(solution)/shard_map/ppermute | solution.py:364
  361.1 5.3 %collective-permute-start.49 = (bf16[8,2688]{1,0:T(8,128)(2,1)S(1)}, bf16[8,2688]{1,0:T(8,128)(2,1)S(1)}, u32[]{:S(2)}, u32[]{:S(2)}) collective-permute-start(bf16[8,2688]{1,0:T(8,128)(2,1)S(1)} %fusion.40), channel_id=1, source_target_pairs={{0,2},{1,7},{2,4},{3,1},{4,6},{5,3},{6,0},{7,5},{8,10},{9,15},{10,... | collective-permute-start | bytes 129032 | tf_op jit(solution)/shard_map/ppermute | solution.py:364
  363.6 5.3 %collective-permute-start.59 = (bf16[8,2688]{1,0:T(8,128)(2,1)S(1)}, bf16[8,2688]{1,0:T(8,128)(2,1)S(1)}, u32[]{:S(2)}, u32[]{:S(2)}) collective-permute-start(bf16[8,2688]{1,0:T(8,128)(2,1)S(1)} %fusion.38), channel_id=1, source_target_pairs={{0,32},{1,97},{32,64},{33,1},{64,96},{65,33},{96,0},{97,65},{2,34}... | collective-permute-start | bytes 129032 | tf_op jit(solution)/shard_map/ppermute | solution.py:364
  (3 other events, 4.2 us)
Sparse Core Ops, SparseCore 0:
  15.8 95.5 all-gather.1

commit v2 on v1

v2 whole, which is shorter than its diff:
```python
import functools

import jax
import jax.numpy as jnp
from jax import lax
from jax.experimental import pallas as pl
from jax.experimental.pallas import tpu as pltpu
from jax.sharding import Mesh
from jax.sharding import PartitionSpec as P

H = 16
HD = 64
PAIR = 2 * HD
PAIRS = H // 2
epsilon = 1e-05
rope_base = 160000.0
masked_score = -1e30
AXES = ("y", "z", "x")
ALL = ("y", "z", "x", "c")
VMEM = 60 * 1024 * 1024
bf16 = jnp.bfloat16
f32 = jnp.float32

D = 1024
FF = 2624
CHUNKS = 3
CW = 896
MIX_AT = 3 * D
GAIN_AT = 4 * D
FF_AT = 4 * D + 128
W_COLS = FF_AT + CHUNKS * 3 * CW
ROWS = 512
HEAD_CUTS = ((0, 3), (3, 6), (6, 8))
MIX_CUTS = ((0, 384), (384, 768), (768, 1024))
A_COLS = (1536, 1536, 1152)


def dot(a, b):
    return lax.dot_general(a, b, (((1,), (0,)), ((), ())), preferred_element_type=f32)


def dot_t(a, b):
    return lax.dot_general(a, b, (((1,), (1,)), ((), ())), preferred_element_type=f32)


def dot_first(a, b):
    return lax.dot_general(a, b, (((0,), (0,)), ((), ())), preferred_element_type=f32)


def norm_parts(values):
    centered = values - jnp.mean(values, axis=-1, keepdims=True)
    scale = lax.rsqrt(jnp.mean(centered * centered, axis=-1, keepdims=True) + epsilon)
    return centered * scale, scale


def half_swapped(v, low_half):
    return jnp.where(low_half, pltpu.roll(v, PAIR - HD // 2, 1), pltpu.roll(v, HD // 2, 1))


def pair_slice(p, at=0):
    return pl.ds(pl.multiple_of(p * PAIR + at, PAIR), PAIR)


def cotangent_kernel(cot_ref, seg_ref, *refs):
    perms, gt_ref, gtts = refs[:CHUNKS], refs[CHUNKS], refs[CHUNKS + 1 :]
    gt = jnp.where(seg_ref[...] < 4, cot_ref[...].astype(f32), 0.0).astype(bf16)
    gt_ref[...] = gt
    for perm, gtt in zip(perms, gtts):
        gtt[...] = dot_t(perm[...], gt).astype(bf16)


def attend_kernel(
    tok_ref, seg_ref, segt_ref, cos_ref, sin_ref, w_ref,
    qkv_ref, prob_ref, res_ref, h1_ref, h2_ref, mixed, gain_ref,
    wp, wm, wg, packed, bias, sems,
):
    copies = [
        pltpu.make_async_copy(w_ref.at[:, pl.ds(GAIN_AT, 128)], wg, sems.at[0]),
        pltpu.make_async_copy(w_ref.at[:, pl.ds(0, 3 * D)], wp, sems.at[1]),
        pltpu.make_async_copy(w_ref.at[:, pl.ds(MIX_AT, D)], wm, sems.at[2]),
    ]
    for c in copies:
        c.start()
    tokens = tok_ref[...].astype(f32)
    xhat, _ = norm_parts(tokens)
    bias[...] = jnp.where(seg_ref[...] == segt_ref[...], 0.0, masked_score)
    copies[0].wait()
    gains = jnp.transpose(wg[...].astype(f32))[:8]
    gain_ref[...] = gains
    h1 = (xhat * gains[0:1]).astype(bf16)
    h1_ref[...] = h1
    copies[1].wait()
    packed[...] = dot(h1, wp[...])
    low_half = lax.broadcasted_iota(jnp.int32, (1, PAIR), 1) % HD < HD // 2
    first = lax.broadcasted_iota(jnp.int32, (1, PAIR), 1) < HD
    zero = jnp.zeros((), bf16)

    def pair(p, carry):
        cos, sin = cos_ref[...], sin_ref[...]
        q = packed[:, pair_slice(p)]
        k = packed[:, pair_slice(p, D)]
        q = (q * cos + half_swapped(q, low_half) * sin).astype(bf16)
        k = (k * cos + half_swapped(k, low_half) * sin).astype(bf16)
        v = packed[:, pair_slice(p, 2 * D)].astype(bf16)
        qkv_ref[:, pair_slice(p)] = q
        qkv_ref[:, pair_slice(p, D)] = k
        qkv_ref[:, pair_slice(p, 2 * D)] = v
        outs = []
        for side in range(2):
            mine = first if side == 0 else jnp.logical_not(first)
            scores = dot_t(jnp.where(mine, q, zero), k) * (HD**-0.5) + bias[...]
            top = jnp.max(scores, axis=-1, keepdims=True)
            e = jnp.exp(scores - top)
            probs = e * (1.0 / jnp.sum(e, axis=-1, keepdims=True))
            prob_ref[2 * p + side] = probs
            outs.append(dot(probs.astype(bf16), v))
        mixed[:, pair_slice(p)] = jnp.where(first, outs[0], outs[1]).astype(bf16)
        return carry

    lax.fori_loop(0, PAIRS, pair, 0)
    copies[2].wait()
    residual = tokens + dot(mixed[...], wm[...])
    res_ref[...] = residual
    xhat2, _ = norm_parts(residual)
    h2_ref[...] = (xhat2 * gains[1:2]).astype(bf16)


def gated_kernel(chunk, has_sum, *refs):
    h2_ref, gt_ref, w_ref = refs[:3]
    refs = refs[3:]
    if has_sum:
        branch_in, gh2_in = refs[:2]
        refs = refs[2:]
    branch_ref, gh2_ref, hid, gg, gu, w, gate, up, gh, sems = refs
    base = FF_AT + chunk * 3 * CW
    copies = [
        pltpu.make_async_copy(
            w_ref.at[:, pl.ds(base + i * CW, CW)], w.at[:, pl.ds(i * CW, CW)], sems.at[i]
        )
        for i in range(3)
    ]
    for c in copies:
        c.start()
    copies[0].wait()
    gate[...] = dot(h2_ref[...], w[:, :CW])
    copies[1].wait()
    up[...] = dot(h2_ref[...], w[:, CW : 2 * CW])
    copies[2].wait()
    gh[...] = dot(gt_ref[...], w[:, 2 * CW :])
    block = 16

    def rows(i, carry):
        r = pl.ds(pl.multiple_of(i * block, block), block)
        g, u, d = gate[r, :], up[r, :], gh[r, :]
        cdf = 0.5 * (1.0 + lax.erf(g * (0.5**0.5)))
        act = g * cdf
        slope = cdf + g * (jnp.exp(-0.5 * g * g) * 0.3989422804014327)
        hid[r, :] = (act * u).astype(bf16)
        gg[r, :] = (d * u * slope).astype(bf16)
        gu[r, :] = (d * act).astype(bf16)
        return carry

    lax.fori_loop(0, gate.shape[0] // block, rows, 0)
    branch = dot_t(hid[...], w[:, 2 * CW :])
    gh2 = dot_t(gg[...], w[:, :CW]) + dot_t(gu[...], w[:, CW : 2 * CW])
    if has_sum:
        branch = branch + branch_in[...]
        gh2 = gh2 + gh2_in[...]
    branch_ref[...] = branch
    gh2_ref[...] = gh2


def gated_grad_kernel(hid, gg, gu, h2_ref, perm_ref, gtt_ref, sib_ref, own_ref, h2t):
    h2t[...] = dot_t(perm_ref[...], h2_ref[...]).astype(bf16)
    for to, rows_at in ((sib_ref, 0), (own_ref, ROWS)):
        rows = pl.ds(rows_at, ROWS)
        to[:, pl.ds(0, CW)] = dot(h2t[rows, :], gg[...]).astype(bf16)
        to[:, pl.ds(CW, CW)] = dot(h2t[rows, :], gu[...]).astype(bf16)
        to[:, pl.ds(2 * CW, CW)] = dot(gtt_ref[rows, :], hid[...]).astype(bf16)


def residual_kernel(
    gt_ref, seg_ref, gain_ref, res_ref, branch_ref, gh2_ref, w_ref,
    out_ref, gr, ga_ref, gm, second_ref, wm, sems,
):
    copy = pltpu.make_async_copy(w_ref.at[:, pl.ds(MIX_AT, D)], wm, sems.at[0])
    copy.start()
    residual = res_ref[...]
    live = seg_ref[...] < 4
    out_ref[...] = jnp.where(live, residual + branch_ref[...], 0.0).astype(bf16)
    xhat2, r2 = norm_parts(residual)
    gh2 = gh2_ref[...]
    second_ref[...] = jnp.broadcast_to(jnp.sum(gh2 * xhat2, axis=0, keepdims=True), (8, D))
    n = gh2 * gain_ref[1:2]
    spread = jnp.mean(n * xhat2, axis=-1, keepdims=True)
    grad_res = gt_ref[...].astype(f32) + r2 * (
        n - jnp.mean(n, axis=-1, keepdims=True) - xhat2 * spread
    )
    gr[...] = grad_res
    ga = grad_res.astype(bf16)
    ga_ref[...] = ga
    copy.wait()
    gm[...] = dot_t(ga, wm[...]).astype(bf16)


def back_kernel(part, *refs):
    cos_ref, sin_ref, gm, ga, qkv_ref, prob_ref, h1_ref, mixed_ref, perm_ref = refs[:9]
    last = part == len(HEAD_CUTS) - 1
    if last:
        tok_ref, gr, gain_ref, second_ref, w_ref, gp0, gp1 = refs[9:16]
        gin_ref, sib, own, h1t, mt, gp, wp, sems = refs[16:]
        copy = pltpu.make_async_copy(w_ref.at[:, pl.ds(0, 3 * D)], wp, sems.at[0])
        copy.start()
    else:
        gp, sib, own, h1t, mt = refs[9:]
    lo, hi = HEAD_CUTS[part]
    width = (hi - lo) * PAIR
    low_half = lax.broadcasted_iota(jnp.int32, (1, PAIR), 1) % HD < HD // 2
    first = lax.broadcasted_iota(jnp.int32, (1, PAIR), 1) < HD
    zero = jnp.zeros((), bf16)

    def pair(i, carry):
        cos, sin = cos_ref[...], sin_ref[...]
        p = i + lo
        q = qkv_ref[:, pair_slice(p)]
        k = qkv_ref[:, pair_slice(p, D)]
        v = qkv_ref[:, pair_slice(p, 2 * D)]
        g = gm[:, pair_slice(p)]
        dq, dk, dv = [], [], []
        for side in range(2):
            mine = first if side == 0 else jnp.logical_not(first)
            probs = prob_ref[2 * p + side]
            grad_probs = dot_t(jnp.where(mine, g, zero), v)
            weighted = probs * grad_probs
            delta = jnp.sum(weighted, axis=-1, keepdims=True)
            gs = (weighted - probs * delta).astype(bf16)
            dq.append(dot(gs, k))
            dk.append(dot_first(gs, q))
            dv.append(dot_first(probs.astype(bf16), g))
        dq = jnp.where(first, dq[0], dq[1]) * (HD**-0.5)
        dk = jnp.where(first, dk[0], dk[1]) * (HD**-0.5)
        dv = jnp.where(first, dv[0], dv[1])
        gp[:, pair_slice(i)] = (dq * cos - half_swapped(dq, low_half) * sin).astype(bf16)
        gp[:, pair_slice(i, width)] = (dk * cos - half_swapped(dk, low_half) * sin).astype(bf16)
        gp[:, pair_slice(i, 2 * width)] = dv.astype(bf16)
        return carry

    lax.fori_loop(0, hi - lo, pair, 0)
    mix = MIX_CUTS[part]
    h1t[...] = dot_t(perm_ref[...], h1_ref[...]).astype(bf16)
    mt[...] = dot_t(perm_ref[...], mixed_ref[...]).astype(bf16)
    for half, to in ((0, sib), (ROWS, own)):
        to[:, pl.ds(0, 3 * width)] = dot(h1t[pl.ds(half, ROWS), :], gp[...]).astype(bf16)
        mixed = dot(mt[pl.ds(half, ROWS), :], ga[:, mix[0] : mix[1]])
        to[:, pl.ds(3 * width, mix[1] - mix[0])] = mixed.astype(bf16)
    if not last:
        return
    copy.wait()
    gh1 = None
    for (at, end), g in zip(HEAD_CUTS, (gp0, gp1, gp)):
        w = (end - at) * PAIR
        for i in range(3):
            term = dot_t(g[:, i * w : (i + 1) * w], wp[:, i * D + at * PAIR : i * D + end * PAIR])
            gh1 = term if gh1 is None else gh1 + term
    xhat1, r1 = norm_parts(tok_ref[...].astype(f32))
    one = jnp.sum(gh1 * xhat1, axis=0, keepdims=True)
    m = gh1 * gain_ref[0:1]
    spread = jnp.mean(m * xhat1, axis=-1, keepdims=True)
    gin_ref[...] = gr[...] + r1 * (m - jnp.mean(m, axis=-1, keepdims=True) - xhat1 * spread)
    row = lax.broadcasted_iota(jnp.int32, (128, D), 0)
    both = jnp.where(row == 0, one, jnp.where(row == 1, second_ref[0:1], 0.0)).astype(bf16)
    for half, to in ((0, sib), (ROWS, own)):
        to[:, pl.ds(3 * width + 256, 128)] = dot_t(perm_ref[pl.ds(half, ROWS), :], both).astype(bf16)


def first_kernel(own, sib, out):
    out[...] = (own[...].astype(f32) + sib[...].astype(f32)).astype(bf16)


def add_kernel(got, *refs):
    total = got[...].astype(f32)
    for r in refs[:-1]:
        total = total + r[...].astype(f32)
    refs[-1][...] = total.astype(refs[-1].dtype)


def turn_kernel(got, own, sib, before, out, send):
    wide = before.shape[1]
    out[:, pl.ds(0, wide)] = before[...]
    total = got[...].astype(f32) + own[...].astype(f32) + sib[...].astype(f32)
    out[:, pl.ds(wide, own.shape[1])] = total.astype(bf16)
    send[...] = out[pl.ds(0, send.shape[0]), :]


def turn_last_kernel(got, held, out, send):
    total = got[...].astype(f32) + held[...].astype(f32)
    out[...] = total
    send[...] = total[: send.shape[0]].astype(bf16)


def arr(shape, dtype):
    return jax.ShapeDtypeStruct(shape, dtype)


VSPEC = pl.BlockSpec(memory_space=pltpu.VMEM)
HSPEC = pl.BlockSpec(memory_space=pl.ANY)
DMA = pltpu.SemaphoreType.DMA


class Chain:
    def __init__(self):
        self.before = None

    def __call__(self, kernel, name, us, inputs, out_shape, scratch=(), in_hbm=(), specs=None):
        count = len(inputs)
        grid = (1,) if specs else ()
        specs = specs or [HSPEC if i in in_hbm else VSPEC for i in range(count)]
        run = kernel
        if self.before is not None:
            inputs, specs = (*inputs, self.before), [*specs, HSPEC]

            def run(*refs):
                kernel(*refs[:count], *refs[count + 1 :])

        out = pl.pallas_call(
            run,
            grid=grid,
            out_shape=out_shape,
            in_specs=specs,
            out_specs=(VSPEC,) * len(out_shape),
            scratch_shapes=list(scratch),
            compiler_params=pltpu.CompilerParams(vmem_limit_bytes=VMEM),
            cost_estimate=pl.CostEstimate(
                flops=int(us * 1e13), bytes_accessed=1024, transcendentals=0
            ),
            name=name,
        )(*inputs)
        self.before = out[-1]
        return out


def token_layout(lengths, slot_count):
    places = jnp.arange(slot_count, dtype=jnp.int32)
    ends = jnp.cumsum(lengths)
    starts = ends - lengths
    segment = jnp.sum((places[:, None] >= ends[None, :]).astype(jnp.int32), axis=1)
    live = places < ends[-1]
    picked = (segment[:, None] == jnp.arange(lengths.shape[0], dtype=jnp.int32)[None, :]).astype(
        jnp.int32
    )
    position = jnp.where(live, places - jnp.sum(picked * starts[None, :], axis=1), 0)
    segment = jnp.where(live, segment, lengths.shape[0] + places)
    return segment, position


def rotary_tables(position):
    frequency = rope_base ** (-(jnp.arange(HD // 2, dtype=f32) * 2.0 / HD))
    angles = position.astype(f32)[:, None] * frequency
    cos, sin = jnp.cos(angles), jnp.sin(angles)
    return (
        jnp.concatenate([cos, cos, cos, cos], axis=-1),
        jnp.concatenate([-sin, sin, -sin, sin], axis=-1),
    )


ORDERS = (("x", "y", "z"), ("y", "z", "x"), ("z", "x", "y"))


def row_order(order):
    core = lax.axis_index("c")
    row = jnp.arange(D, dtype=jnp.int32)
    mine, inner = row >= ROWS, row % ROWS
    side = jnp.where(mine, core, 1 - core)
    step = 1 - 2 * side
    place = {}
    for axis, size in zip(order, (128, 32, 8)):
        place[axis] = (lax.axis_index(axis) + 8 - (inner // size % 4 + 1) * step) % 4
    feature = ((place["y"] * 4 + place["z"]) * 4 + place["x"]) * 16 + side * 8 + inner % 8
    return (feature[:, None] == jnp.arange(D, dtype=jnp.int32)[None, :]).astype(bf16)


def onward(a, axis):
    pairs = [(i * 2 + c, (i + 1 - 2 * c) % 4 * 2 + c) for i in range(4) for c in range(2)]
    return lax.ppermute(a, (axis, "c"), pairs)


def to_sibling(a):
    return lax.ppermute(a, "c", [(0, 1), (1, 0)])


def block(rows, cols, at):
    return pl.BlockSpec((rows, cols), lambda i: (at, 0))


class PartSum:
    def __init__(self, chain, order, sib, own, merged_with=None):
        self.chain, self.order, self.own, self.with_ff = chain, order, own, merged_with
        self.arrived = to_sibling(sib)
        self.step = 0
        self.cols = own.shape[1]
        self.got = self.result = None

    def advance(self):
        t, cols, wide = self.step, self.cols, self.cols
        self.step += 1
        axis = self.order[0 if t < 3 else 1 if t < 6 else 2]
        ahead = [block(128, cols, t)] * 2
        if t == 0:
            (out,) = self.chain(
                first_kernel, "ring", 1, (self.own, self.arrived), (arr((128, cols), bf16),), specs=ahead
            )
        elif t < 3 or t == 3 and self.with_ff is None:
            (out,) = self.chain(
                add_kernel, "ring", 1, (self.got, self.own, self.arrived),
                (arr((128, cols), bf16),), specs=[VSPEC] + ahead,
            )
            if t == 3:
                self.result = out
                return
        elif t == 3:
            ff = self.with_ff.result
            self.cols = cols = cols + ff.shape[1]
            self.held, out = self.chain(
                turn_kernel, "turn", 1, (self.got, self.own, self.arrived, ff),
                (arr((128, cols), bf16), arr((32, cols), bf16)), specs=[VSPEC] + ahead + [VSPEC],
            )
        elif t == 6:
            self.held, out = self.chain(
                turn_last_kernel, "turn_last", 1, (self.got, self.held),
                (arr((32, cols), f32), arr((8, cols), bf16)), specs=[VSPEC, block(32, cols, 3)],
            )
        else:
            rows, at = (32, t - 3) if t < 6 else (8, t - 6)
            (out,) = self.chain(
                add_kernel, "ring", 1, (self.got, self.held),
                (arr((rows, cols), f32 if t == 9 else bf16),), specs=[VSPEC, block(rows, cols, at)],
            )
            if t == 9:
                self.result = out
                return
        self.got = onward(out, axis)


PLAN = (
    "g0 d0 g1 F0 d1 g2 F1 F0 d2 r b0 F2 F1 F0 A0 b1 F2 F1 F0 A1 A0 b2 F2 F1 A2 A1 A0 F2 "
    "A1 A0 A2 A1 A2 A0 A1 A2 A0 A1 A2 A0 A1 A2 A0 A1 A2 A0 A1 A2 A0 A1 A2 A2"
)


def local_step(tokens, cotangent, lengths, weights, perms, part_sum):
    n = tokens.shape[0]
    segment, position = token_layout(lengths, n)
    cos, sin = rotary_tables(position)
    seg_col, seg_row = segment[:, None], segment[None, :]
    tile = arr((n, D), bf16)
    wide = arr((n, D), f32)
    gt, *gtts = Chain()(
        cotangent_kernel, "cotangent", 4, (cotangent, seg_col, *perms),
        (tile,) + (arr((D, n), bf16),) * CHUNKS,
    )
    chain = Chain()
    qkv, probs, residual, h1, h2, mixed, gains = chain(
        attend_kernel, "attend", 21, (tokens, seg_col, seg_row, cos, sin, weights),
        (arr((n, 3 * D), bf16), arr((H, n, n), f32), wide, tile, tile, tile, arr((8, D), f32)),
        [
            pltpu.VMEM((D, 3 * D), bf16), pltpu.VMEM((D, D), bf16), pltpu.VMEM((D, 128), bf16),
            pltpu.VMEM((n, 3 * D), f32), pltpu.VMEM((n, n), f32), DMA((3,)),
        ],
        in_hbm=(5,),
    )
    sums, hidden, gps, ff, att = (), {}, [], {}, {}
    for what, index in (name[:1] + (name[1:] or "0") for name in PLAN.split()):
        i = int(index)
        if what == "g":
            *sums, hid, gg, gu = chain(
                functools.partial(gated_kernel, i, i > 0), "gated", 8, (h2, gt, weights, *sums),
                (wide, wide) + (arr((n, CW), bf16),) * 3,
                [pltpu.VMEM((D, 3 * CW), bf16)] + [pltpu.VMEM((n, CW), f32)] * 3 + [DMA((3,))],
                in_hbm=(2,),
            )
            hidden[i] = (hid, gg, gu)
        elif what == "d":
            sib, own = chain(
                gated_grad_kernel, "gated_grad", 5, (*hidden[i], h2, perms[i], gtts[i]),
                (arr((ROWS, 3 * CW), bf16),) * 2, [pltpu.VMEM((D, n), bf16)],
            )
            ff[i] = part_sum(chain, ORDERS[i], sib, own)
        elif what == "r":
            branch, gh2 = sums
            block_output, gr, ga, gm, second = chain(
                residual_kernel, "residual", 4, (gt, seg_col, gains, residual, branch, gh2, weights),
                (tile, wide, tile, tile, arr((8, D), f32)), [pltpu.VMEM((D, D), bf16), DMA((1,))],
                in_hbm=(6,),
            )
        elif what == "b":
            width = 3 * (HEAD_CUTS[i][1] - HEAD_CUTS[i][0]) * PAIR
            common = (cos, sin, gm, ga, qkv, probs, h1, mixed, perms[i])
            pieces = (arr((ROWS, A_COLS[i]), bf16),) * 2
            kernel = functools.partial(back_kernel, i)
            turned = [pltpu.VMEM((D, n), bf16)] * 2
            if i < 2:
                gp, sib, own = chain(
                    kernel, "back", 8, common, (arr((n, width), bf16),) + pieces, turned
                )
                gps.append(gp)
            else:
                input_grad, sib, own = chain(
                    kernel, "back_last", 12, common + (tokens, gr, gains, second, weights, *gps),
                    (wide,) + pieces,
                    turned + [pltpu.VMEM((n, width), bf16), pltpu.VMEM((D, 3 * D), bf16), DMA((1,))],
                    in_hbm=(13,),
                )
            att[i] = part_sum(chain, ORDERS[i], sib, own, ff[i])
        else:
            (ff if what == "F" else att)[i].advance()
    return block_output, input_grad, ff, att


def own_rows(parts):
    ff = [p[:, : 3 * CW] for p in parts]
    att = [p[:, 3 * CW :] for p in parts]
    gate_g, up_g, red_g = (
        jnp.concatenate([f[:, i * CW : (i + 1) * CW] for f in ff], axis=1)[:, :FF]
        for i in range(3)
    )
    packed, mixer = [[], [], []], []
    for a, (lo, hi), (at, end) in zip(att, HEAD_CUTS, MIX_CUTS):
        width = (hi - lo) * PAIR
        for i in range(3):
            packed[i].append(a[:, i * width : (i + 1) * width])
        mixer.append(a[:, 3 * width : 3 * width + end - at])
    return (
        jnp.concatenate(packed[0] + packed[1] + packed[2], axis=1),
        jnp.concatenate(mixer, axis=1),
        jnp.concatenate([gate_g, up_g], axis=1),
        red_g,
        att[2][:, A_COLS[2] - 128],
        att[2][:, A_COLS[2] - 127],
    )


def body(
    tokens, packed_proj, mixer_proj, expand_proj, reduce_proj, first_gain, second_gain,
    sequence_lengths, cotangent,
):
    pad = CHUNKS * CW - FF
    gate, up, red = (
        jnp.pad(w, ((0, 0), (0, pad)))
        for w in (expand_proj[:, :FF], expand_proj[:, FF:], reduce_proj)
    )
    gains = jnp.pad(jnp.stack([first_gain, second_gain], axis=1), ((0, 0), (0, 126)))
    pieces = [packed_proj, mixer_proj, gains]
    for j in range(CHUNKS):
        pieces += [w[:, j * CW : (j + 1) * CW] for w in (gate, up, red)]
    shard = jnp.concatenate(pieces, axis=1)
    weights = lax.all_gather(shard, ALL, axis=0, tiled=True)
    perms = [row_order(order) for order in ORDERS]
    block_output, input_grad, _, att = local_step(
        tokens, cotangent, sequence_lengths, weights, perms, PartSum
    )
    return (block_output, input_grad, *own_rows([att[i].result for i in range(CHUNKS)]))


def solution(mesh):
    torus = Mesh(mesh.devices.reshape(4, 4, 4, 2), ALL)
    row, flat = P(ALL, None), P(ALL)
    return jax.shard_map(
        body,
        mesh=torus,
        in_specs=(row,) * 5 + (flat, flat, flat, row),
        out_specs=(row,) * 6 + (flat, flat),
        check_vma=False,
    )
```

time: 383 us -> 400 us (1.044)
  Pallas kernels: 80.5 us -> 199 us
  waiting for transfers between devices: 219 us -> 107 us
  local copies, waits for them, and re-layouts: 10.9 us -> 25.2 us
  other arithmetic: 20 us -> 14.4 us
    pallas_call x5 -> x54, Pallas kernels: 80.5 us -> 199 us  [__call__(): pl.pallas_call(run, grid=grid, out_shape=out_shape, in_specs=specs, out_s...]
    ppermute x60 -> x42, waiting for transfers between devices: 132 us -> 29.1 us  [the longest x36 29.1 us: onward(): return lax.ppermute(a, (axis, 'c'), pairs)]
    all_gather x1, waiting for transfers between devices: 86.8 us -> 78 us  [body(): weights = lax.all_gather(shard, ALL, axis=0, tiled=True)]
    slice x10 -> x7, local copies, waits for them, and re-layouts: 0.74 us -> 9.06 us  [the longest x3 3.96 us: own_rows(): mixer.append(a[:, 3 * width:3 * width + end - at])]
    convert_element_type x54 -> x0, other arithmetic: 7.6 us -> none  [the longest x6 4.47 us: summed_part(): (own.astype(f32) + arrived.astype(f32)).astype(bf16).reshape(*sizes, 8, -1)]
    unnamed x23 -> x43, local copies, waits for them, and re-layouts: 6.73 us -> 13.8 us
    ppermute x60 -> x42, starting transfers between devices: 32.3 us -> 32.4 us  [the longest x36 26.6 us: onward(): return lax.ppermute(a, (axis, 'c'), pairs)]
  transfers between devices with their start and end apart: 61 -> 43, of which waited for: 48 -> 16; matrix products, arithmetic and copies ran while one was open for 5% -> 4% of each run, Pallas kernels for 0% -> 41%
where the time goes in v2:
time: 400 us; the launch traced here: 393 us
  Pallas kernels  199 us (50%)
  waiting for transfers between devices  107 us (27%)
  starting transfers between devices  32.5 us (8%)
  local copies, waits for them, and re-layouts  25.2 us (6%)
  between operations  14.7 us (4%)
  other arithmetic  14.4 us (4%)
    pallas_call x54, Pallas kernels, __call__(): pl.pallas_call(run, grid=grid, out_shape=out_shape, in_specs=specs, out_s...  199 us
    all_gather x1, waiting for transfers between devices, body(): weights = lax.all_gather(shard, ALL, axis=0, tiled=True)  78 us
    ppermute x36, waiting for transfers between devices, onward(): return lax.ppermute(a, (axis, 'c'), pairs)  29.1 us
    ppermute x36, starting transfers between devices, onward(): return lax.ppermute(a, (axis, 'c'), pairs)  26.6 us
    unnamed x43, local copies, waits for them, and re-layouts  13.8 us
  transfers between devices with their start and end apart: 43, of which 16 were waited for; matrix products, arithmetic and copies ran while one was open for 4% of the time, Pallas kernels for 41%

profile of v2, /device:TPU:0, one launch (start us, length us, event | category | flops | bytes accessed | tf_op | source)
XLA Modules:
  0.0 393.0 jit_solution(18257573203369739402)
XLA Ops:
  17.4 1.7 fusion.refs_0_.refs_4_.refs_8_
  19.2 1.7 fusion.1.refs_1_.refs_4_.refs_8_
  20.9 1.7 fusion.2.refs_2_.refs_4_.refs_8_
  23.9 6.0 %cotangent.1 = (bf16[256,1024]{1,0:T(8,128)(2,1)}, bf16[1024,256]{1,0:T(8,128)(2,1)}, bf16[1024,256]{1,0:T(8,128)(2,1)}, bf16[1024,256]{1,0:T(8,128)(2,1)}) custom-call(bf16[256,1024]{1,0:T(8,128)(2,1)} %cot_ref.1, s32[256,1]{1,0:T(8,128)} %add_select_fusion.seg_ref.refs_1_, bf16[1024,1024]{1,0:T(8,128)(2,1)} %fusion.refs_0_.refs_4_.refs_8_, ...), custom_call_target="tpu_custom_call" | custom-call | flops 39999999311872 | bytes 1024 | tf_op jit(solution)/shard_map/cotangent/pallas_call | solution.py:325
  33.4 78.0 %all-gather.2.cloned.1.call-done.w_ref.refs_2_.refs_6_.refs_13_ = bf16[1024,12288]{1,0:T(8,128)(2,1)} async-done(((bf16[8,12288]{1,0:T(8,128)(2,1)}), bf16[1024,12288]{1,0:T(8,128)(2,1)}) %all-gather.2.cloned.1.call-update) | async-done | bytes 25165840 | tf_op jit(solution)/shard_map/all_gather | solution.py:556
  111.4 17.7 %attend.1 = (bf16[256,3072]{1,0:T(8,128)(2,1)}, f32[16,256,256]{2,1,0:T(8,128)}, f32[256,1024]{1,0:T(8,128)}, bf16[256,1024]{1,0:T(8,128)(2,1)}, bf16[256,1024]{...) custom-call(bf16[256,1024]{1,0:T(8,128)(2,1)} %refs_9_.1, s32[256,1]{1,0:T(8,128)} %add_select_fusion.seg_ref.refs_1_, ...), custom_call_target="tpu_custom_call" | custom-call | flops 209999993241600 | bytes 1024 | tf_op jit(solution)/shard_map/attend/pallas_call | solution.py:325
  129.2 8.5 %gated.3 = (f32[256,1024]{1,0:T(8,128)}, f32[256,1024]{1,0:T(8,128)}, bf16[256,896]{1,0:T(8,128)(2,1)}, bf16[256,896]{1,0:T(8,128)(2,1)}, bf16[256,896]{1,0:T(8,128)(2,1)}) custom-call(bf16[256,1024]{1,0:T(8,128)(2,1)} %get-tuple-element.69.refs_0_.refs_3_, bf16[256,1024]{1,0:T(8,128)(2,1)} %get-tuple-element.66.refs_1_.refs_0_, ...), custom_call_target="tpu_custom_call" | custom-call | flops 79999998623744 | bytes 1024 | tf_op jit(solution)/shard_map/gated/pallas_call | solution.py:325
  137.7 7.1 %gated_grad.3 = (bf16[512,2688]{1,0:T(8,128)(2,1)}, bf16[512,2688]{1,0:T(8,128)(2,1)}) custom-call(bf16[256,896]{1,0:T(8,128)(2,1)} %get-tuple-element.72.refs_0_, bf16[256,896]{1,0:T(8,128)(2,1)} %get-tuple-element.73.refs_1_, bf16[256,896]{1,0:T(8,128)(2,1)} %get-tuple-element.74.refs_2_.refs_6_, bf16[256,1024]{1,0:T(8,128)(2,1)} %get-tuple-element.69.refs_0_.refs_3_, ...), custom_call_target="tpu_custom_call" | custom-call | flops 50000000188416 | bytes 1024 | tf_op jit(solution)/shard_map/gated_grad/pallas_call | solution.py:325
  145.1 9.0 %gated.4 = (f32[256,1024]{1,0:T(8,128)}, f32[256,1024]{1,0:T(8,128)}, bf16[256,896]{1,0:T(8,128)(2,1)}, bf16[256,896]{1,0:T(8,128)(2,1)}, bf16[256,896]{1,0:T(8,128)(2,1)}) custom-call(bf16[256,1024]{1,0:T(8,128)(2,1)} %get-tuple-element.69.refs_0_.refs_3_, bf16[256,1024]{1,0:T(8,128)(2,1)} %get-tuple-element.66.refs_1_.refs_0_, ...), custom_call_target="tpu_custom_call" | custom-call | flops 79999998623744 | bytes 1024 | tf_op jit(solution)/shard_map/gated/pallas_call | solution.py:325
  154.1 2.4 ring.36.refs_6_
  156.4 1.9 collective-permute-start.1
  158.3 7.2 %gated_grad.4 = (bf16[512,2688]{1,0:T(8,128)(2,1)}, bf16[512,2688]{1,0:T(8,128)(2,1)}) custom-call(bf16[256,896]{1,0:T(8,128)(2,1)} %get-tuple-element.79.refs_0_, bf16[256,896]{1,0:T(8,128)(2,1)} %get-tuple-element.80.refs_1_, bf16[256,896]{1,0:T(8,128)(2,1)} %get-tuple-element.81.refs_2_, bf16[256,1024]{1,0:T(8,128)(2,1)} %get-tuple-element.69.refs_0_.refs_3_, ...), custom_call_target="tpu_custom_call" | custom-call | flops 50000000188416 | bytes 1024 | tf_op jit(solution)/shard_map/gated_grad/pallas_call | solution.py:325
  166.6 9.0 %gated.5 = (f32[256,1024]{1,0:T(8,128)}, f32[256,1024]{1,0:T(8,128)}, bf16[256,896]{1,0:T(8,128)(2,1)}, bf16[256,896]{1,0:T(8,128)(2,1)}, bf16[256,896]{1,0:T(8,128)(2,1)}) custom-call(bf16[256,1024]{1,0:T(8,128)(2,1)} %get-tuple-element.69.refs_0_.refs_3_, bf16[256,1024]{1,0:T(8,128)(2,1)} %get-tuple-element.66.refs_1_.refs_0_, ...), custom_call_target="tpu_custom_call" | custom-call | flops 79999998623744 | bytes 1024 | tf_op jit(solution)/shard_map/gated/pallas_call | solution.py:325
  175.6 2.3 ring.37.refs_3_
  179.4 2.6 ring.38.refs_6_
  182.3 7.2 %gated_grad.5 = (bf16[512,2688]{1,0:T(8,128)(2,1)}, bf16[512,2688]{1,0:T(8,128)(2,1)}) custom-call(bf16[256,896]{1,0:T(8,128)(2,1)} %get-tuple-element.87.refs_0_, bf16[256,896]{1,0:T(8,128)(2,1)} %get-tuple-element.88.refs_1_, bf16[256,896]{1,0:T(8,128)(2,1)} %get-tuple-element.89.refs_2_, bf16[256,1024]{1,0:T(8,128)(2,1)} %get-tuple-element.69.refs_0_.refs_3_, ...), custom_call_target="tpu_custom_call" | custom-call | flops 50000000188416 | bytes 1024 | tf_op jit(solution)/shard_map/gated_grad/pallas_call | solution.py:325
  189.5 1.7 collective-permute-start.6
  191.2 5.3 %residual.1 = (bf16[256,1024]{1,0:T(8,128)(2,1)}, f32[256,1024]{1,0:T(8,128)}, bf16[256,1024]{1,0:T(8,128)(2,1)}, bf16[256,1024]{1,0:T(8,128)(2,1)}, f32[8,1024]{1,0:T(8,128)}) custom-call(bf16[256,1024]{1,0:T(8,128)(2,1)} %get-tuple-element.66.refs_1_.refs_0_, s32[256,1]{1,0:T(8,128)} %add_select_fusion.seg_ref.refs_1_, ...), custom_call_target="tpu_custom_call" | custom-call | flops 39999999311872 | bytes 1024 | tf_op jit(solution)/shard_map/residual/pallas_call | solution.py:325
  196.4 10.5 %back.2 = (bf16[256,1152]{1,0:T(8,128)(2,1)}, bf16[512,1536]{1,0:T(8,128)(2,1)}, bf16[512,1536]{1,0:T(8,128)(2,1)}) custom-call(f32[256,128]{1,0:T(8,128)} %get-tuple-element.146.cos_ref.refs_0_, f32[256,128]{1,0:T(8,128)} %get-tuple-element.147.sin_ref.refs_1_, bf16[256,1024]{1,0:T(8,128)(2,1)} %get-tuple-element.94.refs_2_, ...), custom_call_target="tpu_custom_call" | custom-call | flops 79999998623744 | bytes 1024 | tf_op jit(solution)/shard_map/back/pallas_call | solution.py:325
  207.0 2.3 ring.39.refs_3_
  210.2 2.6 ring.40.refs_3_
  212.9 2.6 ring.41.refs_2_
  215.5 2.0 ring.42.refs_9_
  217.4 10.4 %back.3 = (bf16[256,1152]{1,0:T(8,128)(2,1)}, bf16[512,1536]{1,0:T(8,128)(2,1)}, bf16[512,1536]{1,0:T(8,128)(2,1)}) custom-call(f32[256,128]{1,0:T(8,128)} %get-tuple-element.146.cos_ref.refs_0_, f32[256,128]{1,0:T(8,128)} %get-tuple-element.147.sin_ref.refs_1_, bf16[256,1024]{1,0:T(8,128)(2,1)} %get-tuple-element.94.refs_2_, ...), custom_call_target="tpu_custom_call" | custom-call | flops 79999998623744 | bytes 1024 | tf_op jit(solution)/shard_map/back/pallas_call | solution.py:325
  230.1 1.8 collective-permute-start.8
  231.9 2.6 ring.43.refs_3_
  234.5 6.6 %collective-permute-done.10.refs_0_ = bf16[128,2688]{1,0:T(8,128)(2,1)} collective-permute-done((bf16[128,2688]{1,0:T(8,128)(2,1)}, bf16[128,2688]{1,0:T(8,128)(2,1)}, u32[]{:S(2)}, u32[]{:S(2)}) %collective-permute-start.10) | collective-permute-done | bytes 688160 | tf_op jit(solution)/shard_map/ppermute | solution.py:384
  241.1 2.6 ring.44.refs_3_
  244.6 2.6 ring.45.refs_2_.refs_3_
  247.2 2.0 ring.46.refs_3_
  250.0 2.1 ring.47.refs_16_
  252.1 1.7 collective-permute-start.12
  253.8 13.1 %back_last.1 = (f32[256,1024]{1,0:T(8,128)}, bf16[512,1152]{1,0:T(8,128)(2,1)}, bf16[512,1152]{1,0:T(8,128)(2,1)}) custom-call(f32[256,128]{1,0:T(8,128)} %get-tuple-element.146.cos_ref.refs_0_, f32[256,128]{1,0:T(8,128)} %get-tuple-element.147.sin_ref.refs_1_, bf16[256,1024]{1,0:T(8,128)(2,1)} %get-tuple-element.94.refs_2_, ...), custom_call_target="tpu_custom_call" | custom-call | flops 120000002129920 | bytes 1024 | tf_op jit(solution)/shard_map/back_last/pallas_call | solution.py:325
  267.8 2.6 ring.48.refs_3_
  270.9 2.6 ring.49.refs_2_.refs_3_
  273.6 1.8 ring.50.refs_3_
  276.3 2.1 ring.51.refs_3_
  278.5 1.8 collective-permute-start.18
  280.2 2.1 ring.52.refs_3_
  283.0 2.6 ring.53.refs_3_
  285.7 2.1 collective-permute-done.18.refs_0_
  287.8 2.1 ring.54.refs_4_
  291.6 2.8 turn.3
  295.9 2.0 ring.55.refs_4_
  297.9 2.5 collective-permute-start.22
  300.4 2.9 turn.4
  306.1 2.0 ring.56.refs_2_
  309.4 1.8 ring.57.refs_2_
  311.7 1.8 ring.58.refs_4_
  313.5 2.9 collective-permute-done.25.refs_0_
  316.4 2.7 turn.5
  319.0 1.7 collective-permute-start.28
  320.7 1.8 ring.59.refs_2_
  322.5 1.8 ring.60.refs_2_
  324.3 2.4 collective-permute-done.28.refs_0_
  326.7 1.8 ring.61.refs_2_
  330.5 1.9 turn_last.3
  332.4 1.9 turn_last.4
  334.3 2.0 collective-permute-done.31.refs_0_
  336.3 1.8 ring.62.refs_2_
  342.8 3.0 collective-permute-done.34.refs_0_
  345.8 1.9 turn_last.5
  351.2 2.2 collective-permute-done.37.refs_0_
  366.8 3.1 collective-permute-done.41.refs_0_
  (152 shorter events, 73.1 us)
Async XLA Ops:
  7.2 104.2 %all-gather.2.cloned.1.call-start = ((), (), s32[]{:S(2)}) async-start(), calls=%async_computation | async-start | bytes 25362432 | tf_op jit(solution)/shard_map/all_gather | solution.py:556
  15.0 0.7 copy-start
  16.6 0.7 copy-start.11
  17.3 3.6 copy-start.7
  23.9 6.0 %copy-start.10 = (s32[4]{0:T(128)S(1)}, s32[4]{0:T(128)}, u32[]{:S(2)}) copy-start(s32[4]{0:T(128)} %param.16) | copy-start | bytes 52
  23.9 6.0 %copy-start.12 = (s32[4,1]{0,1:T(1,128)S(1)}, s32[4,1]{0,1:T(1,128)}, u32[]{:S(2)}) copy-start(s32[4,1]{0,1:T(1,128)} %copy-done.11) | copy-start | bytes 52
  23.9 6.1 %copy-start.8 = (s32[256]{0:T(256)S(1)}, s32[256]{0:T(256)}, u32[]{:S(2)}) copy-start(s32[256]{0:T(256)} %copy-done.7) | copy-start | bytes 3076
  144.8 9.2 %collective-permute-start = (bf16[512,2688]{1,0:T(8,128)(2,1)}, bf16[512,2688]{1,0:T(8,128)(2,1)}, u32[]{:S(2)}, u32[]{:S(2)}) collective-permute-start(bf16[512,2688]{1,0:T(8,128)(2,1)} %get-tuple-element.83), channel_id=1, source_target_pairs={{0,1},{1,0},{2,3},{3,2},{4,5},{5,4},{6,7},{7,6},{8,9},{9,8},{10,11... | collective-permute-start | bytes 8257544 | tf_op jit(solution)/shard_map/ppermute | solution.py:388
  156.4 23.0 %collective-permute-start.1 = (bf16[128,2688]{1,0:T(8,128)(2,1)}, bf16[128,2688]{1,0:T(8,128)(2,1)}, u32[]{:S(2)}, u32[]{:S(2)}) collective-permute-start(bf16[128,2688]{1,0:T(8,128)(2,1)} %ring.36.refs_6_), channel_id=1, source_target_pairs={{0,2},{1,7},{2,4},{3,1},{4,6},{5,3},{6,0},{7,5},{8,10},{9,15},{10,... | collective-permute-start | bytes 2064392 | tf_op jit(solution)/shard_map/ppermute | solution.py:384
  165.4 10.2 %collective-permute-start.2 = (bf16[512,2688]{1,0:T(8,128)(2,1)}, bf16[512,2688]{1,0:T(8,128)(2,1)}, u32[]{:S(2)}, u32[]{:S(2)}) collective-permute-start(bf16[512,2688]{1,0:T(8,128)(2,1)} %get-tuple-element.91), channel_id=1, source_target_pairs={{0,1},{1,0},{2,3},{3,2},{4,5},{5,4},{6,7},{7,6},{8,9},{9,8},{10,11... | collective-permute-start | bytes 8257544 | tf_op jit(solution)/shard_map/ppermute | solution.py:388
  178.0 32.3 %collective-permute-start.5 = (bf16[128,2688]{1,0:T(8,128)(2,1)}, bf16[128,2688]{1,0:T(8,128)(2,1)}, u32[]{:S(2)}, u32[]{:S(2)}) collective-permute-start(bf16[128,2688]{1,0:T(8,128)(2,1)} %ring.37.refs_3_), channel_id=1, source_target_pairs={{0,32},{1,97},{32,64},{33,1},{64,96},{65,33},{96,0},{97,65},{2,34}... | collective-permute-start | bytes 2064392 | tf_op jit(solution)/shard_map/ppermute | solution.py:384
  182.1 30.8 %collective-permute-start.4 = (bf16[128,2688]{1,0:T(8,128)(2,1)}, bf16[128,2688]{1,0:T(8,128)(2,1)}, u32[]{:S(2)}, u32[]{:S(2)}) collective-permute-start(bf16[128,2688]{1,0:T(8,128)(2,1)} %ring.38.refs_6_), channel_id=1, source_target_pairs={{0,2},{1,7},{2,4},{3,1},{4,6},{5,3},{6,0},{7,5},{8,10},{9,15},{10,... | collective-permute-start | bytes 2064392 | tf_op jit(solution)/shard_map/ppermute | solution.py:384
  189.5 17.5 %collective-permute-start.6 = (bf16[512,2688]{1,0:T(8,128)(2,1)}, bf16[512,2688]{1,0:T(8,128)(2,1)}, u32[]{:S(2)}, u32[]{:S(2)}) collective-permute-start(bf16[512,2688]{1,0:T(8,128)(2,1)} %get-tuple-element.105), channel_id=1, source_target_pairs={{0,1},{1,0},{2,3},{3,2},{4,5},{5,4},{6,7},{7,6},{8,9},{9,8},{10,11... | collective-permute-start | bytes 8257544 | tf_op jit(solution)/shard_map/ppermute | solution.py:388
  207.0 8.5 %collective-permute-start.3 = (bf16[512,1536]{1,0:T(8,128)(2,1)}, bf16[512,1536]{1,0:T(8,128)(2,1)}, u32[]{:S(2)}, u32[]{:S(2)}) collective-permute-start(bf16[512,1536]{1,0:T(8,128)(2,1)} %get-tuple-element.104), channel_id=1, source_target_pairs={{0,1},{1,0},{2,3},{3,2},{4,5},{5,4},{6,7},{7,6},{8,9},{9,8},{10,11... | collective-permute-start | bytes 4718600 | tf_op jit(solution)/shard_map/ppermute | solution.py:388
  209.3 22.6 %collective-permute-start.11 = (bf16[128,2688]{1,0:T(8,128)(2,1)}, bf16[128,2688]{1,0:T(8,128)(2,1)}, u32[]{:S(2)}, u32[]{:S(2)}) collective-permute-start(bf16[128,2688]{1,0:T(8,128)(2,1)} %ring.39.refs_3_), channel_id=1, source_target_pairs={{0,8},{1,25},{8,16},{9,1},{16,24},{17,9},{24,0},{25,17},{2,10},{3,... | collective-permute-start | bytes 2064392 | tf_op jit(solution)/shard_map/ppermute | solution.py:384
  227.9 22.1 %collective-permute-start.7 = (bf16[128,1536]{1,0:T(8,128)(2,1)}, bf16[128,1536]{1,0:T(8,128)(2,1)}, u32[]{:S(2)}, u32[]{:S(2)}) collective-permute-start(bf16[128,1536]{1,0:T(8,128)(2,1)} %ring.42.refs_9_), channel_id=1, source_target_pairs={{0,2},{1,7},{2,4},{3,1},{4,6},{5,3},{6,0},{7,5},{8,10},{9,15},{10,... | collective-permute-start | bytes 1179656 | tf_op jit(solution)/shard_map/ppermute | solution.py:384
  227.9 16.7 %collective-permute-start.9 = (bf16[128,2688]{1,0:T(8,128)(2,1)}, bf16[128,2688]{1,0:T(8,128)(2,1)}, u32[]{:S(2)}, u32[]{:S(2)}) collective-permute-start(bf16[128,2688]{1,0:T(8,128)(2,1)} %ring.41.refs_2_), channel_id=1, source_target_pairs={{0,2},{1,7},{2,4},{3,1},{4,6},{5,3},{6,0},{7,5},{8,10},{9,15},{10,... | collective-permute-start | bytes 2064392 | tf_op jit(solution)/shard_map/ppermute | solution.py:384
  228.7 12.5 %collective-permute-start.10 = (bf16[128,2688]{1,0:T(8,128)(2,1)}, bf16[128,2688]{1,0:T(8,128)(2,1)}, u32[]{:S(2)}, u32[]{:S(2)}) collective-permute-start(bf16[128,2688]{1,0:T(8,128)(2,1)} %ring.40.refs_3_), channel_id=1, source_target_pairs={{0,32},{1,97},{32,64},{33,1},{64,96},{65,33},{96,0},{97,65},{2,34}... | collective-permute-start | bytes 2064392 | tf_op jit(solution)/shard_map/ppermute | solution.py:384
  230.1 17.1 %collective-permute-start.8 = (bf16[512,1536]{1,0:T(8,128)(2,1)}, bf16[512,1536]{1,0:T(8,128)(2,1)}, u32[]{:S(2)}, u32[]{:S(2)}) collective-permute-start(bf16[512,1536]{1,0:T(8,128)(2,1)} %get-tuple-element.108), channel_id=1, source_target_pairs={{0,1},{1,0},{2,3},{3,2},{4,5},{5,4},{6,7},{7,6},{8,9},{9,8},{10,11... | collective-permute-start | bytes 4718600 | tf_op jit(solution)/shard_map/ppermute | solution.py:388
  234.5 33.3 %collective-permute-start.16 = (bf16[128,2688]{1,0:T(8,128)(2,1)}, bf16[128,2688]{1,0:T(8,128)(2,1)}, u32[]{:S(2)}, u32[]{:S(2)}) collective-permute-start(bf16[128,2688]{1,0:T(8,128)(2,1)} %ring.43.refs_3_), channel_id=1, source_target_pairs={{0,8},{1,25},{8,16},{9,1},{16,24},{17,9},{24,0},{25,17},{2,10},{3,... | collective-permute-start | bytes 2064392 | tf_op jit(solution)/shard_map/ppermute | solution.py:384
  243.8 27.1 %collective-permute-start.15 = (bf16[128,2688]{1,0:T(8,128)(2,1)}, bf16[128,2688]{1,0:T(8,128)(2,1)}, u32[]{:S(2)}, u32[]{:S(2)}) collective-permute-start(bf16[128,2688]{1,0:T(8,128)(2,1)} %ring.44.refs_3_), channel_id=1, source_target_pairs={{0,32},{1,97},{32,64},{33,1},{64,96},{65,33},{96,0},{97,65},{2,34}... | collective-permute-start | bytes 2064392 | tf_op jit(solution)/shard_map/ppermute | solution.py:384
  249.1 27.2 %collective-permute-start.13 = (bf16[128,1536]{1,0:T(8,128)(2,1)}, bf16[128,1536]{1,0:T(8,128)(2,1)}, u32[]{:S(2)}, u32[]{:S(2)}) collective-permute-start(bf16[128,1536]{1,0:T(8,128)(2,1)} %ring.46.refs_3_), channel_id=1, source_target_pairs={{0,32},{1,97},{32,64},{33,1},{64,96},{65,33},{96,0},{97,65},{2,34}... | collective-permute-start | bytes 1179656 | tf_op jit(solution)/shard_map/ppermute | solution.py:384
  252.1 28.1 %collective-permute-start.12 = (bf16[128,1536]{1,0:T(8,128)(2,1)}, bf16[128,1536]{1,0:T(8,128)(2,1)}, u32[]{:S(2)}, u32[]{:S(2)}) collective-permute-start(bf16[128,1536]{1,0:T(8,128)(2,1)} %ring.47.refs_16_), channel_id=1, source_target_pairs={{0,2},{1,7},{2,4},{3,1},{4,6},{5,3},{6,0},{7,5},{8,10},{9,15},{10,... | collective-permute-start | bytes 1179656 | tf_op jit(solution)/shard_map/ppermute | solution.py:384
  266.9 6.6 %collective-permute-start.14 = (bf16[512,1152]{1,0:T(8,128)(2,1)}, bf16[512,1152]{1,0:T(8,128)(2,1)}, u32[]{:S(2)}, u32[]{:S(2)}) collective-permute-start(bf16[512,1152]{1,0:T(8,128)(2,1)} %get-tuple-element.111), channel_id=1, source_target_pairs={{0,1},{1,0},{2,3},{3,2},{4,5},{5,4},{6,7},{7,6},{8,9},{9,8},{10,11... | collective-permute-start | bytes 3538952 | tf_op jit(solution)/shard_map/ppermute | solution.py:388
  270.4 12.6 %collective-permute-start.19 = (bf16[128,2688]{1,0:T(8,128)(2,1)}, bf16[128,2688]{1,0:T(8,128)(2,1)}, u32[]{:S(2)}, u32[]{:S(2)}) collective-permute-start(bf16[128,2688]{1,0:T(8,128)(2,1)} %ring.48.refs_3_), channel_id=1, source_target_pairs={{0,8},{1,25},{8,16},{9,1},{16,24},{17,9},{24,0},{25,17},{2,10},{3,... | collective-permute-start | bytes 2064392 | tf_op jit(solution)/shard_map/ppermute | solution.py:384
  275.4 20.5 %collective-permute-start.21 = (bf16[128,1152]{1,0:T(8,128)(2,1)}, bf16[128,1152]{1,0:T(8,128)(2,1)}, u32[]{:S(2)}, u32[]{:S(2)}) collective-permute-start(bf16[128,1152]{1,0:T(8,128)(2,1)} %ring.50.refs_3_), channel_id=1, source_target_pairs={{0,8},{1,25},{8,16},{9,1},{16,24},{17,9},{24,0},{25,17},{2,10},{3,... | collective-permute-start | bytes 884744 | tf_op jit(solution)/shard_map/ppermute | solution.py:384
  278.5 9.3 %collective-permute-start.18 = (bf16[128,1536]{1,0:T(8,128)(2,1)}, bf16[128,1536]{1,0:T(8,128)(2,1)}, u32[]{:S(2)}, u32[]{:S(2)}) collective-permute-start(bf16[128,1536]{1,0:T(8,128)(2,1)} %ring.51.refs_3_), channel_id=1, source_target_pairs={{0,32},{1,97},{32,64},{33,1},{64,96},{65,33},{96,0},{97,65},{2,34}... | collective-permute-start | bytes 1179656 | tf_op jit(solution)/shard_map/ppermute | solution.py:384
  282.3 9.3 %collective-permute-start.17 = (bf16[128,1536]{1,0:T(8,128)(2,1)}, bf16[128,1536]{1,0:T(8,128)(2,1)}, u32[]{:S(2)}, u32[]{:S(2)}) collective-permute-start(bf16[128,1536]{1,0:T(8,128)(2,1)} %ring.52.refs_3_), channel_id=1, source_target_pairs={{0,2},{1,7},{2,4},{3,1},{4,6},{5,3},{6,0},{7,5},{8,10},{9,15},{10,... | collective-permute-start | bytes 1179656 | tf_op jit(solution)/shard_map/ppermute | solution.py:384
  289.9 10.5 %collective-permute-start.23 = (bf16[128,1536]{1,0:T(8,128)(2,1)}, bf16[128,1536]{1,0:T(8,128)(2,1)}, u32[]{:S(2)}, u32[]{:S(2)}) collective-permute-start(bf16[128,1536]{1,0:T(8,128)(2,1)} %ring.54.refs_4_), channel_id=1, source_target_pairs={{0,32},{1,97},{32,64},{33,1},{64,96},{65,33},{96,0},{97,65},{2,34}... | collective-permute-start | bytes 1179656 | tf_op jit(solution)/shard_map/ppermute | solution.py:384
  294.5 14.9 %collective-permute-start.20 = (bf16[32,4224]{1,0:T(8,128)(2,1)}, bf16[32,4224]{1,0:T(8,128)(2,1)}, u32[]{:S(2)}, u32[]{:S(2)}) collective-permute-start(bf16[32,4224]{1,0:T(8,128)(2,1)} %get-tuple-element.112.refs_3_), channel_id=1, source_target_pairs={{0,32},{1,97},{32,64},{33,1},{64,96},{65,33},{96,0},{97,65},{2,34}... | collective-permute-start | bytes 811016 | tf_op jit(solution)/shard_map/ppermute | solution.py:384
  297.9 8.2 %collective-permute-start.22 = (bf16[128,1152]{1,0:T(8,128)(2,1)}, bf16[128,1152]{1,0:T(8,128)(2,1)}, u32[]{:S(2)}, u32[]{:S(2)}) collective-permute-start(bf16[128,1152]{1,0:T(8,128)(2,1)} %ring.55.refs_4_), channel_id=1, source_target_pairs={{0,8},{1,25},{8,16},{9,1},{16,24},{17,9},{24,0},{25,17},{2,10},{3,... | collective-permute-start | bytes 884744 | tf_op jit(solution)/shard_map/ppermute | solution.py:384
  303.2 8.4 %collective-permute-start.26 = (bf16[32,4224]{1,0:T(8,128)(2,1)}, bf16[32,4224]{1,0:T(8,128)(2,1)}, u32[]{:S(2)}, u32[]{:S(2)}) collective-permute-start(bf16[32,4224]{1,0:T(8,128)(2,1)} %get-tuple-element.114.refs_3_), channel_id=1, source_target_pairs={{0,8},{1,25},{8,16},{9,1},{16,24},{17,9},{24,0},{25,17},{2,10},{3,... | collective-permute-start | bytes 811016 | tf_op jit(solution)/shard_map/ppermute | solution.py:384
  308.1 8.2 %collective-permute-start.25 = (bf16[128,1152]{1,0:T(8,128)(2,1)}, bf16[128,1152]{1,0:T(8,128)(2,1)}, u32[]{:S(2)}, u32[]{:S(2)}) collective-permute-start(bf16[128,1152]{1,0:T(8,128)(2,1)} %ring.56.refs_2_), channel_id=1, source_target_pairs={{0,8},{1,25},{8,16},{9,1},{16,24},{17,9},{24,0},{25,17},{2,10},{3,... | collective-permute-start | bytes 884744 | tf_op jit(solution)/shard_map/ppermute | solution.py:384
  311.2 9.5 %collective-permute-start.24 = (bf16[32,4224]{1,0:T(8,128)(2,1)}, bf16[32,4224]{1,0:T(8,128)(2,1)}, u32[]{:S(2)}, u32[]{:S(2)}) collective-permute-start(bf16[32,4224]{1,0:T(8,128)(2,1)} %ring.57.refs_2_), channel_id=1, source_target_pairs={{0,32},{1,97},{32,64},{33,1},{64,96},{65,33},{96,0},{97,65},{2,34}... | collective-permute-start | bytes 811016 | tf_op jit(solution)/shard_map/ppermute | solution.py:384
  313.5 9.0 %collective-permute-start.29 = (bf16[32,4224]{1,0:T(8,128)(2,1)}, bf16[32,4224]{1,0:T(8,128)(2,1)}, u32[]{:S(2)}, u32[]{:S(2)}) collective-permute-start(bf16[32,4224]{1,0:T(8,128)(2,1)} %ring.58.refs_4_), channel_id=1, source_target_pairs={{0,8},{1,25},{8,16},{9,1},{16,24},{17,9},{24,0},{25,17},{2,10},{3,... | collective-permute-start | bytes 811016 | tf_op jit(solution)/shard_map/ppermute | solution.py:384
  319.0 7.7 %collective-permute-start.28 = (bf16[32,3840]{1,0:T(8,128)(2,1)}, bf16[32,3840]{1,0:T(8,128)(2,1)}, u32[]{:S(2)}, u32[]{:S(2)}) collective-permute-start(bf16[32,3840]{1,0:T(8,128)(2,1)} %get-tuple-element.116.refs_2_), channel_id=1, source_target_pairs={{0,2},{1,7},{2,4},{3,1},{4,6},{5,3},{6,0},{7,5},{8,10},{9,15},{10,... | collective-permute-start | bytes 737288 | tf_op jit(solution)/shard_map/ppermute | solution.py:384
  322.5 8.0 %collective-permute-start.27 = (bf16[32,4224]{1,0:T(8,128)(2,1)}, bf16[32,4224]{1,0:T(8,128)(2,1)}, u32[]{:S(2)}, u32[]{:S(2)}) collective-permute-start(bf16[32,4224]{1,0:T(8,128)(2,1)} %ring.59.refs_2_), channel_id=1, source_target_pairs={{0,32},{1,97},{32,64},{33,1},{64,96},{65,33},{96,0},{97,65},{2,34}... | collective-permute-start | bytes 811016 | tf_op jit(solution)/shard_map/ppermute | solution.py:384
  324.3 8.1 %collective-permute-start.32 = (bf16[32,4224]{1,0:T(8,128)(2,1)}, bf16[32,4224]{1,0:T(8,128)(2,1)}, u32[]{:S(2)}, u32[]{:S(2)}) collective-permute-start(bf16[32,4224]{1,0:T(8,128)(2,1)} %ring.60.refs_2_), channel_id=1, source_target_pairs={{0,8},{1,25},{8,16},{9,1},{16,24},{17,9},{24,0},{25,17},{2,10},{3,... | collective-permute-start | bytes 811016 | tf_op jit(solution)/shard_map/ppermute | solution.py:384
  328.5 7.7 %collective-permute-start.31 = (bf16[32,3840]{1,0:T(8,128)(2,1)}, bf16[32,3840]{1,0:T(8,128)(2,1)}, u32[]{:S(2)}, u32[]{:S(2)}) collective-permute-start(bf16[32,3840]{1,0:T(8,128)(2,1)} %ring.61.refs_2_), channel_id=1, source_target_pairs={{0,2},{1,7},{2,4},{3,1},{4,6},{5,3},{6,0},{7,5},{8,10},{9,15},{10,... | collective-permute-start | bytes 737288 | tf_op jit(solution)/shard_map/ppermute | solution.py:384
  332.4 5.8 %collective-permute-start.30 = (bf16[8,4224]{1,0:T(8,128)(2,1)}, bf16[8,4224]{1,0:T(8,128)(2,1)}, u32[]{:S(2)}, u32[]{:S(2)}) collective-permute-start(bf16[8,4224]{1,0:T(8,128)(2,1)} %get-tuple-element.118.refs_2_), channel_id=1, source_target_pairs={{0,8},{1,25},{8,16},{9,1},{16,24},{17,9},{24,0},{25,17},{2,10},{3,... | collective-permute-start | bytes 202760 | tf_op jit(solution)/shard_map/ppermute | solution.py:384
  334.3 5.8 %collective-permute-start.35 = (bf16[8,4224]{1,0:T(8,128)(2,1)}, bf16[8,4224]{1,0:T(8,128)(2,1)}, u32[]{:S(2)}, u32[]{:S(2)}) collective-permute-start(bf16[8,4224]{1,0:T(8,128)(2,1)} %get-tuple-element.120.refs_2_), channel_id=1, source_target_pairs={{0,2},{1,7},{2,4},{3,1},{4,6},{5,3},{6,0},{7,5},{8,10},{9,15},{10,... | collective-permute-start | bytes 202760 | tf_op jit(solution)/shard_map/ppermute | solution.py:384
  338.1 7.7 %collective-permute-start.34 = (bf16[32,3840]{1,0:T(8,128)(2,1)}, bf16[32,3840]{1,0:T(8,128)(2,1)}, u32[]{:S(2)}, u32[]{:S(2)}) collective-permute-start(bf16[32,3840]{1,0:T(8,128)(2,1)} %ring.62.refs_2_), channel_id=1, source_target_pairs={{0,2},{1,7},{2,4},{3,1},{4,6},{5,3},{6,0},{7,5},{8,10},{9,15},{10,... | collective-permute-start | bytes 737288 | tf_op jit(solution)/shard_map/ppermute | solution.py:384
  339.8 8.2 %collective-permute-start.33 = (bf16[8,4224]{1,0:T(8,128)(2,1)}, bf16[8,4224]{1,0:T(8,128)(2,1)}, u32[]{:S(2)}, u32[]{:S(2)}) collective-permute-start(bf16[8,4224]{1,0:T(8,128)(2,1)} %ring.63.refs_2_), channel_id=1, source_target_pairs={{0,8},{1,25},{8,16},{9,1},{16,24},{17,9},{24,0},{25,17},{2,10},{3,... | collective-permute-start | bytes 202760 | tf_op jit(solution)/shard_map/ppermute | solution.py:384
  341.7 8.0 %collective-permute-start.38 = (bf16[8,4224]{1,0:T(8,128)(2,1)}, bf16[8,4224]{1,0:T(8,128)(2,1)}, u32[]{:S(2)}, u32[]{:S(2)}) collective-permute-start(bf16[8,4224]{1,0:T(8,128)(2,1)} %ring.64.refs_2_), channel_id=1, source_target_pairs={{0,2},{1,7},{2,4},{3,1},{4,6},{5,3},{6,0},{7,5},{8,10},{9,15},{10,... | collective-permute-start | bytes 202760 | tf_op jit(solution)/shard_map/ppermute | solution.py:384
  347.7 5.7 %collective-permute-start.37 = (bf16[8,3840]{1,0:T(8,128)(2,1)}, bf16[8,3840]{1,0:T(8,128)(2,1)}, u32[]{:S(2)}, u32[]{:S(2)}) collective-permute-start(bf16[8,3840]{1,0:T(8,128)(2,1)} %get-tuple-element.122.refs_2_), channel_id=1, source_target_pairs={{0,32},{1,97},{32,64},{33,1},{64,96},{65,33},{96,0},{97,65},{2,34}... | collective-permute-start | bytes 184328 | tf_op jit(solution)/shard_map/ppermute | solution.py:384
  349.6 5.8 %collective-permute-start.36 = (bf16[8,4224]{1,0:T(8,128)(2,1)}, bf16[8,4224]{1,0:T(8,128)(2,1)}, u32[]{:S(2)}, u32[]{:S(2)}) collective-permute-start(bf16[8,4224]{1,0:T(8,128)(2,1)} %ring.65.refs_2_), channel_id=1, source_target_pairs={{0,8},{1,25},{8,16},{9,1},{16,24},{17,9},{24,0},{25,17},{2,10},{3,... | collective-permute-start | bytes 202760 | tf_op jit(solution)/shard_map/ppermute | solution.py:384
  351.2 7.2 %collective-permute-start.39 = (bf16[8,4224]{1,0:T(8,128)(2,1)}, bf16[8,4224]{1,0:T(8,128)(2,1)}, u32[]{:S(2)}, u32[]{:S(2)}) collective-permute-start(bf16[8,4224]{1,0:T(8,128)(2,1)} %ring.66.refs_2_), channel_id=1, source_target_pairs={{0,2},{1,7},{2,4},{3,1},{4,6},{5,3},{6,0},{7,5},{8,10},{9,15},{10,... | collective-permute-start | bytes 202760 | tf_op jit(solution)/shard_map/ppermute | solution.py:384
  355.0 7.7 %collective-permute-start.40 = (bf16[8,3840]{1,0:T(8,128)(2,1)}, bf16[8,3840]{1,0:T(8,128)(2,1)}, u32[]{:S(2)}, u32[]{:S(2)}) collective-permute-start(bf16[8,3840]{1,0:T(8,128)(2,1)} %ring.67.refs_2_), channel_id=1, source_target_pairs={{0,32},{1,97},{32,64},{33,1},{64,96},{65,33},{96,0},{97,65},{2,34}... | collective-permute-start | bytes 184328 | tf_op jit(solution)/shard_map/ppermute | solution.py:384
  364.3 5.6 %collective-permute-start.41 = (bf16[8,3840]{1,0:T(8,128)(2,1)}, bf16[8,3840]{1,0:T(8,128)(2,1)S(1)}, u32[]{:S(2)}, u32[]{:S(2)}) collective-permute-start(bf16[8,3840]{1,0:T(8,128)(2,1)} %ring.70.refs_2_), channel_id=1, source_target_pairs={{0,32},{1,97},{32,64},{33,1},{64,96},{65,33},{96,0},{97,65},{2,34}... | collective-permute-start | bytes 184328 | tf_op jit(solution)/shard_map/ppermute | solution.py:384
  370.0 0.6 copy-start.9
  370.6 13.7 %copy-start.3 = (f32[8,896]{1,0:T(8,128)S(1)}, f32[8,896]{1,0:T(8,128)}, u32[]{:S(2)}) copy-start(f32[8,896]{1,0:T(8,128)} %get-tuple-element.126) | copy-start | bytes 86020
  370.6 13.7 %copy-start.6 = (f32[8,896]{1,0:T(8,128)S(1)}, f32[8,896]{1,0:T(8,128)}, u32[]{:S(2)}) copy-start(f32[8,896]{1,0:T(8,128)} %get-tuple-element.129) | copy-start | bytes 86020
  370.6 14.4 %copy-start.1 = (f32[8,896]{1,0:T(8,128)S(1)}, f32[8,896]{1,0:T(8,128)}, u32[]{:S(2)}) copy-start(f32[8,896]{1,0:T(8,128)} %get-tuple-element.127) | copy-start | bytes 86020
  370.6 14.4 %copy-start.2 = (f32[8,896]{1,0:T(8,128)S(1)}, f32[8,896]{1,0:T(8,128)}, u32[]{:S(2)}) copy-start(f32[8,896]{1,0:T(8,128)} %get-tuple-element.128) | copy-start | bytes 86020
  370.6 14.4 %copy-start.4 = (f32[8,896]{1,0:T(8,128)S(1)}, f32[8,896]{1,0:T(8,128)}, u32[]{:S(2)}) copy-start(f32[8,896]{1,0:T(8,128)} %get-tuple-element.130) | copy-start | bytes 86020
  370.6 14.4 %copy-start.5 = (f32[8,896]{1,0:T(8,128)S(1)}, f32[8,896]{1,0:T(8,128)}, u32[]{:S(2)}) copy-start(f32[8,896]{1,0:T(8,128)} %get-tuple-element.131) | copy-start | bytes 86020
Sparse Core Ops, SparseCore 0:
  15.8 95.5 all-gather.1

commit v3 on v1

v3 whole, which is shorter than its diff:
```python
import functools

import jax
import jax.numpy as jnp
from jax import lax
from jax.experimental import pallas as pl
from jax.experimental.pallas import tpu as pltpu
from jax.sharding import Mesh
from jax.sharding import PartitionSpec as P

H = 16
HD = 64
PAIR = 2 * HD
PAIRS = H // 2
epsilon = 1e-05
rope_base = 160000.0
masked_score = -1e30
AXES = ("y", "z", "x")
ALL = ("y", "z", "x", "c")
VMEM = 60 * 1024 * 1024
bf16 = jnp.bfloat16
f32 = jnp.float32

D = 1024
FF = 2624
CHUNKS = 3
CW = 896
MIX_AT = 3 * D
GAIN_AT = 4 * D
FF_AT = 4 * D + 128
W_COLS = FF_AT + CHUNKS * 3 * CW
ROWS = 512
MIX_CUTS = ((0, 384), (384, 768), (768, 1024))
A_COLS = D + 384


def dot(a, b):
    return lax.dot_general(a, b, (((1,), (0,)), ((), ())), preferred_element_type=f32)


def dot_t(a, b):
    return lax.dot_general(a, b, (((1,), (1,)), ((), ())), preferred_element_type=f32)


def dot_first(a, b):
    return lax.dot_general(a, b, (((0,), (0,)), ((), ())), preferred_element_type=f32)


def norm_parts(values):
    centered = values - jnp.mean(values, axis=-1, keepdims=True)
    scale = lax.rsqrt(jnp.mean(centered * centered, axis=-1, keepdims=True) + epsilon)
    return centered * scale, scale


def half_swapped(v, low_half):
    return jnp.where(low_half, pltpu.roll(v, PAIR - HD // 2, 1), pltpu.roll(v, HD // 2, 1))


def pair_slice(p, at=0):
    return pl.ds(pl.multiple_of(p * PAIR + at, PAIR), PAIR)


def cotangent_kernel(cot_ref, seg_ref, *refs):
    perms, gt_ref, gtts = refs[:CHUNKS], refs[CHUNKS], refs[CHUNKS + 1 :]
    gt = jnp.where(seg_ref[...] < 4, cot_ref[...].astype(f32), 0.0).astype(bf16)
    gt_ref[...] = gt
    for perm, gtt in zip(perms, gtts):
        gtt[...] = dot_t(perm[...], gt).astype(bf16)


def attend_kernel(
    tok_ref, seg_ref, segt_ref, cos_ref, sin_ref, w_ref,
    qkv_ref, prob_ref, res_ref, h1_ref, h2_ref, mixed, gain_ref,
    wp, wm, wg, packed, bias, sems,
):
    copies = [
        pltpu.make_async_copy(w_ref.at[:, pl.ds(GAIN_AT, 128)], wg, sems.at[0]),
        pltpu.make_async_copy(w_ref.at[:, pl.ds(0, 3 * D)], wp, sems.at[1]),
        pltpu.make_async_copy(w_ref.at[:, pl.ds(MIX_AT, D)], wm, sems.at[2]),
    ]
    for c in copies:
        c.start()
    tokens = tok_ref[...].astype(f32)
    xhat, _ = norm_parts(tokens)
    bias[...] = jnp.where(seg_ref[...] == segt_ref[...], 0.0, masked_score)
    copies[0].wait()
    gains = jnp.transpose(wg[...].astype(f32))[:8]
    gain_ref[...] = gains
    h1 = (xhat * gains[0:1]).astype(bf16)
    h1_ref[...] = h1
    copies[1].wait()
    packed[...] = dot(h1, wp[...])
    low_half = lax.broadcasted_iota(jnp.int32, (1, PAIR), 1) % HD < HD // 2
    first = lax.broadcasted_iota(jnp.int32, (1, PAIR), 1) < HD
    zero = jnp.zeros((), bf16)

    def pair(p, carry):
        cos, sin = cos_ref[...], sin_ref[...]
        q = packed[:, pair_slice(p)]
        k = packed[:, pair_slice(p, D)]
        q = (q * cos + half_swapped(q, low_half) * sin).astype(bf16)
        k = (k * cos + half_swapped(k, low_half) * sin).astype(bf16)
        v = packed[:, pair_slice(p, 2 * D)].astype(bf16)
        qkv_ref[:, pair_slice(p)] = q
        qkv_ref[:, pair_slice(p, D)] = k
        qkv_ref[:, pair_slice(p, 2 * D)] = v
        outs = []
        for side in range(2):
            mine = first if side == 0 else jnp.logical_not(first)
            scores = dot_t(jnp.where(mine, q, zero), k) * (HD**-0.5) + bias[...]
            top = jnp.max(scores, axis=-1, keepdims=True)
            e = jnp.exp(scores - top)
            probs = e * (1.0 / jnp.sum(e, axis=-1, keepdims=True))
            prob_ref[2 * p + side] = probs
            outs.append(dot(probs.astype(bf16), v))
        mixed[:, pair_slice(p)] = jnp.where(first, outs[0], outs[1]).astype(bf16)
        return carry

    lax.fori_loop(0, PAIRS, pair, 0)
    copies[2].wait()
    residual = tokens + dot(mixed[...], wm[...])
    res_ref[...] = residual
    xhat2, _ = norm_parts(residual)
    h2_ref[...] = (xhat2 * gains[1:2]).astype(bf16)


def started(pairs, sems):
    copies = [pltpu.make_async_copy(a, b, sems.at[i]) for i, (a, b) in enumerate(pairs)]
    for c in copies:
        c.start()
    return copies


def gated_kernel(chunk, has_sum, h2_hbm, gt_hbm, perm_hbm, gtt_hbm, w_hbm, *refs):
    if has_sum:
        branch_in, gh2_in = refs[:2]
        refs = refs[2:]
    branch_ref, gh2_ref, sib_hbm, own_hbm = refs[:4]
    h2, gt, perm, gtt, w, gate, up, gh, hid, gg, gu, h2t, grads, sems, out_sems = refs[4:]
    base = FF_AT + chunk * 3 * CW
    pieces = [
        (w_hbm.at[:, pl.ds(base + i * CW, CW)], w.at[:, pl.ds(i * CW, CW)]) for i in range(3)
    ]
    copies = started(
        [(h2_hbm, h2), pieces[0], pieces[1], (gt_hbm, gt), pieces[2], (perm_hbm, perm), (gtt_hbm, gtt)],
        sems,
    )
    copies[0].wait()
    copies[1].wait()
    gate[...] = dot(h2[...], w[:, :CW])
    copies[2].wait()
    up[...] = dot(h2[...], w[:, CW : 2 * CW])
    copies[3].wait()
    copies[4].wait()
    gh[...] = dot(gt[...], w[:, 2 * CW :])
    copies[5].wait()
    h2t[...] = dot_t(perm[...], h2[...]).astype(bf16)
    size = 16

    def rows(i, carry):
        r = pl.ds(pl.multiple_of(i * size, size), size)
        g, u, d = gate[r, :], up[r, :], gh[r, :]
        cdf = 0.5 * (1.0 + lax.erf(g * (0.5**0.5)))
        act = g * cdf
        slope = cdf + g * (jnp.exp(-0.5 * g * g) * 0.3989422804014327)
        hid[r, :] = (act * u).astype(bf16)
        gg[r, :] = (d * u * slope).astype(bf16)
        gu[r, :] = (d * act).astype(bf16)
        return carry

    lax.fori_loop(0, gate.shape[0] // size, rows, 0)
    copies[6].wait()
    outs = []
    for half, to in enumerate((sib_hbm, own_hbm)):
        rows_at = pl.ds(half * ROWS, ROWS)
        for i, (left, right) in enumerate(((h2t, gg), (h2t, gu), (gtt, hid))):
            cols = pl.ds(i * CW, CW)
            grads[rows_at, cols] = dot(left[rows_at, :], right[...]).astype(bf16)
            outs.append(
                pltpu.make_async_copy(
                    grads.at[rows_at, cols], to.at[:, cols], out_sems.at[3 * half + i]
                )
            )
            outs[-1].start()
    branch = dot_t(hid[...], w[:, 2 * CW :])
    gh2 = dot_t(gg[...], w[:, :CW]) + dot_t(gu[...], w[:, CW : 2 * CW])
    if has_sum:
        branch = branch + branch_in[...]
        gh2 = gh2 + gh2_in[...]
    branch_ref[...] = branch
    gh2_ref[...] = gh2
    for c in outs:
        c.wait()


def heads_kernel(
    gt_ref, seg_ref, gain_ref, res_ref, branch_ref, gh2_ref, cos_ref, sin_ref,
    qkv_hbm, prob_hbm, w_hbm,
    out_ref, gr, ga_ref, second_ref, gp,
    wm, qkv, prob, gm, sems,
):
    copies = started(
        [(w_hbm.at[:, pl.ds(MIX_AT, D)], wm), (qkv_hbm, qkv), (prob_hbm, prob)], sems
    )
    residual = res_ref[...]
    live = seg_ref[...] < 4
    out_ref[...] = jnp.where(live, residual + branch_ref[...], 0.0).astype(bf16)
    xhat2, r2 = norm_parts(residual)
    gh2 = gh2_ref[...]
    second_ref[...] = jnp.broadcast_to(jnp.sum(gh2 * xhat2, axis=0, keepdims=True), (8, D))
    n = gh2 * gain_ref[1:2]
    spread = jnp.mean(n * xhat2, axis=-1, keepdims=True)
    grad_res = gt_ref[...].astype(f32) + r2 * (
        n - jnp.mean(n, axis=-1, keepdims=True) - xhat2 * spread
    )
    gr[...] = grad_res
    ga = grad_res.astype(bf16)
    ga_ref[...] = ga
    copies[0].wait()
    gm[...] = dot_t(ga, wm[...]).astype(bf16)
    copies[1].wait()
    copies[2].wait()
    low_half = lax.broadcasted_iota(jnp.int32, (1, PAIR), 1) % HD < HD // 2
    first = lax.broadcasted_iota(jnp.int32, (1, PAIR), 1) < HD
    zero = jnp.zeros((), bf16)

    def pair(p, carry):
        cos, sin = cos_ref[...], sin_ref[...]
        q = qkv[:, pair_slice(p)]
        k = qkv[:, pair_slice(p, D)]
        v = qkv[:, pair_slice(p, 2 * D)]
        g = gm[:, pair_slice(p)]
        dq, dk, dv = [], [], []
        for side in range(2):
            mine = first if side == 0 else jnp.logical_not(first)
            probs = prob[2 * p + side]
            grad_probs = dot_t(jnp.where(mine, g, zero), v)
            weighted = probs * grad_probs
            delta = jnp.sum(weighted, axis=-1, keepdims=True)
            gs = (weighted - probs * delta).astype(bf16)
            dq.append(dot(gs, k))
            dk.append(dot_first(gs, q))
            dv.append(dot_first(probs.astype(bf16), g))
        dq = jnp.where(first, dq[0], dq[1]) * (HD**-0.5)
        dk = jnp.where(first, dk[0], dk[1]) * (HD**-0.5)
        dv = jnp.where(first, dv[0], dv[1])
        gp[:, pair_slice(p)] = (dq * cos - half_swapped(dq, low_half) * sin).astype(bf16)
        gp[:, pair_slice(p, D)] = (dk * cos - half_swapped(dk, low_half) * sin).astype(bf16)
        gp[:, pair_slice(p, 2 * D)] = dv.astype(bf16)
        return carry

    lax.fori_loop(0, PAIRS, pair, 0)


def back_kernel(
    h1_ref, mixed_ref, ga, gp, tok_ref, gr, gain_ref, second_ref, perm0, perm1, perm2, w_hbm,
    gin_ref, sib0, sib1, sib2, own0, own1, own2,
    p0, p1, p2, wp, h1t, mt, grads, sems, out_sems,
):
    perms = (p0, p1, p2)
    copies = started(
        [(perm0, p0), (perm1, p1), (perm2, p2), (w_hbm.at[:, pl.ds(0, 3 * D)], wp)], sems
    )
    outs = []
    for j in range(CHUNKS):
        copies[j].wait()
        h1t[...] = dot_t(perms[j][...], h1_ref[...]).astype(bf16)
        mt[...] = dot_t(perms[j][...], mixed_ref[...]).astype(bf16)
        lo, hi = MIX_CUTS[j]
        to = grads.at[j]
        to[:, pl.ds(0, D)] = dot(h1t[...], gp[:, j * D : (j + 1) * D]).astype(bf16)
        to[:, pl.ds(D, hi - lo)] = dot(mt[...], ga[:, lo:hi]).astype(bf16)
        if j == CHUNKS - 1:
            copies[3].wait()
            gh1 = dot_t(gp[...], wp[...])
            xhat1, r1 = norm_parts(tok_ref[...].astype(f32))
            one = jnp.sum(gh1 * xhat1, axis=0, keepdims=True)
            m = gh1 * gain_ref[0:1]
            spread = jnp.mean(m * xhat1, axis=-1, keepdims=True)
            gin_ref[...] = gr[...] + r1 * (m - jnp.mean(m, axis=-1, keepdims=True) - xhat1 * spread)
            row = lax.broadcasted_iota(jnp.int32, (128, D), 0)
            both = jnp.where(row == 0, one, jnp.where(row == 1, second_ref[0:1], 0.0)).astype(bf16)
            to[:, pl.ds(D + 256, 128)] = dot_t(perms[j][...], both).astype(bf16)
        for half, group in enumerate(((sib0, sib1, sib2), (own0, own1, own2))):
            outs.append(
                pltpu.make_async_copy(
                    grads.at[j, pl.ds(half * ROWS, ROWS)], group[j], out_sems.at[2 * j + half]
                )
            )
            outs[-1].start()
    for c in outs:
        c.wait()


def turn_kernel(*refs):
    send, keep, whole = refs[8:]
    at = 0
    for terms in (refs[:4], refs[4:8]):
        total = terms[0][...].astype(f32)
        for t in terms[1:]:
            total = total + t[...].astype(f32)
        whole[:, pl.ds(at, total.shape[1])] = total
        at += total.shape[1]
    send[...] = whole[pl.ds(0, 64), :].astype(bf16)
    keep[...] = whole[pl.ds(64, 64), :].astype(bf16)


def pack_kernel(packed, mixer, expand, reduce, gains, out, wide):
    out[:, pl.ds(0, MIX_AT)] = packed[...]
    out[:, pl.ds(MIX_AT, D)] = mixer[...]
    out[:, pl.ds(GAIN_AT, 128)] = gains[...]
    both = expand[...].astype(f32)
    wide[...] = jnp.zeros(wide.shape, f32)
    wide[0, :, pl.ds(0, FF)] = both[:, :FF]
    wide[1, :, pl.ds(0, FF)] = pltpu.roll(both, FF, 1)[:, :FF]
    wide[2, :, pl.ds(0, FF)] = reduce[...].astype(f32)
    for j in range(CHUNKS):
        for i in range(3):
            out[:, pl.ds(FF_AT + (3 * j + i) * CW, CW)] = wide[i, :, pl.ds(j * CW, CW)].astype(bf16)


def finish_kernel(*refs):
    gots, kepts = refs[:3], refs[3:6]
    packed, mixer, expand, reduce, gain, wide = refs[6:]
    ff = 3 * CW
    for j in range(CHUNKS):
        total = gots[j][...].astype(f32) + kepts[j][...].astype(f32)
        for i in range(3):
            wide[i, :, pl.ds(j * CW, CW)] = total[:, i * CW : (i + 1) * CW]
        packed[:, pl.ds(j * D, D)] = total[:, ff : ff + D]
        lo, hi = MIX_CUTS[j]
        mixer[:, pl.ds(lo, hi - lo)] = total[:, ff + D : ff + D + hi - lo]
    gain[...] = total[:, ff + D + 256 :]
    reduce[...] = wide[2, :, pl.ds(0, FF)]
    lane = lax.broadcasted_iota(jnp.int32, (1, 2 * FF), 1)
    pad = jnp.zeros((8, 2 * FF - CHUNKS * CW), f32)
    gate = jnp.concatenate([wide[0], pad], axis=1)
    up = pltpu.roll(jnp.concatenate([wide[1], pad], axis=1), FF, 1)
    expand[...] = jnp.where(lane < FF, gate, up)


def arr(shape, dtype):
    return jax.ShapeDtypeStruct(shape, dtype)


VSPEC = pl.BlockSpec(memory_space=pltpu.VMEM)
HSPEC = pl.BlockSpec(memory_space=pl.ANY)
DMA = pltpu.SemaphoreType.DMA


def run(
    kernel, name, inputs, out_shape, scratch=(), in_hbm=(), out_hbm=(), after=(), through=(), specs=()
):
    count, outs, extra = len(inputs), len(out_shape), len(after) + len(through)

    def with_order(*refs):
        rest = refs[count + extra :]
        kernel(*refs[:count], *rest[:outs], *rest[outs + len(through) :])

    return pl.pallas_call(
        with_order,
        out_shape=tuple(out_shape) + tuple(arr(t.shape, t.dtype) for t in through),
        grid=(1,) if specs else (),
        in_specs=(list(specs) or [HSPEC if i in in_hbm else VSPEC for i in range(count)])
        + [HSPEC] * extra,
        out_specs=tuple(HSPEC if i in out_hbm else VSPEC for i in range(outs))
        + (HSPEC,) * len(through),
        input_output_aliases={count + len(after) + i: outs + i for i in range(len(through))},
        scratch_shapes=list(scratch),
        compiler_params=pltpu.CompilerParams(vmem_limit_bytes=VMEM),
        cost_estimate=pl.CostEstimate(flops=10**14, bytes_accessed=1024, transcendentals=0),
        name=name,
    )(*inputs, *after, *through)


def token_layout(lengths, slot_count):
    places = jnp.arange(slot_count, dtype=jnp.int32)
    ends = jnp.cumsum(lengths)
    starts = ends - lengths
    segment = jnp.sum((places[:, None] >= ends[None, :]).astype(jnp.int32), axis=1)
    live = places < ends[-1]
    picked = (segment[:, None] == jnp.arange(lengths.shape[0], dtype=jnp.int32)[None, :]).astype(
        jnp.int32
    )
    position = jnp.where(live, places - jnp.sum(picked * starts[None, :], axis=1), 0)
    segment = jnp.where(live, segment, lengths.shape[0] + places)
    return segment, position


def rotary_tables(position):
    frequency = rope_base ** (-(jnp.arange(HD // 2, dtype=f32) * 2.0 / HD))
    angles = position.astype(f32)[:, None] * frequency
    cos, sin = jnp.cos(angles), jnp.sin(angles)
    return (
        jnp.concatenate([cos, cos, cos, cos], axis=-1),
        jnp.concatenate([-sin, sin, -sin, sin], axis=-1),
    )


ORDERS = (("x", "y", "z"), ("y", "z", "x"), ("z", "x", "y"))


def hops(core):
    return (1, 3) if core == 0 else (3, 1)


def row_order(order):
    core = lax.axis_index("c")
    row = jnp.arange(D, dtype=jnp.int32)
    mine, inner = row >= ROWS, row % ROWS
    side = jnp.where(mine, core, 1 - core)
    place = {}
    for axis, size in zip(order, (128, 32, 8)):
        turn = inner // size % 4
        apart = jnp.where(turn == 0, 2, jnp.where(turn == 3, 0, jnp.where((turn == 1) == (side == 0), 1, 3)))
        place[axis] = lax.axis_index(axis) ^ apart
    feature = ((place["y"] * 4 + place["z"]) * 4 + place["x"]) * 16 + side * 8 + inner % 8
    return (feature[:, None] == jnp.arange(D, dtype=jnp.int32)[None, :]).astype(bf16)


def to_partner(a, axis, step):
    pairs = [(i * 2 + c, (i ^ hops(c)[step]) * 2 + c) for i in range(4) for c in range(2)]
    return lax.ppermute(a, (axis, "c"), pairs)


def to_sibling(a):
    return lax.ppermute(a, "c", [(0, 1), (1, 0)])


def added(*arrays):
    return sum(a.astype(f32) for a in arrays).astype(bf16)


class PartSum:
    def __init__(self, order, sib, own):
        self.axis = order[0]
        self.own, self.arrived = own, to_sibling(sib)
        self.lo, self.step, self.got = 0, 0, None

    def piece(self, lo, rows):
        at = slice(lo, lo + rows)
        terms = [self.own[at], self.arrived[at]]
        if self.got is not None:
            terms.append(self.got[lo - self.lo : lo - self.lo + rows])
        return added(*terms)

    def send(self):
        rows = (ROWS - self.lo) // 2
        out = self.piece(self.lo, rows)
        got = to_partner(out, self.axis, self.step)
        self.got = got if self.got is None else (got, self.got)
        self.lo += rows
        self.step += 1
        return out

    def last_terms(self):
        cols = self.own.shape[1]
        got, kept = self.got
        specs = [pl.BlockSpec((128, cols), lambda i, at=at: (at, 0)) for at in (3, 3, 0, 1)]
        return (self.own, self.arrived, got, kept), specs


def halves(a):
    n = a.shape[0] // 2
    return a[:n], a[n:]


def local_step(tokens, cotangent, lengths, weights, perms, part_sum):
    n = tokens.shape[0]
    segment, position = token_layout(lengths, n)
    cos, sin = rotary_tables(position)
    seg_col, seg_row = segment[:, None], segment[None, :]
    tile = arr((n, D), bf16)
    wide = arr((n, D), f32)
    vm = pltpu.VMEM
    gt, *gtts = run(
        cotangent_kernel, "cotangent", (cotangent, seg_col, *perms),
        (tile,) + (arr((D, n), bf16),) * CHUNKS,
    )
    qkv, probs, residual, h1, h2, mixed, gains = run(
        attend_kernel, "attend", (tokens, seg_col, seg_row, cos, sin, weights),
        (arr((n, 3 * D), bf16), arr((H, n, n), f32), wide, tile, tile, tile, arr((8, D), f32)),
        [
            vm((D, 3 * D), bf16), vm((D, D), bf16), vm((D, 128), bf16), vm((n, 3 * D), f32),
            vm((n, n), f32), DMA((3,)),
        ],
        in_hbm=(5,),
    )
    sums, ff, after = (), [], ()
    for j in range(CHUNKS):
        through = (ff[1].own,) if j == 2 else ()
        results = run(
            functools.partial(gated_kernel, j, j > 0), "gated",
            (h2, gt, perms[j], gtts[j], weights, *sums),
            (wide, wide) + (arr((ROWS, 3 * CW), bf16),) * 2,
            [vm((n, D), bf16), vm((n, D), bf16), vm((D, D), bf16), vm((D, n), bf16), vm((D, 3 * CW), bf16)]
            + [vm((n, CW), f32)] * 3
            + [vm((n, CW), bf16)] * 3
            + [vm((D, n), bf16), vm((D, 3 * CW), bf16), DMA((7,)), DMA((6,))],
            in_hbm=(0, 1, 2, 3, 4),
            out_hbm=(2, 3),
            after=after,
            through=through,
        )
        sums = results[:2]
        ff.append(part_sum(ORDERS[j], results[2], results[3]))
        if j == 2:
            ff[1].own = results[4]
        if j > 0:
            after = (ff[j - 1].send(),)
    branch, gh2 = sums
    block_output, gr, ga, second, gp = run(
        heads_kernel, "heads",
        (gt, seg_col, gains, residual, branch, gh2, cos, sin, qkv, probs, weights),
        (tile, wide, tile, arr((8, D), f32), arr((n, 3 * D), bf16)),
        [vm((D, D), bf16), vm((n, 3 * D), bf16), vm((H, n, n), f32), vm((n, D), bf16), DMA((3,))],
        in_hbm=(8, 9, 10),
        after=after,
    )
    after = (ff[2].send(), ff[0].send())
    input_grad, *pieces = run(
        back_kernel, "back", (h1, mixed, ga, gp, tokens, gr, gains, second, *perms, weights),
        (wide,) + (arr((ROWS, A_COLS), bf16),) * 6,
        [vm((D, D), bf16)] * 3
        + [vm((D, 3 * D), bf16), vm((D, n), bf16), vm((D, n), bf16), vm((3, D, A_COLS), bf16)]
        + [DMA((4,)), DMA((6,))],
        in_hbm=(8, 9, 10, 11),
        out_hbm=(1, 2, 3, 4, 5, 6),
        after=after,
        through=(ff[0].own, ff[1].own),
    )
    ff[0].own, ff[1].own = pieces[6:]
    att = [part_sum(ORDERS[j], pieces[j], pieces[3 + j]) for j in range(CHUNKS)]
    return block_output, input_grad, ff, att


def summed(ff, att):
    for part in (ff[1], att[0], ff[2], att[1], att[2], *att):
        part.send()
    pairs = []
    for f, a in zip(ff, att):
        (f_terms, f_specs), (a_terms, a_specs) = f.last_terms(), a.last_terms()
        cols = f.own.shape[1] + a.own.shape[1]
        pairs.append(
            run(
                turn_kernel, "turn", f_terms + a_terms, (arr((64, cols), bf16),) * 2,
                [pltpu.VMEM((128, cols), f32)], specs=f_specs + a_specs,
            )
        )
    for ring, step in ((1, 0), (1, 1), (2, 0), (2, 1)):
        gots = [to_partner(p[0], order[ring], step) for p, order in zip(pairs, ORDERS)]
        kept = [p[1] for p in pairs]
        if (ring, step) != (2, 1):
            pairs = [halves(added(g, k)) for g, k in zip(gots, kept)]
    return gots, kept


def own_rows(gots, kept):
    n = 8
    *grads, gains = run(
        finish_kernel, "finish", (*gots, *kept),
        tuple(arr((n, c), f32) for c in (3 * D, D, 2 * FF, FF, 128)),
        [pltpu.VMEM((3, n, CHUNKS * CW), f32)],
    )
    return (*grads, gains[:, 0], gains[:, 1])


def body(
    tokens, packed_proj, mixer_proj, expand_proj, reduce_proj, first_gain, second_gain,
    sequence_lengths, cotangent,
):
    gains = jnp.pad(jnp.stack([first_gain, second_gain], axis=1), ((0, 0), (0, 126)))
    (shard,) = run(
        pack_kernel, "pack", (packed_proj, mixer_proj, expand_proj, reduce_proj, gains),
        (arr((8, W_COLS), bf16),), [pltpu.VMEM((3, 8, CHUNKS * CW), f32)],
    )
    weights = lax.all_gather(shard, ALL, axis=0, tiled=True)
    perms = [row_order(order) for order in ORDERS]
    block_output, input_grad, ff, att = local_step(
        tokens, cotangent, sequence_lengths, weights, perms, PartSum
    )
    return (block_output, input_grad, *own_rows(*summed(ff, att)))


def solution(mesh):
    torus = Mesh(mesh.devices.reshape(4, 4, 4, 2), ALL)
    row, flat = P(ALL, None), P(ALL)
    return jax.shard_map(
        body,
        mesh=torus,
        in_specs=(row,) * 5 + (flat, flat, flat, row),
        out_specs=(row,) * 6 + (flat, flat),
        check_vma=False,
    )
```

time: 383 us -> 308 us (0.80)
  waiting for transfers between devices: 219 us -> 110 us
  Pallas kernels: 80.5 us -> 107 us
  other arithmetic: 20 us -> 33 us
  local copies, waits for them, and re-layouts: 10.9 us -> 6.59 us
    ppermute x60 -> x30, waiting for transfers between devices: 132 us -> 30 us  [the longest x24 30 us: to_partner(): return lax.ppermute(a, (axis, 'c'), pairs)]
    pallas_call x5 -> x12, Pallas kernels: 80.5 us -> 107 us  [run(): pl.pallas_call(with_order, out_shape=tuple(out_shape) + tuple((arr(t.shap...]
    convert_element_type x54 -> x21, other arithmetic: 7.6 us -> 21.9 us  [added(): return sum((a.astype(f32) for a in arrays)).astype(bf16)]
    all_gather x1, waiting for transfers between devices: 86.8 us -> 79.6 us  [body(): weights = lax.all_gather(shard, ALL, axis=0, tiled=True)]
    unnamed x23 -> x50, local copies, waits for them, and re-layouts: 6.73 us -> 1.73 us
    ppermute x60 -> x30, starting transfers between devices: 32.3 us -> 32.1 us  [the longest x24 28.5 us: to_partner(): return lax.ppermute(a, (axis, 'c'), pairs)]
  transfers between devices with their start and end apart: 61 -> 31, of which waited for: 48 -> 13; matrix products, arithmetic and copies ran while one was open for 5% -> 12% of each run, Pallas kernels for 0% -> 24%
where the time goes in v3:
time: 308 us; the launch traced here: 303 us
  waiting for transfers between devices  110 us (36%)
  Pallas kernels  107 us (35%)
  other arithmetic  33 us (11%)
  starting transfers between devices  32.1 us (10%)
  between operations  14.9 us (5%)
  local copies, waits for them, and re-layouts  6.59 us (2%)
    pallas_call x12, Pallas kernels, run(): pl.pallas_call(with_order, out_shape=tuple(out_shape) + tuple((arr(t.shap...  107 us
    all_gather x1, waiting for transfers between devices, body(): weights = lax.all_gather(shard, ALL, axis=0, tiled=True)  79.6 us
    ppermute x24, waiting for transfers between devices, to_partner(): return lax.ppermute(a, (axis, 'c'), pairs)  30 us
    ppermute x24, starting transfers between devices, to_partner(): return lax.ppermute(a, (axis, 'c'), pairs)  28.5 us
    convert_element_type x21, other arithmetic, added(): return sum((a.astype(f32) for a in arrays)).astype(bf16)  21.9 us
  transfers between devices with their start and end apart: 31, of which 13 were waited for; matrix products, arithmetic and copies ran while one was open for 12% of the time, Pallas kernels for 24%

profile of v3, /device:TPU:0, one launch (start us, length us, event | category | flops | bytes accessed | tf_op | source)
XLA Modules:
  0.0 302.9 jit_solution(4526083326491041872)
XLA Ops:
  7.2 0.7 pad_maximum_fusion.2
  8.6 1.7 pack.1
  11.4 1.8 fusion.refs_2_.refs_8_
  13.2 1.8 fusion.1.refs_3_.refs_2_.refs_9_
  15.0 1.7 fusion.2.refs_4_.refs_2_.refs_10_
  16.7 1.3 add_select_fusion.refs_1_
  18.0 6.1 %cotangent.1 = (bf16[256,1024]{1,0:T(8,128)(2,1)}, bf16[1024,256]{1,0:T(8,128)(2,1)}, bf16[1024,256]{1,0:T(8,128)(2,1)}, bf16[1024,256]{1,0:T(8,128)(2,1)}) custom-call(bf16[256,1024]{1,0:T(8,128)(2,1)} %refs_0_.3, s32[256,1]{1,0:T(8,128)} %add_select_fusion.refs_1_, bf16[1024,1024]{1,0:T(8,128)(2,1)} %fusion.refs_2_.refs_8_, ...), custom_call_target="tpu_custom_call" | custom-call | flops 100000000376832 | bytes 1024 | tf_op jit(solution)/shard_map/cotangent/pallas_call | solution.py:360
  24.2 0.7 fusion.22
  25.4 1.0 pad_maximum_fusion
  26.4 1.2 compare_select_fusion.refs_2_
  27.6 79.6 %all-gather.2.cloned.1.call-done.refs_5_.refs_4_.refs_10_.refs_11_ = bf16[1024,12288]{1,0:T(8,128)(2,1)} async-done(((bf16[8,12288]{1,0:T(8,128)(2,1)}), bf16[1024,12288]{1,0:T(8,128)(2,1)}) %all-gather.2.cloned.1.call-update) | async-done | bytes 25165840 | tf_op jit(solution)/shard_map/all_gather | solution.py:577
  107.3 18.0 %attend.1 = (bf16[256,3072]{1,0:T(8,128)(2,1)}, f32[16,256,256]{2,1,0:T(8,128)}, f32[256,1024]{1,0:T(8,128)}, bf16[256,1024]{1,0:T(8,128)(2,1)}, bf16[256,1024]{...) custom-call(bf16[256,1024]{1,0:T(8,128)(2,1)} %refs_4_.1, s32[256,1]{1,0:T(8,128)} %add_select_fusion.refs_1_, ...), custom_call_target="tpu_custom_call" | custom-call | flops 100000000376832 | bytes 1024 | tf_op jit(solution)/shard_map/attend/pallas_call | solution.py:360
  125.3 11.4 %gated.3 = (f32[256,1024]{1,0:T(8,128)}, f32[256,1024]{1,0:T(8,128)}, bf16[512,2688]{1,0:T(8,128)(2,1)}, bf16[512,2688]{1,0:T(8,128)(2,1)}) custom-call(bf16[256,1024]{1,0:T(8,128)(2,1)} %get-tuple-element.60.refs_0_, bf16[256,1024]{1,0:T(8,128)(2,1)} %get-tuple-element.57.refs_1_.refs_0_, bf16[1024,1024]{1,0:T(8,128)(2,1)} %fusion.refs_2_.refs_8_, ...), custom_call_target="tpu_custom_call" | custom-call | flops 100000000376832 | bytes 1024 | tf_op jit(solution)/shard_map/gated/pallas_call | solution.py:360
  137.0 13.3 %gated.4 = (f32[256,1024]{1,0:T(8,128)}, f32[256,1024]{1,0:T(8,128)}, bf16[512,2688]{1,0:T(8,128)(2,1)}, bf16[512,2688]{1,0:T(8,128)(2,1)}) custom-call(bf16[256,1024]{1,0:T(8,128)(2,1)} %get-tuple-element.60.refs_0_, bf16[256,1024]{1,0:T(8,128)(2,1)} %get-tuple-element.57.refs_1_.refs_0_, bf16[1024,1024]{1,0:T(8,128)(2,1)} %fusion.1.refs_3_.refs_2_.refs_9_, ...), custom_call_target="tpu_custom_call" | custom-call | flops 100000000376832 | bytes 1024 | tf_op jit(solution)/shard_map/gated/pallas_call | solution.py:360
  150.7 2.8 add_convert_fusion.2.refs_7_
  153.4 1.5 collective-permute-start.3
  154.9 12.9 %gated.5 = (f32[256,1024]{1,0:T(8,128)}, f32[256,1024]{1,0:T(8,128)}, bf16[512,2688]{1,0:T(8,128)(2,1)}, bf16[512,2688]{1,0:T(8,128)(2,1)}, bf16[512,2688]{1,0:T(8,128)(2,1)}) custom-call(bf16[256,1024]{1,0:T(8,128)(2,1)} %get-tuple-element.60.refs_0_, bf16[256,1024]{1,0:T(8,128)(2,1)} %get-tuple-element.57.refs_1_.refs_0_, ...), custom_call_target="tpu_custom_call", output_to_operand_aliasing={{4}: (8, {})} | custom-call | flops 100000000376832 | bytes 1024 | tf_op jit(solution)/shard_map/gated/pallas_call | solution.py:360
  167.8 1.3 collective-permute-start.2
  169.1 3.2 %add_convert_fusion.1.refs_11_ = bf16[256,2688]{1,0:T(8,128)(2,1)} fusion(bf16[512,2688]{1,0:T(8,128)(2,1)} %collective-permute-done.1.refs_1_, bf16[512,2688]{1,0:T(8,128)(2,1)} %get-tuple-element.75.refs_15_), kind=kLoop, calls=%fused_computation.7 | loop fusion | flops 2752512 | bytes 4128768 | tf_op jit(solution)/shard_map/convert_element_type | solution.py:431
  172.3 1.7 collective-permute-start.12
  174.0 14.6 %heads.1 = (bf16[256,1024]{1,0:T(8,128)(2,1)}, f32[256,1024]{1,0:T(8,128)}, bf16[256,1024]{1,0:T(8,128)(2,1)}, f32[8,1024]{1,0:T(8,128)}, bf16[256,3072]{1,0:T(8,128)(2,1)}) custom-call(bf16[256,1024]{1,0:T(8,128)(2,1)} %get-tuple-element.57.refs_1_.refs_0_, s32[256,1]{1,0:T(8,128)} %add_select_fusion.refs_1_, f32[8,1024]{1,0:T(8,128)} %get-tuple-element.58.refs_2_.refs_6_, ...), custom_call_target="tpu_custom_call" | custom-call | flops 100000000376832 | bytes 1024 | tf_op jit(solution)/shard_map/heads/pallas_call | solution.py:360
  188.6 2.8 add_convert_fusion.8.refs_13_
  191.4 0.9 collective-permute-start.4
  192.3 2.8 add_convert_fusion.refs_12_
  195.7 16.5 %back.1 = (f32[256,1024]{1,0:T(8,128)}, bf16[512,1408]{1,0:T(8,128)(2,1)}, bf16[512,1408]{1,0:T(8,128)(2,1)}, bf16[512,1408]{1,0:T(8,128)(2,1)}, bf16[512,1408]{...) custom-call(bf16[256,1024]{1,0:T(8,128)(2,1)} %get-tuple-element.78., ...), custom_call_target="tpu_custom_call", output_to_operand_aliasing={{7}: (14, {}), {8}: (15, {})} | custom-call | flops 100000000376832 | bytes 1024 | tf_op jit(solution)/shard_map/back/pallas_call | solution.py:360
  212.2 1.5 collective-permute-start.5
  213.8 2.6 add_convert_fusion.7
  216.4 1.3 collective-permute-start.13
  217.7 2.6 add_convert_fusion.6
  220.4 2.3 collective-permute-start.22
  223.2 1.7 collective-permute-start.15
  225.3 8.9 %collective-permute-done.6.refs_7_ = bf16[256,1408]{1,0:T(8,128)(2,1)S(1)} collective-permute-done((bf16[256,1408]{1,0:T(8,128)(2,1)S(1)}, bf16[256,1408]{1,0:T(8,128)(2,1)S(1)}, u32[]{:S(2)}, u32[]{:S(2)}) %collective-permute-start.6) | collective-permute-done | bytes 720928 | tf_op jit(solution)/shard_map/ppermute | solution.py:423
  234.2 0.7 collective-permute-start.24
  235.0 1.2 collective-permute-start.7
  236.2 0.9 add_convert_fusion.13
  237.1 8.4 %collective-permute-done.24.refs_7_ = bf16[256,1408]{1,0:T(8,128)(2,1)S(1)} collective-permute-done((bf16[256,1408]{1,0:T(8,128)(2,1)S(1)}, bf16[256,1408]{1,0:T(8,128)(2,1)S(1)}, u32[]{:S(2)}, u32[]{:S(2)}) %collective-permute-start.24) | collective-permute-done | bytes 720928 | tf_op jit(solution)/shard_map/ppermute | solution.py:423
  245.5 1.1 collective-permute-start.16
  246.6 0.9 add_convert_fusion.12
  247.5 1.8 collective-permute-start.25
  249.3 0.7 copy-done.17
  250.1 3.5 %turn.3 = (bf16[64,4096]{1,0:T(8,128)(2,1)}, bf16[64,4096]{1,0:T(8,128)(2,1)}) custom-call(bf16[512,2688]{1,0:T(8,128)(2,1)} %get-tuple-element.87.refs_0_, bf16[512,2688]{1,0:T(8,128)(2,1)} %collective-permute-done.refs_1_, bf16[128,2688]{1,0:T(8,128)(2,1)} %collective-permute-done.4.refs_2_, bf16[256,2688]{1,0:T(8,128)(2,1)} %collective-permute-done.3.refs_3_, ...), custom_call_target="tpu_custom_call" | custom-call | flops 100000000376832 | bytes 1024 | tf_op jit(solution)/shard_map/turn/pallas_call | solution.py:360
  253.6 0.8 collective-permute-done.16.refs_6_
  254.4 3.4 %turn.4 = (bf16[64,4096]{1,0:T(8,128)(2,1)}, bf16[64,4096]{1,0:T(8,128)(2,1)}) custom-call(bf16[512,2688]{1,0:T(8,128)(2,1)} %get-tuple-element.92.refs_0_, bf16[512,2688]{1,0:T(8,128)(2,1)} %collective-permute-done.1.refs_1_, bf16[128,2688]{1,0:T(8,128)(2,1)} %collective-permute-done.13.refs_2_, bf16[256,2688]{1,0:T(8,128)(2,1)} %collective-permute-done.12.refs_3_, ...), custom_call_target="tpu_custom_call" | custom-call | flops 100000000376832 | bytes 1024 | tf_op jit(solution)/shard_map/turn/pallas_call | solution.py:360
  257.9 0.7 collective-permute-start.17
  258.6 3.5 %turn.5 = (bf16[64,4096]{1,0:T(8,128)(2,1)}, bf16[64,4096]{1,0:T(8,128)(2,1)}) custom-call(bf16[512,2688]{1,0:T(8,128)(2,1)} %get-tuple-element.84.refs_0_, bf16[512,2688]{1,0:T(8,128)(2,1)} %collective-permute-done.2.refs_1_, bf16[128,2688]{1,0:T(8,128)(2,1)} %collective-permute-done.22.refs_2_, bf16[256,2688]{1,0:T(8,128)(2,1)} %collective-permute-done.21.refs_3_, ...), custom_call_target="tpu_custom_call" | custom-call | flops 100000000376832 | bytes 1024 | tf_op jit(solution)/shard_map/turn/pallas_call | solution.py:360
  262.1 1.0 collective-permute-done.8
  263.1 1.2 add_convert_fusion.11
  264.3 2.7 collective-permute-start.9
  267.4 1.2 add_convert_fusion.10
  268.6 1.1 collective-permute-start.18
  269.7 1.8 collective-permute-done.26
  271.6 1.2 collective-permute-start.27
  272.9 1.7 collective-permute-start.10
  274.6 3.0 collective-permute-done.18
  277.8 2.2 collective-permute-done.27
  281.1 2.0 collective-permute-start.11
  283.5 0.6 fusion.24
  284.1 1.2 collective-permute-start.20
  285.6 0.6 fusion.23
  286.3 2.5 collective-permute-start.29
  288.8 0.8 collective-permute-done.20.refs_1_
  289.6 2.1 collective-permute-done.29.refs_2_
  292.4 1.8 finish.1
  294.1 1.5 slice_reduce_fusion
  (112 shorter events, 8.1 us)
Async XLA Ops:
  7.2 100.1 %all-gather.2.cloned.1.call-start = ((), (), s32[]{:S(2)}) async-start(), calls=%async_computation | async-start | bytes 25362432 | tf_op jit(solution)/shard_map/all_gather | solution.py:577
  8.6 1.9 copy-start.21
  10.6 0.7 copy-start.23
  11.3 3.7 %copy-start.14 = (s32[256]{0:T(256)}, s32[256]{0:T(256)S(1)}, u32[]{:S(2)}) copy-start(s32[256]{0:T(256)S(1)} %convert_reduce_fusion) | copy-start | bytes 3076
  18.0 6.1 %copy-start.22 = (s32[4]{0:T(128)S(1)}, s32[4]{0:T(128)}, u32[]{:S(2)}) copy-start(s32[4]{0:T(128)} %param.16) | copy-start | bytes 52
  18.0 6.1 %copy-start.24 = (s32[4,1]{0,1:T(1,128)S(1)}, s32[4,1]{0,1:T(1,128)}, u32[]{:S(2)}) copy-start(s32[4,1]{0,1:T(1,128)} %copy-done.23) | copy-start | bytes 52
  18.0 6.1 %copy-start.15 = (s32[256]{0:T(256)S(1)}, s32[256]{0:T(256)}, u32[]{:S(2)}) copy-start(s32[256]{0:T(256)} %copy-done.14) | copy-start | bytes 3076
  136.7 14.0 %collective-permute-start = (bf16[512,2688]{1,0:T(8,128)(2,1)}, bf16[512,2688]{1,0:T(8,128)(2,1)}, u32[]{:S(2)}, u32[]{:S(2)}) collective-permute-start(bf16[512,2688]{1,0:T(8,128)(2,1)} %get-tuple-element.69), channel_id=1, source_target_pairs={{0,1},{1,0},{2,3},{3,2},{4,5},{5,4},{6,7},{7,6},{8,9},{9,8},{10,11... | collective-permute-start | bytes 8257544 | tf_op jit(solution)/shard_map/ppermute | solution.py:427
  137.0 13.6 %copy-start.1 = (bf16[512,2688]{1,0:T(8,128)(2,1)S(1)}, bf16[512,2688]{1,0:T(8,128)(2,1)}, u32[]{:S(2)}) copy-start(bf16[512,2688]{1,0:T(8,128)(2,1)} %get-tuple-element.68.refs_14_) | copy-start | bytes 8257540
  150.3 18.8 %collective-permute-start.1 = (bf16[512,2688]{1,0:T(8,128)(2,1)}, bf16[512,2688]{1,0:T(8,128)(2,1)}, u32[]{:S(2)}, u32[]{:S(2)}) collective-permute-start(bf16[512,2688]{1,0:T(8,128)(2,1)} %get-tuple-element.76), channel_id=1, source_target_pairs={{0,1},{1,0},{2,3},{3,2},{4,5},{5,4},{6,7},{7,6},{8,9},{9,8},{10,11... | collective-permute-start | bytes 8257544 | tf_op jit(solution)/shard_map/ppermute | solution.py:427
  153.4 35.2 %collective-permute-start.3 = (bf16[256,2688]{1,0:T(8,128)(2,1)}, bf16[256,2688]{1,0:T(8,128)(2,1)}, u32[]{:S(2)}, u32[]{:S(2)}) collective-permute-start(bf16[256,2688]{1,0:T(8,128)(2,1)} %add_convert_fusion.2.refs_7_), channel_id=1, source_target_pairs={{0,2},{1,7},{2,0},{3,5},{4,6},{5,3},{6,4},{7,1},{8,10},{9,15},{10,... | collective-permute-start | bytes 4128776 | tf_op jit(solution)/shard_map/ppermute | solution.py:423
  167.8 24.4 %collective-permute-start.2 = (bf16[512,2688]{1,0:T(8,128)(2,1)}, bf16[512,2688]{1,0:T(8,128)(2,1)}, u32[]{:S(2)}, u32[]{:S(2)}) collective-permute-start(bf16[512,2688]{1,0:T(8,128)(2,1)} %get-tuple-element.85), channel_id=1, source_target_pairs={{0,1},{1,0},{2,3},{3,2},{4,5},{5,4},{6,7},{7,6},{8,9},{9,8},{10,11... | collective-permute-start | bytes 8257544 | tf_op jit(solution)/shard_map/ppermute | solution.py:427
  172.3 41.4 %collective-permute-start.12 = (bf16[256,2688]{1,0:T(8,128)(2,1)}, bf16[256,2688]{1,0:T(8,128)(2,1)}, u32[]{:S(2)}, u32[]{:S(2)}) collective-permute-start(bf16[256,2688]{1,0:T(8,128)(2,1)} %add_convert_fusion.1.refs_11_), channel_id=1, source_target_pairs={{0,32},{1,97},{32,0},{33,65},{64,96},{65,33},{96,64},{97,1},{2,34}... | collective-permute-start | bytes 4128776 | tf_op jit(solution)/shard_map/ppermute | solution.py:423
  188.6 3.7 %copy-start = (bf16[512,2688]{1,0:T(8,128)(2,1)S(1)}, bf16[512,2688]{1,0:T(8,128)(2,1)}, u32[]{:S(2)}) copy-start(bf16[512,2688]{1,0:T(8,128)(2,1)} %get-tuple-element.84.refs_0_) | copy-start | bytes 8257540
  191.4 56.1 %collective-permute-start.4 = (bf16[128,2688]{1,0:T(8,128)(2,1)}, bf16[128,2688]{1,0:T(8,128)(2,1)}, u32[]{:S(2)}, u32[]{:S(2)}) collective-permute-start(bf16[128,2688]{1,0:T(8,128)(2,1)} %add_convert_fusion.8.refs_13_), channel_id=1, source_target_pairs={{0,6},{1,3},{2,4},{3,1},{4,2},{5,7},{6,0},{7,5},{8,14},{9,11},{10,... | collective-permute-start | bytes 2064392 | tf_op jit(solution)/shard_map/ppermute | solution.py:423
  195.1 22.6 %collective-permute-start.21 = (bf16[256,2688]{1,0:T(8,128)(2,1)}, bf16[256,2688]{1,0:T(8,128)(2,1)}, u32[]{:S(2)}, u32[]{:S(2)}) collective-permute-start(bf16[256,2688]{1,0:T(8,128)(2,1)} %add_convert_fusion.refs_12_), channel_id=1, source_target_pairs={{0,8},{1,25},{8,0},{9,17},{16,24},{17,9},{24,16},{25,1},{2,10},{3,... | collective-permute-start | bytes 4128776 | tf_op jit(solution)/shard_map/ppermute | solution.py:423
  212.2 5.6 %copy-start.16 = (bf16[512,1408]{1,0:T(8,128)(2,1)S(1)}, bf16[512,1408]{1,0:T(8,128)(2,1)}, u32[]{:S(2)}) copy-start(bf16[512,1408]{1,0:T(8,128)(2,1)} %get-tuple-element.98) | copy-start | bytes 4325380
  212.2 8.2 %collective-permute-start.5 = (bf16[512,1408]{1,0:T(8,128)(2,1)}, bf16[512,1408]{1,0:T(8,128)(2,1)S(1)}, u32[]{:S(2)}, u32[]{:S(2)}) collective-permute-start(bf16[512,1408]{1,0:T(8,128)(2,1)} %get-tuple-element.89), channel_id=1, source_target_pairs={{0,1},{1,0},{2,3},{3,2},{4,5},{5,4},{6,7},{7,6},{8,9},{9,8},{10,11... | collective-permute-start | bytes 4325384 | tf_op jit(solution)/shard_map/ppermute | solution.py:427
  213.7 9.2 %collective-permute-start.14 = (bf16[512,1408]{1,0:T(8,128)(2,1)}, bf16[512,1408]{1,0:T(8,128)(2,1)S(1)}, u32[]{:S(2)}, u32[]{:S(2)}) collective-permute-start(bf16[512,1408]{1,0:T(8,128)(2,1)} %get-tuple-element.94), channel_id=1, source_target_pairs={{0,1},{1,0},{2,3},{3,2},{4,5},{5,4},{6,7},{7,6},{8,9},{9,8},{10,11... | collective-permute-start | bytes 4325384 | tf_op jit(solution)/shard_map/ppermute | solution.py:427
  216.4 6.2 %copy-start.5 = (bf16[512,1408]{1,0:T(8,128)(2,1)S(1)}, bf16[512,1408]{1,0:T(8,128)(2,1)}, u32[]{:S(2)}) copy-start(bf16[512,1408]{1,0:T(8,128)(2,1)} %get-tuple-element.88.refs_4_) | copy-start | bytes 4325380
  216.4 37.2 %collective-permute-start.13 = (bf16[128,2688]{1,0:T(8,128)(2,1)}, bf16[128,2688]{1,0:T(8,128)(2,1)}, u32[]{:S(2)}, u32[]{:S(2)}) collective-permute-start(bf16[128,2688]{1,0:T(8,128)(2,1)} %add_convert_fusion.7), channel_id=1, source_target_pairs={{0,96},{1,33},{32,64},{33,1},{64,32},{65,97},{96,0},{97,65},{2,98}... | collective-permute-start | bytes 2064392 | tf_op jit(solution)/shard_map/ppermute | solution.py:423
  217.7 5.4 %collective-permute-start.23 = (bf16[512,1408]{1,0:T(8,128)(2,1)S(1)}, bf16[512,1408]{1,0:T(8,128)(2,1)S(1)}, u32[]{:S(2)}, u32[]{:S(2)}) collective-permute-start(bf16[512,1408]{1,0:T(8,128)(2,1)S(1)} %copy-done.16), channel_id=1, source_target_pairs={{0,1},{1,0},{2,3},{3,2},{4,5},{5,4},{6,7},{7,6},{8,9},{9,8},{10,11... | collective-permute-start | bytes 4325384 | tf_op jit(solution)/shard_map/ppermute | solution.py:427
  220.3 2.6 copy-start.3
  220.3 14.5 %copy-start.7 = (bf16[512,1408]{1,0:T(8,128)(2,1)}, bf16[512,1408]{1,0:T(8,128)(2,1)S(1)}, u32[]{:S(2)}) copy-start(bf16[512,1408]{1,0:T(8,128)(2,1)S(1)} %collective-permute-done.5.refs_5_) | copy-start | bytes 4325380
  220.4 38.2 %collective-permute-start.22 = (bf16[128,2688]{1,0:T(8,128)(2,1)}, bf16[128,2688]{1,0:T(8,128)(2,1)}, u32[]{:S(2)}, u32[]{:S(2)}) collective-permute-start(bf16[128,2688]{1,0:T(8,128)(2,1)} %add_convert_fusion.6), channel_id=1, source_target_pairs={{0,24},{1,9},{8,16},{9,1},{16,8},{17,25},{24,0},{25,17},{2,26},{3,... | collective-permute-start | bytes 2064392 | tf_op jit(solution)/shard_map/ppermute | solution.py:423
  222.8 2.4 copy-start.2
  222.8 13.4 %copy-start.6 = (bf16[512,1408]{1,0:T(8,128)(2,1)}, bf16[512,1408]{1,0:T(8,128)(2,1)S(1)}, u32[]{:S(2)}) copy-start(bf16[512,1408]{1,0:T(8,128)(2,1)S(1)} %collective-permute-done.14.refs_5_) | copy-start | bytes 4325380
  222.8 11.4 %collective-permute-start.6 = (bf16[256,1408]{1,0:T(8,128)(2,1)S(1)}, bf16[256,1408]{1,0:T(8,128)(2,1)S(1)}, u32[]{:S(2)}, u32[]{:S(2)}) collective-permute-start(bf16[256,1408]{1,0:T(8,128)(2,1)S(1)} %add_convert_fusion.5), channel_id=1, source_target_pairs={{0,2},{1,7},{2,0},{3,5},{4,6},{5,3},{6,4},{7,1},{8,10},{9,15},{10,... | collective-permute-start | bytes 2162696 | tf_op jit(solution)/shard_map/ppermute | solution.py:423
  223.2 23.4 %copy-start.4 = (bf16[512,1408]{1,0:T(8,128)(2,1)}, bf16[512,1408]{1,0:T(8,128)(2,1)S(1)}, u32[]{:S(2)}) copy-start(bf16[512,1408]{1,0:T(8,128)(2,1)S(1)} %collective-permute-done.23.refs_5_) | copy-start | bytes 4325380
  223.2 11.8 %collective-permute-start.15 = (bf16[256,1408]{1,0:T(8,128)(2,1)S(1)}, bf16[256,1408]{1,0:T(8,128)(2,1)S(1)}, u32[]{:S(2)}, u32[]{:S(2)}) collective-permute-start(bf16[256,1408]{1,0:T(8,128)(2,1)S(1)} %add_convert_fusion.4), channel_id=1, source_target_pairs={{0,32},{1,97},{32,0},{33,65},{64,96},{65,33},{96,64},{97,1},{2,34}... | collective-permute-start | bytes 2162696 | tf_op jit(solution)/shard_map/ppermute | solution.py:423
  234.2 2.9 copy-start.13
  234.2 11.3 %collective-permute-start.24 = (bf16[256,1408]{1,0:T(8,128)(2,1)S(1)}, bf16[256,1408]{1,0:T(8,128)(2,1)S(1)}, u32[]{:S(2)}, u32[]{:S(2)}) collective-permute-start(bf16[256,1408]{1,0:T(8,128)(2,1)S(1)} %add_convert_fusion.3), channel_id=1, source_target_pairs={{0,8},{1,25},{8,0},{9,17},{16,24},{17,9},{24,16},{25,1},{2,10},{3,... | collective-permute-start | bytes 2162696 | tf_op jit(solution)/shard_map/ppermute | solution.py:423
  235.0 12.5 %copy-start.12 = (bf16[256,1408]{1,0:T(8,128)(2,1)}, bf16[256,1408]{1,0:T(8,128)(2,1)S(1)}, u32[]{:S(2)}) copy-start(bf16[256,1408]{1,0:T(8,128)(2,1)S(1)} %collective-permute-done.15.refs_7_) | copy-start | bytes 2162692
  235.0 14.3 %collective-permute-start.7 = (bf16[128,1408]{1,0:T(8,128)(2,1)S(1)}, bf16[128,1408]{1,0:T(8,128)(2,1)S(1)}, u32[]{:S(2)}, u32[]{:S(2)}) collective-permute-start(bf16[128,1408]{1,0:T(8,128)(2,1)S(1)} %add_convert_fusion.14), channel_id=1, source_target_pairs={{0,6},{1,3},{2,4},{3,1},{4,2},{5,7},{6,0},{7,5},{8,14},{9,11},{10,... | collective-permute-start | bytes 1081352 | tf_op jit(solution)/shard_map/ppermute | solution.py:423
  245.5 3.9 %copy-start.11 = (bf16[256,1408]{1,0:T(8,128)(2,1)}, bf16[256,1408]{1,0:T(8,128)(2,1)S(1)}, u32[]{:S(2)}) copy-start(bf16[256,1408]{1,0:T(8,128)(2,1)S(1)} %collective-permute-done.24.refs_7_) | copy-start | bytes 2162692
  245.5 9.0 %collective-permute-start.16 = (bf16[128,1408]{1,0:T(8,128)(2,1)}, bf16[128,1408]{1,0:T(8,128)(2,1)}, u32[]{:S(2)}, u32[]{:S(2)}) collective-permute-start(bf16[128,1408]{1,0:T(8,128)(2,1)} %add_convert_fusion.13), channel_id=1, source_target_pairs={{0,96},{1,33},{32,64},{33,1},{64,32},{65,97},{96,0},{97,65},{2,98}... | collective-permute-start | bytes 1081352 | tf_op jit(solution)/shard_map/ppermute | solution.py:423
  247.5 11.0 %collective-permute-start.25 = (bf16[128,1408]{1,0:T(8,128)(2,1)}, bf16[128,1408]{1,0:T(8,128)(2,1)}, u32[]{:S(2)}, u32[]{:S(2)}) collective-permute-start(bf16[128,1408]{1,0:T(8,128)(2,1)} %add_convert_fusion.12), channel_id=1, source_target_pairs={{0,24},{1,9},{8,16},{9,1},{16,8},{17,25},{24,0},{25,17},{2,26},{3,... | collective-permute-start | bytes 1081352 | tf_op jit(solution)/shard_map/ppermute | solution.py:423
  249.3 0.7 copy-start.17
  253.6 9.5 %collective-permute-start.8 = (bf16[64,4096]{1,0:T(8,128)(2,1)}, bf16[64,4096]{1,0:T(8,128)(2,1)}, u32[]{:S(2)}, u32[]{:S(2)}) collective-permute-start(bf16[64,4096]{1,0:T(8,128)(2,1)} %get-tuple-element.90), channel_id=1, source_target_pairs={{0,32},{1,97},{32,0},{33,65},{64,96},{65,33},{96,64},{97,1},{2,34}... | collective-permute-start | bytes 1572872 | tf_op jit(solution)/shard_map/ppermute | solution.py:423
  257.9 9.5 %collective-permute-start.17 = (bf16[64,4096]{1,0:T(8,128)(2,1)}, bf16[64,4096]{1,0:T(8,128)(2,1)}, u32[]{:S(2)}, u32[]{:S(2)}) collective-permute-start(bf16[64,4096]{1,0:T(8,128)(2,1)} %get-tuple-element.95), channel_id=1, source_target_pairs={{0,8},{1,25},{8,0},{9,17},{16,24},{17,9},{24,16},{25,1},{2,10},{3,... | collective-permute-start | bytes 1572872 | tf_op jit(solution)/shard_map/ppermute | solution.py:423
  258.6 4.5 %copy-start.8 = (bf16[64,4096]{1,0:T(8,128)(2,1)S(1)}, bf16[64,4096]{1,0:T(8,128)(2,1)}, u32[]{:S(2)}) copy-start(bf16[64,4096]{1,0:T(8,128)(2,1)} %get-tuple-element.91) | copy-start | bytes 1572868
  262.1 5.3 %copy-start.9 = (bf16[64,4096]{1,0:T(8,128)(2,1)S(1)}, bf16[64,4096]{1,0:T(8,128)(2,1)}, u32[]{:S(2)}) copy-start(bf16[64,4096]{1,0:T(8,128)(2,1)} %get-tuple-element.96) | copy-start | bytes 1572868
  262.1 9.4 %collective-permute-start.26 = (bf16[64,4096]{1,0:T(8,128)(2,1)}, bf16[64,4096]{1,0:T(8,128)(2,1)S(1)}, u32[]{:S(2)}, u32[]{:S(2)}) collective-permute-start(bf16[64,4096]{1,0:T(8,128)(2,1)} %get-tuple-element.99), channel_id=1, source_target_pairs={{0,2},{1,7},{2,0},{3,5},{4,6},{5,3},{6,4},{7,1},{8,10},{9,15},{10,... | collective-permute-start | bytes 1572872 | tf_op jit(solution)/shard_map/ppermute | solution.py:423
  264.3 7.2 %copy-start.10 = (bf16[64,4096]{1,0:T(8,128)(2,1)S(1)}, bf16[64,4096]{1,0:T(8,128)(2,1)}, u32[]{:S(2)}) copy-start(bf16[64,4096]{1,0:T(8,128)(2,1)} %get-tuple-element.100) | copy-start | bytes 1572868
  264.3 8.5 %collective-permute-start.9 = (bf16[32,4096]{1,0:T(8,128)(2,1)S(1)}, bf16[32,4096]{1,0:T(8,128)(2,1)S(1)}, u32[]{:S(2)}, u32[]{:S(2)}) collective-permute-start(bf16[32,4096]{1,0:T(8,128)(2,1)S(1)} %slice.213), channel_id=1, source_target_pairs={{0,96},{1,33},{32,64},{33,1},{64,32},{65,97},{96,0},{97,65},{2,98}... | collective-permute-start | bytes 786440 | tf_op jit(solution)/shard_map/ppermute | solution.py:423
  268.6 9.1 %collective-permute-start.18 = (bf16[32,4096]{1,0:T(8,128)(2,1)S(1)}, bf16[32,4096]{1,0:T(8,128)(2,1)S(1)}, u32[]{:S(2)}, u32[]{:S(2)}) collective-permute-start(bf16[32,4096]{1,0:T(8,128)(2,1)S(1)} %slice.223), channel_id=1, source_target_pairs={{0,24},{1,9},{8,16},{9,1},{16,8},{17,25},{24,0},{25,17},{2,26},{3,... | collective-permute-start | bytes 786440 | tf_op jit(solution)/shard_map/ppermute | solution.py:423
  271.6 8.4 %collective-permute-start.27 = (bf16[32,4096]{1,0:T(8,128)(2,1)S(1)}, bf16[32,4096]{1,0:T(8,128)(2,1)S(1)}, u32[]{:S(2)}, u32[]{:S(2)}) collective-permute-start(bf16[32,4096]{1,0:T(8,128)(2,1)S(1)} %slice.233), channel_id=1, source_target_pairs={{0,6},{1,3},{2,4},{3,1},{4,2},{5,7},{6,0},{7,5},{8,14},{9,11},{10,... | collective-permute-start | bytes 786440 | tf_op jit(solution)/shard_map/ppermute | solution.py:423
  272.9 7.6 %collective-permute-start.10 = (bf16[16,4096]{1,0:T(8,128)(2,1)S(1)}, bf16[16,4096]{1,0:T(8,128)(2,1)S(1)}, u32[]{:S(2)}, u32[]{:S(2)}) collective-permute-start(bf16[16,4096]{1,0:T(8,128)(2,1)S(1)} %slice.215), channel_id=1, source_target_pairs={{0,8},{1,25},{8,0},{9,17},{16,24},{17,9},{24,16},{25,1},{2,10},{3,... | collective-permute-start | bytes 393224 | tf_op jit(solution)/shard_map/ppermute | solution.py:423
  277.7 5.7 %collective-permute-start.19 = (bf16[16,4096]{1,0:T(8,128)(2,1)S(1)}, bf16[16,4096]{1,0:T(8,128)(2,1)S(1)}, u32[]{:S(2)}, u32[]{:S(2)}) collective-permute-start(bf16[16,4096]{1,0:T(8,128)(2,1)S(1)} %slice.225), channel_id=1, source_target_pairs={{0,2},{1,7},{2,0},{3,5},{4,6},{5,3},{6,4},{7,1},{8,10},{9,15},{10,... | collective-permute-start | bytes 393224 | tf_op jit(solution)/shard_map/ppermute | solution.py:423
  280.1 5.5 %collective-permute-start.28 = (bf16[16,4096]{1,0:T(8,128)(2,1)S(1)}, bf16[16,4096]{1,0:T(8,128)(2,1)S(1)}, u32[]{:S(2)}, u32[]{:S(2)}) collective-permute-start(bf16[16,4096]{1,0:T(8,128)(2,1)S(1)} %slice.235), channel_id=1, source_target_pairs={{0,32},{1,97},{32,0},{33,65},{64,96},{65,33},{96,64},{97,1},{2,34}... | collective-permute-start | bytes 393224 | tf_op jit(solution)/shard_map/ppermute | solution.py:423
  281.1 7.7 %collective-permute-start.11 = (bf16[8,4096]{1,0:T(8,128)(2,1)S(1)}, bf16[8,4096]{1,0:T(8,128)(2,1)S(1)}, u32[]{:S(2)}, u32[]{:S(2)}) collective-permute-start(bf16[8,4096]{1,0:T(8,128)(2,1)S(1)} %get-tuple-element.113), channel_id=1, source_target_pairs={{0,24},{1,9},{8,16},{9,1},{16,8},{17,25},{24,0},{25,17},{2,26},{3,... | collective-permute-start | bytes 196616 | tf_op jit(solution)/shard_map/ppermute | solution.py:423
  284.1 5.5 %collective-permute-start.20 = (bf16[8,4096]{1,0:T(8,128)(2,1)S(1)}, bf16[8,4096]{1,0:T(8,128)(2,1)S(1)}, u32[]{:S(2)}, u32[]{:S(2)}) collective-permute-start(bf16[8,4096]{1,0:T(8,128)(2,1)S(1)} %get-tuple-element.111), channel_id=1, source_target_pairs={{0,6},{1,3},{2,4},{3,1},{4,2},{5,7},{6,0},{7,5},{8,14},{9,11},{10,... | collective-permute-start | bytes 196616 | tf_op jit(solution)/shard_map/ppermute | solution.py:423
  286.3 5.5 %collective-permute-start.29 = (bf16[8,4096]{1,0:T(8,128)(2,1)S(1)}, bf16[8,4096]{1,0:T(8,128)(2,1)S(1)}, u32[]{:S(2)}, u32[]{:S(2)}) collective-permute-start(bf16[8,4096]{1,0:T(8,128)(2,1)S(1)} %get-tuple-element.109), channel_id=1, source_target_pairs={{0,96},{1,33},{32,64},{33,1},{64,32},{65,97},{96,0},{97,65},{2,98}... | collective-permute-start | bytes 196616 | tf_op jit(solution)/shard_map/ppermute | solution.py:423
  288.8 3.0 copy-start.18
  289.6 2.1 copy-start.19
  291.8 0.6 copy-start.20
Sparse Core Ops, SparseCore 0:
  11.7 95.5 all-gather.1

commit v4 on v3

--- a/solution.py
+++ b/solution.py
@@ -70,8 +70,8 @@
 
 def attend_kernel(
     tok_ref, seg_ref, segt_ref, cos_ref, sin_ref, w_ref,
-    qkv_ref, prob_ref, res_ref, h1_ref, h2_ref, mixed, gain_ref,
-    wp, wm, wg, packed, bias, sems,
+    qkv_hbm, prob_hbm, res_ref, h1_ref, h2_ref, mixed, gain_ref,
+    wp, wm, wg, packed, bias, qkv, prob, sems, out_sems,
 ):
     copies = [
         pltpu.make_async_copy(w_ref.at[:, pl.ds(GAIN_AT, 128)], wg, sems.at[0]),
@@ -101,9 +101,9 @@
         q = (q * cos + half_swapped(q, low_half) * sin).astype(bf16)
         k = (k * cos + half_swapped(k, low_half) * sin).astype(bf16)
         v = packed[:, pair_slice(p, 2 * D)].astype(bf16)
-        qkv_ref[:, pair_slice(p)] = q
-        qkv_ref[:, pair_slice(p, D)] = k
-        qkv_ref[:, pair_slice(p, 2 * D)] = v
+        qkv[:, pair_slice(p)] = q
+        qkv[:, pair_slice(p, D)] = k
+        qkv[:, pair_slice(p, 2 * D)] = v
         outs = []
         for side in range(2):
             mine = first if side == 0 else jnp.logical_not(first)
@@ -111,17 +111,26 @@
             top = jnp.max(scores, axis=-1, keepdims=True)
             e = jnp.exp(scores - top)
             probs = e * (1.0 / jnp.sum(e, axis=-1, keepdims=True))
-            prob_ref[2 * p + side] = probs
+            prob[2 * p + side] = probs
             outs.append(dot(probs.astype(bf16), v))
         mixed[:, pair_slice(p)] = jnp.where(first, outs[0], outs[1]).astype(bf16)
         return carry
 
-    lax.fori_loop(0, PAIRS, pair, 0)
+    outs = []
+    for i in range(2):
+        lax.fori_loop(i * PAIRS // 2, (i + 1) * PAIRS // 2, pair, 0)
+        part = pl.ds(i * PAIRS, PAIRS)
+        outs.append(pltpu.make_async_copy(prob.at[part], prob_hbm.at[part], out_sems.at[i]))
+        outs[-1].start()
+    outs.append(pltpu.make_async_copy(qkv, qkv_hbm, out_sems.at[2]))
+    outs[-1].start()
     copies[2].wait()
     residual = tokens + dot(mixed[...], wm[...])
     res_ref[...] = residual
     xhat2, _ = norm_parts(residual)
     h2_ref[...] = (xhat2 * gains[1:2]).astype(bf16)
+    for c in outs:
+        c.wait()
 
 
 def started(pairs, sems):
@@ -135,8 +144,8 @@
     if has_sum:
         branch_in, gh2_in = refs[:2]
         refs = refs[2:]
-    branch_ref, gh2_ref, sib_hbm, own_hbm = refs[:4]
-    h2, gt, perm, gtt, w, gate, up, gh, hid, gg, gu, h2t, grads, sems, out_sems = refs[4:]
+    branch_hbm, gh2_hbm, sib_hbm, own_hbm = refs[:4]
+    h2, gt, perm, gtt, w, gate, up, gh, hid, gg, gu, h2t, grads, totals, sems, out_sems = refs[4:]
     base = FF_AT + chunk * 3 * CW
     pieces = [
         (w_hbm.at[:, pl.ds(base + i * CW, CW)], w.at[:, pl.ds(i * CW, CW)]) for i in range(3)
@@ -145,6 +154,14 @@
         [(h2_hbm, h2), pieces[0], pieces[1], (gt_hbm, gt), pieces[2], (perm_hbm, perm), (gtt_hbm, gtt)],
         sems,
     )
+    sums_in = []
+    if has_sum:
+        sums_in = [
+            pltpu.make_async_copy(a, totals.at[i], out_sems.at[i])
+            for i, a in enumerate((branch_in, gh2_in))
+        ]
+        for c in sums_in:
+            c.start()
     copies[0].wait()
     copies[1].wait()
     gate[...] = dot(h2[...], w[:, :CW])
@@ -169,8 +186,19 @@
         return carry
 
     lax.fori_loop(0, gate.shape[0] // size, rows, 0)
+    branch = dot_t(hid[...], w[:, 2 * CW :])
+    gh2 = dot_t(gg[...], w[:, :CW]) + dot_t(gu[...], w[:, CW : 2 * CW])
+    for c in sums_in:
+        c.wait()
+    totals[0] = branch + totals[0] if has_sum else branch
+    totals[1] = gh2 + totals[1] if has_sum else gh2
+    outs = [
+        pltpu.make_async_copy(totals.at[i], to, out_sems.at[i])
+        for i, to in enumerate((branch_hbm, gh2_hbm))
+    ]
+    for c in outs:
+        c.start()
     copies[6].wait()
-    outs = []
     for half, to in enumerate((sib_hbm, own_hbm)):
         rows_at = pl.ds(half * ROWS, ROWS)
         for i, (left, right) in enumerate(((h2t, gg), (h2t, gu), (gtt, hid))):
@@ -178,36 +206,39 @@
             grads[rows_at, cols] = dot(left[rows_at, :], right[...]).astype(bf16)
             outs.append(
                 pltpu.make_async_copy(
-                    grads.at[rows_at, cols], to.at[:, cols], out_sems.at[3 * half + i]
+                    grads.at[rows_at, cols], to.at[:, cols], out_sems.at[2 + 3 * half + i]
                 )
             )
             outs[-1].start()
-    branch = dot_t(hid[...], w[:, 2 * CW :])
-    gh2 = dot_t(gg[...], w[:, :CW]) + dot_t(gu[...], w[:, CW : 2 * CW])
-    if has_sum:
-        branch = branch + branch_in[...]
-        gh2 = gh2 + gh2_in[...]
-    branch_ref[...] = branch
-    gh2_ref[...] = gh2
     for c in outs:
         c.wait()
 
 
-def heads_kernel(
-    gt_ref, seg_ref, gain_ref, res_ref, branch_ref, gh2_ref, cos_ref, sin_ref,
-    qkv_hbm, prob_hbm, w_hbm,
-    out_ref, gr, ga_ref, second_ref, gp,
-    wm, qkv, prob, gm, sems,
+def back_kernel(
+    gain_ref, seg_ref, cos_ref, sin_ref, gt_ref, res_hbm, branch_hbm, gh2_hbm, qkv_hbm, prob_hbm,
+    h1_hbm, mixed_hbm, tok_hbm, perm0, perm1, perm2, w_hbm,
+    out_ref, gin_ref, sib0, sib1, sib2, own0, own1, own2,
+    res_ref, branch_ref, gh2_ref, qkv, prob, h1, mixed, tok, p0, p1, p2, wp, wm,
+    gr, ga_ref, gm, gp, h1t, mt, grads, sems, out_sems,
 ):
+    perms = (p0, p1, p2)
     copies = started(
-        [(w_hbm.at[:, pl.ds(MIX_AT, D)], wm), (qkv_hbm, qkv), (prob_hbm, prob)], sems
-    )
+        [
+            (res_hbm, res_ref), (branch_hbm, branch_ref), (gh2_hbm, gh2_ref),
+            (w_hbm.at[:, pl.ds(MIX_AT, D)], wm), (qkv_hbm, qkv), (prob_hbm, prob),
+            (h1_hbm, h1), (mixed_hbm, mixed), (perm0, p0), (perm1, p1), (perm2, p2),
+            (w_hbm.at[:, pl.ds(0, 3 * D)], wp), (tok_hbm, tok),
+        ],
+        sems,
+    )
+    for c in copies[:3]:
+        c.wait()
     residual = res_ref[...]
     live = seg_ref[...] < 4
     out_ref[...] = jnp.where(live, residual + branch_ref[...], 0.0).astype(bf16)
     xhat2, r2 = norm_parts(residual)
     gh2 = gh2_ref[...]
-    second_ref[...] = jnp.broadcast_to(jnp.sum(gh2 * xhat2, axis=0, keepdims=True), (8, D))
+    second = jnp.sum(gh2 * xhat2, axis=0, keepdims=True)
     n = gh2 * gain_ref[1:2]
     spread = jnp.mean(n * xhat2, axis=-1, keepdims=True)
     grad_res = gt_ref[...].astype(f32) + r2 * (
@@ -216,10 +247,10 @@
     gr[...] = grad_res
     ga = grad_res.astype(bf16)
     ga_ref[...] = ga
-    copies[0].wait()
+    copies[3].wait()
     gm[...] = dot_t(ga, wm[...]).astype(bf16)
-    copies[1].wait()
-    copies[2].wait()
+    copies[4].wait()
+    copies[5].wait()
     low_half = lax.broadcasted_iota(jnp.int32, (1, PAIR), 1) % HD < HD // 2
     first = lax.broadcasted_iota(jnp.int32, (1, PAIR), 1) < HD
     zero = jnp.zeros((), bf16)
@@ -250,36 +281,28 @@
         return carry
 
     lax.fori_loop(0, PAIRS, pair, 0)
-
-
-def back_kernel(
-    h1_ref, mixed_ref, ga, gp, tok_ref, gr, gain_ref, second_ref, perm0, perm1, perm2, w_hbm,
-    gin_ref, sib0, sib1, sib2, own0, own1, own2,
-    p0, p1, p2, wp, h1t, mt, grads, sems, out_sems,
-):
-    perms = (p0, p1, p2)
-    copies = started(
-        [(perm0, p0), (perm1, p1), (perm2, p2), (w_hbm.at[:, pl.ds(0, 3 * D)], wp)], sems
-    )
+    copies[6].wait()
+    copies[7].wait()
     outs = []
     for j in range(CHUNKS):
-        copies[j].wait()
-        h1t[...] = dot_t(perms[j][...], h1_ref[...]).astype(bf16)
-        mt[...] = dot_t(perms[j][...], mixed_ref[...]).astype(bf16)
+        copies[8 + j].wait()
+        h1t[...] = dot_t(perms[j][...], h1[...]).astype(bf16)
+        mt[...] = dot_t(perms[j][...], mixed[...]).astype(bf16)
         lo, hi = MIX_CUTS[j]
         to = grads.at[j]
         to[:, pl.ds(0, D)] = dot(h1t[...], gp[:, j * D : (j + 1) * D]).astype(bf16)
-        to[:, pl.ds(D, hi - lo)] = dot(mt[...], ga[:, lo:hi]).astype(bf16)
+        to[:, pl.ds(D, hi - lo)] = dot(mt[...], ga_ref[:, lo:hi]).astype(bf16)
         if j == CHUNKS - 1:
-            copies[3].wait()
+            copies[11].wait()
+            copies[12].wait()
             gh1 = dot_t(gp[...], wp[...])
-            xhat1, r1 = norm_parts(tok_ref[...].astype(f32))
+            xhat1, r1 = norm_parts(tok[...].astype(f32))
             one = jnp.sum(gh1 * xhat1, axis=0, keepdims=True)
             m = gh1 * gain_ref[0:1]
             spread = jnp.mean(m * xhat1, axis=-1, keepdims=True)
             gin_ref[...] = gr[...] + r1 * (m - jnp.mean(m, axis=-1, keepdims=True) - xhat1 * spread)
             row = lax.broadcasted_iota(jnp.int32, (128, D), 0)
-            both = jnp.where(row == 0, one, jnp.where(row == 1, second_ref[0:1], 0.0)).astype(bf16)
+            both = jnp.where(row == 0, one, jnp.where(row == 1, second, 0.0)).astype(bf16)
             to[:, pl.ds(D + 256, 128)] = dot_t(perms[j][...], both).astype(bf16)
         for half, group in enumerate(((sib0, sib1, sib2), (own0, own1, own2))):
             outs.append(
@@ -292,10 +315,10 @@
         c.wait()
 
 
-def turn_kernel(*refs):
-    send, keep, whole = refs[8:]
+def turn_kernel(ff_terms, *refs):
+    send, keep, whole = refs[ff_terms + 4 :]
     at = 0
-    for terms in (refs[:4], refs[4:8]):
+    for terms in (refs[:ff_terms], refs[ff_terms : ff_terms + 4]):
         total = terms[0][...].astype(f32)
         for t in terms[1:]:
             total = total + t[...].astype(f32)
@@ -330,7 +353,7 @@
         packed[:, pl.ds(j * D, D)] = total[:, ff : ff + D]
         lo, hi = MIX_CUTS[j]
         mixer[:, pl.ds(lo, hi - lo)] = total[:, ff + D : ff + D + hi - lo]
-    gain[...] = total[:, ff + D + 256 :]
+    gain[...] = jnp.transpose(total[:, ff + D + 256 :])[:8]
     reduce[...] = wide[2, :, pl.ds(0, FF)]
     lane = lax.broadcasted_iota(jnp.int32, (1, 2 * FF), 1)
     pad = jnp.zeros((8, 2 * FF - CHUNKS * CW), f32)
@@ -428,7 +451,10 @@
 
 
 def added(*arrays):
-    return sum(a.astype(f32) for a in arrays).astype(bf16)
+    total = arrays[0]
+    for a in arrays[1:]:
+        total = total + a
+    return total
 
 
 class PartSum:
@@ -458,6 +484,11 @@
         got, kept = self.got
         specs = [pl.BlockSpec((128, cols), lambda i, at=at: (at, 0)) for at in (3, 3, 0, 1)]
         return (self.own, self.arrived, got, kept), specs
+
+    def total(self):
+        got, kept = self.got
+        at = slice(self.lo, ROWS)
+        return (added(self.own[at], self.arrived[at], got, kept[ROWS // 4 :]),), [VSPEC]
 
 
 def halves(a):
@@ -482,9 +513,10 @@
         (arr((n, 3 * D), bf16), arr((H, n, n), f32), wide, tile, tile, tile, arr((8, D), f32)),
         [
             vm((D, 3 * D), bf16), vm((D, D), bf16), vm((D, 128), bf16), vm((n, 3 * D), f32),
-            vm((n, n), f32), DMA((3,)),
+            vm((n, n), f32), vm((n, 3 * D), bf16), vm((H, n, n), f32), DMA((3,)), DMA((3,)),
         ],
         in_hbm=(5,),
+        out_hbm=(0, 1),
     )
     sums, ff, after = (), [], ()
     for j in range(CHUNKS):
@@ -496,9 +528,9 @@
             [vm((n, D), bf16), vm((n, D), bf16), vm((D, D), bf16), vm((D, n), bf16), vm((D, 3 * CW), bf16)]
             + [vm((n, CW), f32)] * 3
             + [vm((n, CW), bf16)] * 3
-            + [vm((D, n), bf16), vm((D, 3 * CW), bf16), DMA((7,)), DMA((6,))],
-            in_hbm=(0, 1, 2, 3, 4),
-            out_hbm=(2, 3),
+            + [vm((D, n), bf16), vm((D, 3 * CW), bf16), vm((2, n, D), f32), DMA((7,)), DMA((8,))],
+            in_hbm=range(5 + len(sums)),
+            out_hbm=range(4),
             after=after,
             through=through,
         )
@@ -509,23 +541,20 @@
         if j > 0:
             after = (ff[j - 1].send(),)
     branch, gh2 = sums
-    block_output, gr, ga, second, gp = run(
-        heads_kernel, "heads",
-        (gt, seg_col, gains, residual, branch, gh2, cos, sin, qkv, probs, weights),
-        (tile, wide, tile, arr((8, D), f32), arr((n, 3 * D), bf16)),
-        [vm((D, D), bf16), vm((n, 3 * D), bf16), vm((H, n, n), f32), vm((n, D), bf16), DMA((3,))],
-        in_hbm=(8, 9, 10),
-        after=after,
-    )
-    after = (ff[2].send(), ff[0].send())
-    input_grad, *pieces = run(
-        back_kernel, "back", (h1, mixed, ga, gp, tokens, gr, gains, second, *perms, weights),
-        (wide,) + (arr((ROWS, A_COLS), bf16),) * 6,
-        [vm((D, D), bf16)] * 3
-        + [vm((D, 3 * D), bf16), vm((D, n), bf16), vm((D, n), bf16), vm((3, D, A_COLS), bf16)]
-        + [DMA((4,)), DMA((6,))],
-        in_hbm=(8, 9, 10, 11),
-        out_hbm=(1, 2, 3, 4, 5, 6),
+    after += (ff[2].send(),)
+    block_output, input_grad, *pieces = run(
+        back_kernel, "back",
+        (gains, seg_col, cos, sin, gt, residual, branch, gh2, qkv, probs, h1, mixed, tokens, *perms, weights),
+        (tile, wide) + (arr((ROWS, A_COLS), bf16),) * 6,
+        [vm((n, D), f32)] * 3
+        + [vm((n, 3 * D), bf16), vm((H, n, n), f32)]
+        + [vm((n, D), bf16)] * 3
+        + [vm((D, D), bf16)] * 3
+        + [vm((D, 3 * D), bf16), vm((D, D), bf16), vm((n, D), f32), vm((n, D), bf16), vm((n, D), bf16)]
+        + [vm((n, 3 * D), bf16), vm((D, n), bf16), vm((D, n), bf16), vm((3, D, A_COLS), bf16)]
+        + [DMA((13,)), DMA((6,))],
+        in_hbm=range(5, 17),
+        out_hbm=range(2, 8),
         after=after,
         through=(ff[0].own, ff[1].own),
     )
@@ -535,15 +564,20 @@
 
 
 def summed(ff, att):
-    for part in (ff[1], att[0], ff[2], att[1], att[2], *att):
-        part.send()
+    for f in ff:
+        f.send()
+    for f, a in zip(ff, att):
+        f.own, _ = lax.optimization_barrier((f.own, a.send()))
+    for a in att:
+        a.send()
     pairs = []
     for f, a in zip(ff, att):
-        (f_terms, f_specs), (a_terms, a_specs) = f.last_terms(), a.last_terms()
+        f_terms, f_specs = f.total()
+        a_terms, a_specs = a.last_terms()
         cols = f.own.shape[1] + a.own.shape[1]
         pairs.append(
             run(
-                turn_kernel, "turn", f_terms + a_terms, (arr((64, cols), bf16),) * 2,
+                functools.partial(turn_kernel, len(f_terms)), "turn", f_terms + a_terms, (arr((64, cols), bf16),) * 2,
                 [pltpu.VMEM((128, cols), f32)], specs=f_specs + a_specs,
             )
         )
@@ -559,10 +593,10 @@
     n = 8
     *grads, gains = run(
         finish_kernel, "finish", (*gots, *kept),
-        tuple(arr((n, c), f32) for c in (3 * D, D, 2 * FF, FF, 128)),
+        tuple(arr((n, c), f32) for c in (3 * D, D, 2 * FF, FF, 8)),
         [pltpu.VMEM((3, n, CHUNKS * CW), f32)],
     )
-    return (*grads, gains[:, 0], gains[:, 1])
+    return (*grads, gains[0], gains[1])
 
 
 def body(

time: 308 us -> 300 us (0.974)
  Pallas kernels: 107 us -> 98.8 us
  waiting for transfers between devices: 110 us -> 106 us
    add x0 -> x24, other arithmetic: none -> 23.7 us  [added(): total = total + a]
    convert_element_type x21 -> x0, other arithmetic: 21.9 us -> none  [added(): return sum((a.astype(f32) for a in arrays)).astype(bf16)]
    pallas_call x12 -> x11, Pallas kernels: 107 us -> 98.8 us  [run(): pl.pallas_call(with_order, out_shape=tuple(out_shape) + tuple((arr(t.shap...]
    ppermute x24, waiting for transfers between devices: 30 us -> 25.9 us  [to_partner(): return lax.ppermute(a, (axis, 'c'), pairs)]
  transfers between devices with their start and end apart: 31 -> 31, of which waited for: 13 -> 13; matrix products, arithmetic and copies ran while one was open for 12% -> 12% of each run, Pallas kernels for 24% -> 22%
where the time goes in v4:
time: 300 us; the launch traced here: 294 us
  waiting for transfers between devices  106 us (35%)
  Pallas kernels  98.8 us (33%)
  other arithmetic  34.8 us (12%)
  starting transfers between devices  33.4 us (11%)
  between operations  14.9 us (5%)
  local copies, waits for them, and re-layouts  6.83 us (2%)
    pallas_call x11, Pallas kernels, run(): pl.pallas_call(with_order, out_shape=tuple(out_shape) + tuple((arr(t.shap...  98.8 us
    all_gather x1, waiting for transfers between devices, body(): weights = lax.all_gather(shard, ALL, axis=0, tiled=True)  79.7 us
    ppermute x24, starting transfers between devices, to_partner(): return lax.ppermute(a, (axis, 'c'), pairs)  29.5 us
    ppermute x24, waiting for transfers between devices, to_partner(): return lax.ppermute(a, (axis, 'c'), pairs)  25.9 us
    add x24, other arithmetic, added(): total = total + a  23.7 us
  transfers between devices with their start and end apart: 31, of which 13 were waited for; matrix products, arithmetic and copies ran while one was open for 12% of the time, Pallas kernels for 22%

profile of v4, /device:TPU:0, one launch (start us, length us, event | category | flops | bytes accessed | tf_op | source)
XLA Modules:
  0.0 294.3 jit_solution(8846222900322864448)
XLA Ops:
  7.2 0.7 pad_maximum_fusion.2
  8.6 1.7 pack.1
  11.4 1.8 fusion.refs_2_.refs_13_
  13.2 1.8 fusion.1.refs_3_.refs_2_.refs_14_
  15.0 1.7 fusion.2.refs_4_.refs_2_.refs_15_
  16.7 1.3 add_select_fusion.refs_1_
  18.0 6.0 %cotangent.1 = (bf16[256,1024]{1,0:T(8,128)(2,1)}, bf16[1024,256]{1,0:T(8,128)(2,1)}, bf16[1024,256]{1,0:T(8,128)(2,1)}, bf16[1024,256]{1,0:T(8,128)(2,1)}) custom-call(bf16[256,1024]{1,0:T(8,128)(2,1)} %refs_0_.5, s32[256,1]{1,0:T(8,128)} %add_select_fusion.refs_1_, bf16[1024,1024]{1,0:T(8,128)(2,1)} %fusion.refs_2_.refs_13_, ...), custom_call_target="tpu_custom_call" | custom-call | flops 100000000376832 | bytes 1024 | tf_op jit(solution)/shard_map/cotangent/pallas_call | solution.py:383
  24.2 0.7 fusion.25
  25.4 1.0 pad_maximum_fusion
  26.4 1.2 compare_select_fusion.refs_2_
  27.6 79.7 %all-gather.2.cloned.1.call-done.refs_5_.refs_4_.refs_16_ = bf16[1024,12288]{1,0:T(8,128)(2,1)} async-done(((bf16[8,12288]{1,0:T(8,128)(2,1)}), bf16[1024,12288]{1,0:T(8,128)(2,1)}) %all-gather.2.cloned.1.call-update) | async-done | bytes 25165840 | tf_op jit(solution)/shard_map/all_gather | solution.py:611
  107.3 17.9 %attend.1 = (bf16[256,3072]{1,0:T(8,128)(2,1)}, f32[16,256,256]{2,1,0:T(8,128)}, f32[256,1024]{1,0:T(8,128)}, bf16[256,1024]{1,0:T(8,128)(2,1)}, bf16[256,1024]{...) custom-call(bf16[256,1024]{1,0:T(8,128)(2,1)} %refs_12_.1, s32[256,1]{1,0:T(8,128)} %add_select_fusion.refs_1_, ...), custom_call_target="tpu_custom_call" | custom-call | flops 100000000376832 | bytes 1024 | tf_op jit(solution)/shard_map/attend/pallas_call | solution.py:383
  125.1 11.4 %gated.3 = (f32[256,1024]{1,0:T(8,128)}, f32[256,1024]{1,0:T(8,128)}, bf16[512,2688]{1,0:T(8,128)(2,1)}, bf16[512,2688]{1,0:T(8,128)(2,1)}) custom-call(bf16[256,1024]{1,0:T(8,128)(2,1)} %get-tuple-element.59.refs_0_, bf16[256,1024]{1,0:T(8,128)(2,1)} %get-tuple-element.57.refs_1_.refs_4_, bf16[1024,1024]{1,0:T(8,128)(2,1)} %fusion.refs_2_.refs_13_, ...), custom_call_target="tpu_custom_call" | custom-call | flops 100000000376832 | bytes 1024 | tf_op jit(solution)/shard_map/gated/pallas_call | solution.py:383
  136.8 13.1 %gated.4 = (f32[256,1024]{1,0:T(8,128)}, f32[256,1024]{1,0:T(8,128)}, bf16[512,2688]{1,0:T(8,128)(2,1)}, bf16[512,2688]{1,0:T(8,128)(2,1)}) custom-call(bf16[256,1024]{1,0:T(8,128)(2,1)} %get-tuple-element.59.refs_0_, bf16[256,1024]{1,0:T(8,128)(2,1)} %get-tuple-element.57.refs_1_.refs_4_, bf16[1024,1024]{1,0:T(8,128)(2,1)} %fusion.1.refs_3_.refs_2_.refs_14_, ...), custom_call_target="tpu_custom_call" | custom-call | flops 100000000376832 | bytes 1024 | tf_op jit(solution)/shard_map/gated/pallas_call | solution.py:383
  150.3 2.6 slice_add_fusion.2.refs_7_
  152.9 12.8 %gated.5 = (f32[256,1024]{1,0:T(8,128)}, f32[256,1024]{1,0:T(8,128)}, bf16[512,2688]{1,0:T(8,128)(2,1)}, bf16[512,2688]{1,0:T(8,128)(2,1)}, bf16[512,2688]{1,0:T(8,128)(2,1)}) custom-call(bf16[256,1024]{1,0:T(8,128)(2,1)} %get-tuple-element.59.refs_0_, bf16[256,1024]{1,0:T(8,128)(2,1)} %get-tuple-element.57.refs_1_.refs_4_, ...), custom_call_target="tpu_custom_call", output_to_operand_aliasing={{4}: (8, {})} | custom-call | flops 100000000376832 | bytes 1024 | tf_op jit(solution)/shard_map/gated/pallas_call | solution.py:383
  166.0 1.5 collective-permute-start.4
  167.5 3.0 %slice_add_fusion.1.refs_17_ = bf16[256,2688]{1,0:T(8,128)(2,1)} fusion(bf16[512,2688]{1,0:T(8,128)(2,1)} %collective-permute-done.1, bf16[512,2688]{1,0:T(8,128)(2,1)} %get-tuple-element.76.refs_20_), kind=kLoop, calls=%fused_computation.7 | loop fusion | flops 688128 | bytes 4128768 | tf_op jit(solution)/shard_map/add | solution.py:456
  170.5 1.5 collective-permute-start.13
  172.0 1.4 slice_add_fusion.refs_18_
  174.2 26.3 %back.1 = (bf16[256,1024]{1,0:T(8,128)(2,1)}, f32[256,1024]{1,0:T(8,128)}, bf16[512,1408]{1,0:T(8,128)(2,1)}, bf16[512,1408]{1,0:T(8,128)(2,1)}, bf16[512,1408]{...) custom-call(f32[8,1024]{1,0:T(8,128)} %get-tuple-element.56.refs_0_,, ...), custom_call_target="tpu_custom_call", output_to_operand_aliasing={{8}: (19, {}), {9}: (20, {})} | custom-call | flops 100000000376832 | bytes 1024 | tf_op jit(solution)/shard_map/back/pallas_call | solution.py:383
  200.5 2.7 collective-permute-start.21
  203.3 1.8 slice_add_fusion.11
  205.1 1.8 collective-permute-start.14
  206.9 1.7 slice_add_fusion.15
  208.7 1.3 collective-permute-start.5
  210.0 1.3 slice_add_fusion.7
  211.3 2.4 collective-permute-start.23
  214.5 2.8 collective-permute-done.14
  217.6 2.5 slice_add_fusion.10.refs_0_
  220.1 2.7 collective-permute-done.5
  222.8 2.6 slice_add_fusion.14.refs_0_
  225.4 5.3 %collective-permute-done.23 = bf16[128,2688]{1,0:T(8,128)(2,1)S(1)} collective-permute-done((bf16[128,2688]{1,0:T(8,128)(2,1)S(1)}, bf16[128,2688]{1,0:T(8,128)(2,1)S(1)}, u32[]{:S(2)}, u32[]{:S(2)}) %collective-permute-start.23) | collective-permute-done | bytes 688160 | tf_op jit(solution)/shard_map/ppermute | solution.py:446
  230.7 2.2 slice_add_fusion.6.refs_0_
  233.0 1.8 collective-permute-start.25
  234.8 0.9 slice_add_fusion.20
  235.6 1.6 collective-permute-start.16
  237.2 0.9 slice_add_fusion.22
  238.3 1.3 collective-permute-start.7
  239.6 2.1 collective-permute-done.25.refs_3_
  241.7 0.7 copy-done.19
  242.4 2.6 turn.5
  245.0 2.6 turn.4
  247.7 2.1 collective-permute-done.7.refs_3_
  249.8 2.6 turn.3
  252.4 2.1 collective-permute-done.26
  254.5 1.2 add.435
  255.7 2.1 collective-permute-start.27
  257.9 1.2 add.424
  259.1 2.8 collective-permute-start.18
  261.9 1.5 collective-permute-done.8
  263.6 4.2 %collective-permute-start.9 = (bf16[32,4096]{1,0:T(8,128)(2,1)S(1)}, bf16[32,4096]{1,0:T(8,128)(2,1)S(1)}, u32[]{:S(2)}, u32[]{:S(2)}) collective-permute-start(bf16[32,4096]{1,0:T(8,128)(2,1)S(1)} %slice.251), channel_id=1, source_target_pairs={{0,96},{1,33},{32,64},{33,1},{64,32},{65,97},{96,0},{97,65},{2,98}... | collective-permute-start | bytes 786440 | tf_op jit(solution)/shard_map/ppermute | solution.py:446
  268.2 4.0 %collective-permute-done.9 = bf16[32,4096]{1,0:T(8,128)(2,1)S(1)} collective-permute-done((bf16[32,4096]{1,0:T(8,128)(2,1)S(1)}, bf16[32,4096]{1,0:T(8,128)(2,1)S(1)}, u32[]{:S(2)}, u32[]{:S(2)}) %collective-permute-start.9) | collective-permute-done | bytes 262176 | tf_op jit(solution)/shard_map/ppermute | solution.py:446
  272.3 0.6 collective-permute-done.28
  272.9 0.6 fusion.26
  273.5 2.6 collective-permute-start.29
  276.2 0.6 fusion.27
  277.3 0.6 fusion.28
  277.9 3.2 %collective-permute-start.11 = (bf16[8,4096]{1,0:T(8,128)(2,1)S(1)}, bf16[8,4096]{1,0:T(8,128)(2,1)S(1)}, u32[]{:S(2)}, u32[]{:S(2)}) collective-permute-start(bf16[8,4096]{1,0:T(8,128)(2,1)S(1)} %get-tuple-element.109), channel_id=1, source_target_pairs={{0,24},{1,9},{8,16},{9,1},{16,8},{17,25},{24,0},{25,17},{2,26},{3,... | collective-permute-start | bytes 196616 | tf_op jit(solution)/shard_map/ppermute | solution.py:446
  281.1 1.2 collective-permute-done.20.refs_1_
  282.3 1.0 collective-permute-done.11.refs_0_
  283.4 0.6 copy-done.22
  284.0 1.8 finish.1
  285.8 1.3 slice_bitcast_fusion
  (118 shorter events, 6.7 us)
Async XLA Ops:
  7.2 100.1 %all-gather.2.cloned.1.call-start = ((), (), s32[]{:S(2)}) async-start(), calls=%async_computation | async-start | bytes 25362432 | tf_op jit(solution)/shard_map/all_gather | solution.py:611
  8.6 1.9 copy-start.23
  10.6 0.7 copy-start.25
  11.3 3.7 %copy-start.17 = (s32[256]{0:T(256)}, s32[256]{0:T(256)S(1)}, u32[]{:S(2)}) copy-start(s32[256]{0:T(256)S(1)} %convert_reduce_fusion) | copy-start | bytes 3076
  18.0 6.1 %copy-start.24 = (s32[4]{0:T(128)S(1)}, s32[4]{0:T(128)}, u32[]{:S(2)}) copy-start(s32[4]{0:T(128)} %param.16) | copy-start | bytes 52
  18.0 6.1 %copy-start.26 = (s32[4,1]{0,1:T(1,128)S(1)}, s32[4,1]{0,1:T(1,128)}, u32[]{:S(2)}) copy-start(s32[4,1]{0,1:T(1,128)} %copy-done.25) | copy-start | bytes 52
  18.0 6.1 %copy-start.18 = (s32[256]{0:T(256)S(1)}, s32[256]{0:T(256)}, u32[]{:S(2)}) copy-start(s32[256]{0:T(256)} %copy-done.17) | copy-start | bytes 3076
  136.5 13.8 %collective-permute-start = (bf16[512,2688]{1,0:T(8,128)(2,1)}, bf16[512,2688]{1,0:T(8,128)(2,1)}, u32[]{:S(2)}, u32[]{:S(2)}) collective-permute-start(bf16[512,2688]{1,0:T(8,128)(2,1)} %get-tuple-element.68), channel_id=1, source_target_pairs={{0,1},{1,0},{2,3},{3,2},{4,5},{5,4},{6,7},{7,6},{8,9},{9,8},{10,11... | collective-permute-start | bytes 8257544 | tf_op jit(solution)/shard_map/ppermute | solution.py:450
  136.8 13.5 %copy-start.4 = (bf16[512,2688]{1,0:T(8,128)(2,1)S(1)}, bf16[512,2688]{1,0:T(8,128)(2,1)}, u32[]{:S(2)}) copy-start(bf16[512,2688]{1,0:T(8,128)(2,1)} %get-tuple-element.67.refs_19_) | copy-start | bytes 8257540
  150.0 17.5 %collective-permute-start.1 = (bf16[512,2688]{1,0:T(8,128)(2,1)}, bf16[512,2688]{1,0:T(8,128)(2,1)}, u32[]{:S(2)}, u32[]{:S(2)}) collective-permute-start(bf16[512,2688]{1,0:T(8,128)(2,1)} %get-tuple-element.77), channel_id=1, source_target_pairs={{0,1},{1,0},{2,3},{3,2},{4,5},{5,4},{6,7},{7,6},{8,9},{9,8},{10,11... | collective-permute-start | bytes 8257544 | tf_op jit(solution)/shard_map/ppermute | solution.py:450
  165.7 6.3 %copy-start = (bf16[512,2688]{1,0:T(8,128)(2,1)S(1)}, bf16[512,2688]{1,0:T(8,128)(2,1)}, u32[]{:S(2)}) copy-start(bf16[512,2688]{1,0:T(8,128)(2,1)} %get-tuple-element.96) | copy-start | bytes 8257540
  165.7 6.3 %collective-permute-start.2 = (bf16[512,2688]{1,0:T(8,128)(2,1)}, bf16[512,2688]{1,0:T(8,128)(2,1)S(1)}, u32[]{:S(2)}, u32[]{:S(2)}) collective-permute-start(bf16[512,2688]{1,0:T(8,128)(2,1)} %get-tuple-element.79), channel_id=1, source_target_pairs={{0,1},{1,0},{2,3},{3,2},{4,5},{5,4},{6,7},{7,6},{8,9},{9,8},{10,11... | collective-permute-start | bytes 8257544 | tf_op jit(solution)/shard_map/ppermute | solution.py:450
  166.0 40.9 %collective-permute-start.4 = (bf16[256,2688]{1,0:T(8,128)(2,1)}, bf16[256,2688]{1,0:T(8,128)(2,1)}, u32[]{:S(2)}, u32[]{:S(2)}) collective-permute-start(bf16[256,2688]{1,0:T(8,128)(2,1)} %slice_add_fusion.2.refs_7_), channel_id=1, source_target_pairs={{0,2},{1,7},{2,0},{3,5},{4,6},{5,3},{6,4},{7,1},{8,10},{9,15},{10,... | collective-permute-start | bytes 4128776 | tf_op jit(solution)/shard_map/ppermute | solution.py:446
  170.5 32.8 %collective-permute-start.13 = (bf16[256,2688]{1,0:T(8,128)(2,1)}, bf16[256,2688]{1,0:T(8,128)(2,1)}, u32[]{:S(2)}, u32[]{:S(2)}) collective-permute-start(bf16[256,2688]{1,0:T(8,128)(2,1)} %slice_add_fusion.1.refs_17_), channel_id=1, source_target_pairs={{0,32},{1,97},{32,0},{33,65},{64,96},{65,33},{96,64},{97,1},{2,34}... | collective-permute-start | bytes 4128776 | tf_op jit(solution)/shard_map/ppermute | solution.py:446
  172.0 2.0 copy-start.2
  174.0 34.7 %collective-permute-start.22 = (bf16[256,2688]{1,0:T(8,128)(2,1)}, bf16[256,2688]{1,0:T(8,128)(2,1)}, u32[]{:S(2)}, u32[]{:S(2)}) collective-permute-start(bf16[256,2688]{1,0:T(8,128)(2,1)} %slice_add_fusion.refs_18_), channel_id=1, source_target_pairs={{0,8},{1,25},{8,0},{9,17},{16,24},{17,9},{24,16},{25,1},{2,10},{3,... | collective-permute-start | bytes 4128776 | tf_op jit(solution)/shard_map/ppermute | solution.py:446
  200.5 10.7 %collective-permute-start.21 = (bf16[512,1408]{1,0:T(8,128)(2,1)}, bf16[512,1408]{1,0:T(8,128)(2,1)S(1)}, u32[]{:S(2)}, u32[]{:S(2)}) collective-permute-start(bf16[512,1408]{1,0:T(8,128)(2,1)} %get-tuple-element.95), channel_id=1, source_target_pairs={{0,1},{1,0},{2,3},{3,2},{4,5},{5,4},{6,7},{7,6},{8,9},{9,8},{10,11... | collective-permute-start | bytes 4325384 | tf_op jit(solution)/shard_map/ppermute | solution.py:450
  203.2 10.6 %collective-permute-start.12 = (bf16[512,1408]{1,0:T(8,128)(2,1)}, bf16[512,1408]{1,0:T(8,128)(2,1)S(1)}, u32[]{:S(2)}, u32[]{:S(2)}) collective-permute-start(bf16[512,1408]{1,0:T(8,128)(2,1)} %get-tuple-element.90), channel_id=1, source_target_pairs={{0,1},{1,0},{2,3},{3,2},{4,5},{5,4},{6,7},{7,6},{8,9},{9,8},{10,11... | collective-permute-start | bytes 4325384 | tf_op jit(solution)/shard_map/ppermute | solution.py:450
  203.3 6.7 %copy-start.3 = (bf16[512,2688]{1,0:T(8,128)(2,1)S(1)}, bf16[512,2688]{1,0:T(8,128)(2,1)}, u32[]{:S(2)}) copy-start(bf16[512,2688]{1,0:T(8,128)(2,1)} %copy-done.2) | copy-start | bytes 8257540
  205.1 4.9 %copy-start.1 = (bf16[512,2688]{1,0:T(8,128)(2,1)S(1)}, bf16[512,2688]{1,0:T(8,128)(2,1)}, u32[]{:S(2)}) copy-start(bf16[512,2688]{1,0:T(8,128)(2,1)} %get-tuple-element.96) | copy-start | bytes 8257540
  205.1 12.2 %collective-permute-start.14 = (bf16[128,2688]{1,0:T(8,128)(2,1)S(1)}, bf16[128,2688]{1,0:T(8,128)(2,1)S(1)}, u32[]{:S(2)}, u32[]{:S(2)}) collective-permute-start(bf16[128,2688]{1,0:T(8,128)(2,1)S(1)} %slice_add_fusion.11), channel_id=1, source_target_pairs={{0,96},{1,33},{32,64},{33,1},{64,32},{65,97},{96,0},{97,65},{2,98}... | collective-permute-start | bytes 2064392 | tf_op jit(solution)/shard_map/ppermute | solution.py:446
  206.9 7.1 %collective-permute-start.3 = (bf16[512,1408]{1,0:T(8,128)(2,1)}, bf16[512,1408]{1,0:T(8,128)(2,1)S(1)}, u32[]{:S(2)}, u32[]{:S(2)}) collective-permute-start(bf16[512,1408]{1,0:T(8,128)(2,1)} %get-tuple-element.84), channel_id=1, source_target_pairs={{0,1},{1,0},{2,3},{3,2},{4,5},{5,4},{6,7},{7,6},{8,9},{9,8},{10,11... | collective-permute-start | bytes 4325384 | tf_op jit(solution)/shard_map/ppermute | solution.py:450
  206.9 6.8 %copy-start.7 = (bf16[512,1408]{1,0:T(8,128)(2,1)S(1)}, bf16[512,1408]{1,0:T(8,128)(2,1)}, u32[]{:S(2)}) copy-start(bf16[512,1408]{1,0:T(8,128)(2,1)} %get-tuple-element.94.refs_1_) | copy-start | bytes 4325380
  208.7 5.2 %copy-start.6 = (bf16[512,1408]{1,0:T(8,128)(2,1)S(1)}, bf16[512,1408]{1,0:T(8,128)(2,1)}, u32[]{:S(2)}) copy-start(bf16[512,1408]{1,0:T(8,128)(2,1)} %get-tuple-element.89.refs_1_) | copy-start | bytes 4325380
  208.7 14.1 %collective-permute-start.5 = (bf16[128,2688]{1,0:T(8,128)(2,1)S(1)}, bf16[128,2688]{1,0:T(8,128)(2,1)S(1)}, u32[]{:S(2)}, u32[]{:S(2)}) collective-permute-start(bf16[128,2688]{1,0:T(8,128)(2,1)S(1)} %slice_add_fusion.15), channel_id=1, source_target_pairs={{0,6},{1,3},{2,4},{3,1},{4,2},{5,7},{6,0},{7,5},{8,14},{9,11},{10,... | collective-permute-start | bytes 2064392 | tf_op jit(solution)/shard_map/ppermute | solution.py:446
  211.2 3.2 %copy-start.5 = (bf16[512,1408]{1,0:T(8,128)(2,1)S(1)}, bf16[512,1408]{1,0:T(8,128)(2,1)}, u32[]{:S(2)}) copy-start(bf16[512,1408]{1,0:T(8,128)(2,1)} %get-tuple-element.83.refs_1_) | copy-start | bytes 4325380
  211.3 21.6 %copy-start.10 = (bf16[512,1408]{1,0:T(8,128)(2,1)}, bf16[512,1408]{1,0:T(8,128)(2,1)S(1)}, u32[]{:S(2)}) copy-start(bf16[512,1408]{1,0:T(8,128)(2,1)S(1)} %collective-permute-done.21.refs_2_) | copy-start | bytes 4325380
  211.3 19.5 %collective-permute-start.23 = (bf16[128,2688]{1,0:T(8,128)(2,1)S(1)}, bf16[128,2688]{1,0:T(8,128)(2,1)S(1)}, u32[]{:S(2)}, u32[]{:S(2)}) collective-permute-start(bf16[128,2688]{1,0:T(8,128)(2,1)S(1)} %slice_add_fusion.7), channel_id=1, source_target_pairs={{0,24},{1,9},{8,16},{9,1},{16,8},{17,25},{24,0},{25,17},{2,26},{3,... | collective-permute-start | bytes 2064392 | tf_op jit(solution)/shard_map/ppermute | solution.py:446
  213.8 21.0 %copy-start.8 = (bf16[512,1408]{1,0:T(8,128)(2,1)}, bf16[512,1408]{1,0:T(8,128)(2,1)S(1)}, u32[]{:S(2)}) copy-start(bf16[512,1408]{1,0:T(8,128)(2,1)S(1)} %collective-permute-done.12.refs_2_) | copy-start | bytes 4325380
  213.8 19.1 %collective-permute-start.24 = (bf16[256,1408]{1,0:T(8,128)(2,1)S(1)}, bf16[256,1408]{1,0:T(8,128)(2,1)S(1)}, u32[]{:S(2)}, u32[]{:S(2)}) collective-permute-start(bf16[256,1408]{1,0:T(8,128)(2,1)S(1)} %slice_add_fusion.3), channel_id=1, source_target_pairs={{0,8},{1,25},{8,0},{9,17},{16,24},{17,9},{24,16},{25,1},{2,10},{3,... | collective-permute-start | bytes 2162696 | tf_op jit(solution)/shard_map/ppermute | solution.py:446
  214.0 23.2 %copy-start.9 = (bf16[512,1408]{1,0:T(8,128)(2,1)}, bf16[512,1408]{1,0:T(8,128)(2,1)S(1)}, u32[]{:S(2)}) copy-start(bf16[512,1408]{1,0:T(8,128)(2,1)S(1)} %collective-permute-done.3.refs_2_) | copy-start | bytes 4325380
  214.0 20.7 %collective-permute-start.15 = (bf16[256,1408]{1,0:T(8,128)(2,1)S(1)}, bf16[256,1408]{1,0:T(8,128)(2,1)S(1)}, u32[]{:S(2)}, u32[]{:S(2)}) collective-permute-start(bf16[256,1408]{1,0:T(8,128)(2,1)S(1)} %slice_add_fusion.4), channel_id=1, source_target_pairs={{0,32},{1,97},{32,0},{33,65},{64,96},{65,33},{96,64},{97,1},{2,34}... | collective-permute-start | bytes 2162696 | tf_op jit(solution)/shard_map/ppermute | solution.py:446
  217.3 19.9 %collective-permute-start.6 = (bf16[256,1408]{1,0:T(8,128)(2,1)S(1)}, bf16[256,1408]{1,0:T(8,128)(2,1)S(1)}, u32[]{:S(2)}, u32[]{:S(2)}) collective-permute-start(bf16[256,1408]{1,0:T(8,128)(2,1)S(1)} %slice_add_fusion.5), channel_id=1, source_target_pairs={{0,2},{1,7},{2,0},{3,5},{4,6},{5,3},{6,4},{7,1},{8,10},{9,15},{10,... | collective-permute-start | bytes 2162696 | tf_op jit(solution)/shard_map/ppermute | solution.py:446
  232.9 5.2 %copy-start.16 = (bf16[256,1408]{1,0:T(8,128)(2,1)}, bf16[256,1408]{1,0:T(8,128)(2,1)S(1)}, u32[]{:S(2)}) copy-start(bf16[256,1408]{1,0:T(8,128)(2,1)S(1)} %collective-permute-done.24.refs_4_) | copy-start | bytes 2162692
  233.0 8.7 %collective-permute-start.25 = (bf16[128,1408]{1,0:T(8,128)(2,1)S(1)}, bf16[128,1408]{1,0:T(8,128)(2,1)S(1)}, u32[]{:S(2)}, u32[]{:S(2)}) collective-permute-start(bf16[128,1408]{1,0:T(8,128)(2,1)S(1)} %slice_add_fusion.18), channel_id=1, source_target_pairs={{0,24},{1,9},{8,16},{9,1},{16,8},{17,25},{24,0},{25,17},{2,26},{3,... | collective-permute-start | bytes 1081352 | tf_op jit(solution)/shard_map/ppermute | solution.py:446
  234.8 4.8 %copy-start.15 = (bf16[256,1408]{1,0:T(8,128)(2,1)}, bf16[256,1408]{1,0:T(8,128)(2,1)S(1)}, u32[]{:S(2)}) copy-start(bf16[256,1408]{1,0:T(8,128)(2,1)S(1)} %collective-permute-done.15.refs_4_) | copy-start | bytes 2162692
  235.6 9.4 %collective-permute-start.16 = (bf16[128,1408]{1,0:T(8,128)(2,1)}, bf16[128,1408]{1,0:T(8,128)(2,1)}, u32[]{:S(2)}, u32[]{:S(2)}) collective-permute-start(bf16[128,1408]{1,0:T(8,128)(2,1)} %slice_add_fusion.20), channel_id=1, source_target_pairs={{0,96},{1,33},{32,64},{33,1},{64,32},{65,97},{96,0},{97,65},{2,98}... | collective-permute-start | bytes 1081352 | tf_op jit(solution)/shard_map/ppermute | solution.py:446
  237.2 1.1 copy-start.14
  238.3 11.5 %collective-permute-start.7 = (bf16[128,1408]{1,0:T(8,128)(2,1)}, bf16[128,1408]{1,0:T(8,128)(2,1)}, u32[]{:S(2)}, u32[]{:S(2)}) collective-permute-start(bf16[128,1408]{1,0:T(8,128)(2,1)} %slice_add_fusion.22), channel_id=1, source_target_pairs={{0,6},{1,3},{2,4},{3,1},{4,2},{5,7},{6,0},{7,5},{8,14},{9,11},{10,... | collective-permute-start | bytes 1081352 | tf_op jit(solution)/shard_map/ppermute | solution.py:446
  241.7 0.7 copy-start.19
  245.0 9.5 %collective-permute-start.26 = (bf16[64,4096]{1,0:T(8,128)(2,1)}, bf16[64,4096]{1,0:T(8,128)(2,1)}, u32[]{:S(2)}, u32[]{:S(2)}) collective-permute-start(bf16[64,4096]{1,0:T(8,128)(2,1)} %get-tuple-element.97), channel_id=1, source_target_pairs={{0,2},{1,7},{2,0},{3,5},{4,6},{5,3},{6,4},{7,1},{8,10},{9,15},{10,... | collective-permute-start | bytes 1572872 | tf_op jit(solution)/shard_map/ppermute | solution.py:446
  247.7 10.2 %collective-permute-start.17 = (bf16[64,4096]{1,0:T(8,128)(2,1)}, bf16[64,4096]{1,0:T(8,128)(2,1)}, u32[]{:S(2)}, u32[]{:S(2)}) collective-permute-start(bf16[64,4096]{1,0:T(8,128)(2,1)} %get-tuple-element.92), channel_id=1, source_target_pairs={{0,8},{1,25},{8,0},{9,17},{16,24},{17,9},{24,16},{25,1},{2,10},{3,... | collective-permute-start | bytes 1572872 | tf_op jit(solution)/shard_map/ppermute | solution.py:446
  249.8 4.7 %copy-start.11 = (bf16[64,4096]{1,0:T(8,128)(2,1)S(1)}, bf16[64,4096]{1,0:T(8,128)(2,1)}, u32[]{:S(2)}) copy-start(bf16[64,4096]{1,0:T(8,128)(2,1)} %get-tuple-element.98) | copy-start | bytes 1572868
  252.4 5.5 %copy-start.12 = (bf16[64,4096]{1,0:T(8,128)(2,1)S(1)}, bf16[64,4096]{1,0:T(8,128)(2,1)}, u32[]{:S(2)}) copy-start(bf16[64,4096]{1,0:T(8,128)(2,1)} %get-tuple-element.93) | copy-start | bytes 1572868
  252.4 11.0 %copy-start.13 = (bf16[64,4096]{1,0:T(8,128)(2,1)S(1)}, bf16[64,4096]{1,0:T(8,128)(2,1)}, u32[]{:S(2)}) copy-start(bf16[64,4096]{1,0:T(8,128)(2,1)} %get-tuple-element.87) | copy-start | bytes 1572868
  252.4 11.0 %collective-permute-start.8 = (bf16[64,4096]{1,0:T(8,128)(2,1)}, bf16[64,4096]{1,0:T(8,128)(2,1)S(1)}, u32[]{:S(2)}, u32[]{:S(2)}) collective-permute-start(bf16[64,4096]{1,0:T(8,128)(2,1)} %get-tuple-element.86), channel_id=1, source_target_pairs={{0,32},{1,97},{32,0},{33,65},{64,96},{65,33},{96,64},{97,1},{2,34}... | collective-permute-start | bytes 1572872 | tf_op jit(solution)/shard_map/ppermute | solution.py:446
  255.7 12.1 %collective-permute-start.27 = (bf16[32,4096]{1,0:T(8,128)(2,1)S(1)}, bf16[32,4096]{1,0:T(8,128)(2,1)S(1)}, u32[]{:S(2)}, u32[]{:S(2)}) collective-permute-start(bf16[32,4096]{1,0:T(8,128)(2,1)S(1)} %slice.275), channel_id=1, source_target_pairs={{0,6},{1,3},{2,4},{3,1},{4,2},{5,7},{6,0},{7,5},{8,14},{9,11},{10,... | collective-permute-start | bytes 786440 | tf_op jit(solution)/shard_map/ppermute | solution.py:446
  259.1 8.9 %collective-permute-start.18 = (bf16[32,4096]{1,0:T(8,128)(2,1)S(1)}, bf16[32,4096]{1,0:T(8,128)(2,1)S(1)}, u32[]{:S(2)}, u32[]{:S(2)}) collective-permute-start(bf16[32,4096]{1,0:T(8,128)(2,1)S(1)} %slice.263), channel_id=1, source_target_pairs={{0,24},{1,9},{8,16},{9,1},{16,8},{17,25},{24,0},{25,17},{2,26},{3,... | collective-permute-start | bytes 786440 | tf_op jit(solution)/shard_map/ppermute | solution.py:446
  263.6 8.6 %collective-permute-start.9 = (bf16[32,4096]{1,0:T(8,128)(2,1)S(1)}, bf16[32,4096]{1,0:T(8,128)(2,1)S(1)}, u32[]{:S(2)}, u32[]{:S(2)}) collective-permute-start(bf16[32,4096]{1,0:T(8,128)(2,1)S(1)} %slice.251), channel_id=1, source_target_pairs={{0,96},{1,33},{32,64},{33,1},{64,32},{65,97},{96,0},{97,65},{2,98}... | collective-permute-start | bytes 786440 | tf_op jit(solution)/shard_map/ppermute | solution.py:446
  267.8 5.0 %collective-permute-start.28 = (bf16[16,4096]{1,0:T(8,128)(2,1)S(1)}, bf16[16,4096]{1,0:T(8,128)(2,1)S(1)}, u32[]{:S(2)}, u32[]{:S(2)}) collective-permute-start(bf16[16,4096]{1,0:T(8,128)(2,1)S(1)} %slice.277), channel_id=1, source_target_pairs={{0,32},{1,97},{32,0},{33,65},{64,96},{65,33},{96,64},{97,1},{2,34}... | collective-permute-start | bytes 393224 | tf_op jit(solution)/shard_map/ppermute | solution.py:446
  268.0 8.2 %collective-permute-start.19 = (bf16[16,4096]{1,0:T(8,128)(2,1)S(1)}, bf16[16,4096]{1,0:T(8,128)(2,1)S(1)}, u32[]{:S(2)}, u32[]{:S(2)}) collective-permute-start(bf16[16,4096]{1,0:T(8,128)(2,1)S(1)} %slice.265), channel_id=1, source_target_pairs={{0,2},{1,7},{2,0},{3,5},{4,6},{5,3},{6,4},{7,1},{8,10},{9,15},{10,... | collective-permute-start | bytes 393224 | tf_op jit(solution)/shard_map/ppermute | solution.py:446
  272.2 5.0 %collective-permute-start.10 = (bf16[16,4096]{1,0:T(8,128)(2,1)S(1)}, bf16[16,4096]{1,0:T(8,128)(2,1)S(1)}, u32[]{:S(2)}, u32[]{:S(2)}) collective-permute-start(bf16[16,4096]{1,0:T(8,128)(2,1)S(1)} %slice.253), channel_id=1, source_target_pairs={{0,8},{1,25},{8,0},{9,17},{16,24},{17,9},{24,16},{25,1},{2,10},{3,... | collective-permute-start | bytes 393224 | tf_op jit(solution)/shard_map/ppermute | solution.py:446
  273.5 7.6 %collective-permute-start.29 = (bf16[8,4096]{1,0:T(8,128)(2,1)S(1)}, bf16[8,4096]{1,0:T(8,128)(2,1)S(1)}, u32[]{:S(2)}, u32[]{:S(2)}) collective-permute-start(bf16[8,4096]{1,0:T(8,128)(2,1)S(1)} %get-tuple-element.105), channel_id=1, source_target_pairs={{0,96},{1,33},{32,64},{33,1},{64,32},{65,97},{96,0},{97,65},{2,98}... | collective-permute-start | bytes 196616 | tf_op jit(solution)/shard_map/ppermute | solution.py:446
  276.8 5.5 %collective-permute-start.20 = (bf16[8,4096]{1,0:T(8,128)(2,1)S(1)}, bf16[8,4096]{1,0:T(8,128)(2,1)S(1)}, u32[]{:S(2)}, u32[]{:S(2)}) collective-permute-start(bf16[8,4096]{1,0:T(8,128)(2,1)S(1)} %get-tuple-element.107), channel_id=1, source_target_pairs={{0,6},{1,3},{2,4},{3,1},{4,2},{5,7},{6,0},{7,5},{8,14},{9,11},{10,... | collective-permute-start | bytes 196616 | tf_op jit(solution)/shard_map/ppermute | solution.py:446
  277.9 5.5 %collective-permute-start.11 = (bf16[8,4096]{1,0:T(8,128)(2,1)S(1)}, bf16[8,4096]{1,0:T(8,128)(2,1)S(1)}, u32[]{:S(2)}, u32[]{:S(2)}) collective-permute-start(bf16[8,4096]{1,0:T(8,128)(2,1)S(1)} %get-tuple-element.109), channel_id=1, source_target_pairs={{0,24},{1,9},{8,16},{9,1},{16,8},{17,25},{24,0},{25,17},{2,26},{3,... | collective-permute-start | bytes 196616 | tf_op jit(solution)/shard_map/ppermute | solution.py:446
  281.1 2.2 copy-start.20
  282.3 1.1 copy-start.21
  283.4 0.6 copy-start.22
Sparse Core Ops, SparseCore 0:
  11.7 95.5 all-gather.1
